TPU v7x, 32 devices: a whole 2x2x4 slice. The times are simulated.
32 devices in a mesh: section: 2 (over core), dp: 16 (over z, y, x).
Axes of the slice: x: 2, y: 2, z: 4, core: 2. Of those that a mesh axis runs over, the one named last changes fastest.
Arguments:
- features: bfloat16 [3, 32, 2048, 652], P(None, 'dp'), may hold values from -24 to 24
- lengths: int32 [3, 32], P(None, 'dp'), may hold values from 512 to 2048, as said below
- gain_first: float32 [652], replicated, may hold values from 0.5 to 1.5
- shift_first: float32 [652], replicated, may hold values from -3 to 3
- conv_first: bfloat16 [5, 652, 768], replicated, may hold values from -0.109375 to 0.109375
- bias_first: float32 [768], replicated, may hold values from -3 to 3
- gain_second: float32 [768], replicated, may hold values from 0.5 to 1.5
- shift_second: float32 [768], replicated, may hold values from -3 to 3
- conv_second: bfloat16 [3, 768, 384], replicated, may hold values from -0.125 to 0.125
- gain_third: float32 [384], replicated, may hold values from 0.5 to 1.5
- shift_third: float32 [384], replicated, may hold values from -3 to 3
- conv_point: bfloat16 [384, 768], replicated, may hold values from -0.3125 to 0.3125
- bias_point: float32 [768], replicated, may hold values from -3 to 3
- mean_first: float32 [652], replicated, may hold values from -4 to 4
- variance_first: float32 [652], replicated, may hold values from 0.5 to 2
- mean_second: float32 [768], replicated, may hold values from -4 to 4
- variance_second: float32 [768], replicated, may hold values from 0.5 to 2
- mean_third: float32 [384], replicated, may hold values from -4 to 4
- variance_third: float32 [384], replicated, may hold values from 0.5 to 2
- cotangent: bfloat16 [3, 32, 1024, 768], P(None, 'dp'), may hold values from -6 to 6
Outputs:
- block_output: bfloat16 [3, 32, 1024, 768], P(None, 'dp', None, 'section')
- input_grad: bfloat16 [3, 32, 2048, 652], P(None, 'dp', None, 'section')
- grad_gain_first: float32 [652], replicated
- grad_shift_first: float32 [652], replicated
- grad_conv_first: float32 [5, 652, 768], replicated
- grad_bias_first: float32 [768], replicated
- grad_gain_second: float32 [768], replicated
- grad_shift_second: float32 [768], replicated
- grad_conv_second: float32 [3, 768, 384], replicated
- grad_gain_third: float32 [384], replicated
- grad_shift_third: float32 [384], replicated
- grad_point: float32 [384, 768], replicated
- grad_bias_point: float32 [768], replicated
- new_mean_first: float32 [652], replicated
- new_variance_first: float32 [652], replicated
- new_mean_second: float32 [768], replicated
- new_variance_second: float32 [768], replicated
- new_mean_third: float32 [384], replicated
- new_variance_third: float32 [384], replicated
Inputs may be any that keep to these rules, and one draw needn't show every extreme that they name: `lengths`: in every micro-batch some window has all 2048 bins valid.
All inputs are finite; a program needn't handle non-finite values.
Results may differ from a plain program's by a relative error of at most 0.008.
The roundings to bfloat16 on the way count: a program that leaves them out, or rounds other values in their place, can miss the bound.
Values may be sent and summed in bfloat16 or wider, within the bound.
No kernel may reach another device: no remote copies, remote signals or barrier semaphores. Data moves between devices by JAX's collectives and lax.ppermute only.
A program may use at most 576 MiB of HBM per device.

v0:
```python
from math import pi, sqrt

import jax
import jax.numpy as jnp
from jax import lax
from jax.experimental import pallas as pl
from jax.experimental.pallas import tpu as pltpu
from jax.sharding import PartitionSpec as P

EPSILON = 1e-05
MOMENTUM = 0.4
CURVE = sqrt(2.0 / pi)
CUBIC = CURVE * 0.044715
BF16 = jnp.bfloat16
F32 = jnp.float32
LANES = 128
TILE = 256
BOTH = ("section", "dp")


def up(value, step):
    return -(-value // step) * step


def nn(left, right):
    return jnp.dot(left, right, preferred_element_type=F32)


def nt(left, right):
    return lax.dot_general(left, right, (((1,), (1,)), ((), ())), preferred_element_type=F32)


def iota(shape, axis):
    return lax.broadcasted_iota(jnp.int32, shape, axis)


def choose(flag):
    return jnp.where(flag, 1.0, 0.0)


def identity():
    return choose(iota((TILE, TILE), 0) == iota((TILE, TILE), 1)).astype(BF16)


def gelu(v):
    half = 0.5 * v
    return half + half * jnp.tanh(v * (CURVE + CUBIC * (v * v)))


def gelu_slope(v):
    square = v * v
    bent = jnp.tanh(v * (CURVE + CUBIC * square))
    half = 0.5 * v
    slope = (0.5 + 0.5 * bent) + half * (1.0 - bent * bent) * (CURVE + (3.0 * CUBIC) * square)
    return half + half * bent, slope


def column(row):
    return jnp.transpose(jnp.broadcast_to(row, (LANES, row.shape[1])))


def as_row(partial_sums):
    return jnp.sum(jnp.transpose(partial_sums), axis=0, keepdims=True)


def wide(block, lanes):
    return jnp.concatenate([block] * (lanes // LANES), axis=1)


def fold(block):
    parts = [block[:, at : at + LANES] for at in range(0, block.shape[1], LANES)]
    while len(parts) > 1:
        parts = [a + b for a, b in zip(parts[::2], parts[1::2])]
    return parts[0]


def before(block):
    rolled = pltpu.roll(block, 1, 1)
    inner = choose(iota((block.shape[0], LANES), 1) > 0).astype(block.dtype)
    return jnp.concatenate([rolled[:, :LANES] * inner, rolled[:, LANES:]], axis=1)


def after(block):
    last = block.shape[1] - LANES
    rolled = pltpu.roll(block, block.shape[1] - 1, 1)
    inner = choose(iota((block.shape[0], LANES), 1) < LANES - 1).astype(block.dtype)
    return jnp.concatenate([rolled[:, :last], rolled[:, last:] * inner], axis=1)


def aligned(value):
    return value if isinstance(value, int) else pl.multiple_of(value, 16)


def each_rows(total, body, unroll, step=16):
    group = step * unroll
    full = total // group

    def run(index, carry):
        for turn in range(unroll):
            start = pl.multiple_of(index * group + turn * step, step)
            body(pl.ds(start, step), start)
        return carry

    lax.fori_loop(0, full, run, 0)
    for start in range(full * group, total, step):
        body(pl.ds(start, step), start)


def pool_mask(length, lanes, start=0):
    return choose(2 * (iota((1, lanes), 1) + start) < length)


def odd_mask(length, lanes, start=0):
    return choose(2 * (iota((1, lanes), 1) + start) + 1 < length)


def whole(shape, buffered=None):
    zeros = (0,) * len(shape)
    if buffered is None:
        return pl.BlockSpec(shape, lambda *_: zeros)
    return pl.BlockSpec(shape, lambda *_: zeros, pipeline_mode=pl.Buffered(buffered))


def per_batch(shape):
    return pl.BlockSpec((1,) + shape, lambda k, *_: (k,) + (0,) * len(shape))


def per_lanes(shape):
    return pl.BlockSpec((1,) + shape, lambda k, j, _: (k,) + (0,) * (len(shape) - 1) + (j,))


def shape_of(shape, dtype=F32):
    return jax.ShapeDtypeStruct(shape, dtype)


def call(name, body, grid, in_specs, out_specs, out_shape, scratch=(), limit=58):
    return pl.pallas_call(
        body,
        grid_spec=pltpu.PrefetchScalarGridSpec(
            num_scalar_prefetch=1,
            grid=grid,
            in_specs=in_specs,
            out_specs=out_specs,
            scratch_shapes=list(scratch),
        ),
        out_shape=out_shape,
        compiler_params=pltpu.CompilerParams(vmem_limit_bytes=limit * 2**20),
        name=name,
    )


def row_pair(ref, k):
    table = ref[...]
    at = iota(table.shape, 0) - 2 * k
    rows = [jnp.sum(jnp.where(at == r, table, 0.0), axis=0, keepdims=True) for r in range(2)]
    return jnp.concatenate(rows, axis=0)


def put_rows(ref, k, first, second):
    table = ref[...]
    at = iota(table.shape, 0) - 2 * k
    ref[...] = jnp.where(at == 0, first, jnp.where(at == 1, second, table))


def finish_rows(total, count):
    centre = total[0:1] / count
    variance = total[1:2] / count - centre * centre
    return centre, variance, lax.rsqrt(variance + EPSILON)


def first_rows(ref, k, c_in):
    total = row_pair(ref, k)
    lane = iota((1, total.shape[1]), 1)
    counts = jnp.sum(jnp.where(lane == c_in, total, 0.0), axis=1, keepdims=True)
    total = jnp.where(lane < c_in, total, 0.0)
    return finish_rows(total, counts[0:1]), counts[0:1], counts[1:2]


def back_rows(total, count, gain, inverse):
    outer = gain * inverse
    return outer, outer * inverse * (total[1:2] / count), outer * (total[0:1] / count)


def prepare_weights(conv_first, conv_second, conv_point, vectors, c_lane):
    taps, c_in, c_mid = conv_first.shape
    taps_b, _, c_res = conv_second.shape
    c_pad = up(c_in, 16)
    depth = up(taps * c_pad, TILE)
    room = up(c_pad + (taps - 1) * (c_pad % LANES), LANES)
    base = c_pad - c_pad % LANES
    many = len(vectors)

    def body(info, first, second, point, *rest):
        vector_refs = rest[:many]
        first_out, back_out, second_out, second_back, point_out, table, wide_sum = rest[many:]
        for index, ref in enumerate(vector_refs):
            value = ref[...]
            if value.shape[0] < c_lane:
                value = jnp.pad(value, (0, c_lane - value.shape[0]))
            table[index : index + 1, :] = value.reshape(1, c_lane)
        eye = identity()
        for row in range(0, c_mid, TILE):
            wide_sum[...] = jnp.zeros_like(wide_sum)
            for tap in range(taps):
                turned = nt(eye, first[tap, :, row : row + TILE])
                padded = jnp.concatenate([turned, jnp.zeros((TILE, room - c_in), F32)], axis=1)
                moved = pltpu.roll(padded, tap * (c_pad % LANES), 1) if tap else padded
                wide_sum[:, tap * base : tap * base + room] += moved
            first_out[row : row + TILE, :] = wide_sum[:, :depth].astype(BF16)
        for tap in range(taps):
            back_out[:c_in, tap * c_mid : (tap + 1) * c_mid] = first[tap]
        back_out[c_in:, :] = jnp.zeros((c_pad - c_in, taps * c_mid), BF16)
        eye_res = choose(iota((c_res, c_res), 0) == iota((c_res, c_res), 1)).astype(BF16)
        for tap in range(taps_b):
            second_out[:, tap * c_mid : (tap + 1) * c_mid] = nt(eye_res, second[tap]).astype(BF16)
            second_back[:, tap * c_res : (tap + 1) * c_res] = second[tap]
        eye_mid = choose(iota((c_mid, c_mid), 0) == iota((c_mid, c_mid), 1)).astype(BF16)
        point_out[...] = nt(eye_mid, point[...]).astype(BF16)

    outs = [
        ((c_mid, depth), BF16),
        ((c_pad, taps * c_mid), BF16),
        ((c_res, taps_b * c_mid), BF16),
        ((c_mid, taps_b * c_res), BF16),
        ((c_mid, c_res), BF16),
        ((up(many, 8), c_lane), F32),
    ]
    return call(
        "prepare_weights",
        body,
        (1,),
        [whole(a.shape) for a in (conv_first, conv_second, conv_point, *vectors)],
        [whole(s) for s, _ in outs],
        [shape_of(s, t) for s, t in outs],
        [pltpu.VMEM((TILE, max(depth, (taps - 1) * base + room)), F32)],
    )


def load_features(micro, bins, c_in):
    c_pad = up(c_in, 16)
    c_lane = up(c_in, LANES)
    step = 2 * TILE
    steps = bins // step

    def body(info, f_ref, x_ref, st_ref, own, s_acc, q_acc):
        k, at = pl.program_id(0), pl.program_id(1)
        section, length = info[0], info[1 + k]

        @pl.when(at == 0)
        def _():
            s_acc[...] = jnp.zeros_like(s_acc)
            q_acc[...] = jnp.zeros_like(q_acc)

        @pl.when((at == 0) & (k == 0))
        def _():
            st_ref[...] = jnp.zeros_like(st_ref)

        flat = f_ref[0].reshape(2 * c_in, step)
        spot = iota((TILE, TILE), 1)
        source = jnp.where(spot < LANES, 2 * spot, 2 * spot - (TILE - 1))
        split = choose(iota((TILE, TILE), 0) == source).astype(BF16)
        keep = choose(iota((1, step), 1) + at * step < length)
        for row in range(0, c_in, LANES):
            count = min(LANES, c_in - row)
            count_pad = up(count, 16)
            pick = choose(
                iota((count_pad, 2 * count), 1) == 2 * iota((count_pad, 2 * count), 0) + section
            ).astype(BF16)
            chosen = nn(pick, flat[2 * row : 2 * (row + count)])
            own[row : row + count_pad, :] = (chosen * keep).astype(BF16)
        low = nn(own[:, :TILE], split)
        high = nn(own[:, TILE:], split)
        x_ref[0, 0, :, :LANES] = low[:, :LANES].astype(BF16)
        x_ref[0, 0, :, LANES:] = high[:, :LANES].astype(BF16)
        x_ref[0, 1, :, :LANES] = low[:, LANES:].astype(BF16)
        x_ref[0, 1, :, LANES:] = high[:, LANES:].astype(BF16)
        s_acc[:c_pad, :] += fold(low) + fold(high)
        q_acc[:c_pad, :] += fold(low * low) + fold(high * high)

        @pl.when(at == steps - 1)
        def _():
            lane = iota((1, c_lane), 1)
            count_in = length.astype(F32)
            count_pool = ((length + 1) // 2).astype(F32)
            put_rows(
                st_ref,
                k,
                jnp.where(lane < c_in, as_row(s_acc[...]), count_in),
                jnp.where(lane < c_in, as_row(q_acc[...]), count_pool),
            )

    return call(
        "load_features",
        body,
        (micro, steps),
        [pl.BlockSpec((1, c_in, 2, step), lambda k, j, _: (k, 0, 0, j))],
        [per_lanes((2, c_pad, TILE)), whole((8, c_lane))],
        [shape_of((micro, 2, c_pad, bins // 2), BF16), shape_of((8, c_lane))],
        [pltpu.VMEM((c_pad, step), BF16)] + [pltpu.VMEM((c_lane, LANES), F32)] * 2,
    )


def forward_first(micro, c_in, c_mid, taps, pooled):
    c_pad = up(c_in, 16)
    c_lane = up(c_in, LANES)
    depth = up(taps * c_pad, TILE)
    extra = depth - taps * c_pad
    steps = pooled // TILE
    stack_rows = (taps + 1) * c_pad + extra

    def body(info, x_ref, sums, table, weight, hid, diff, act, st_ref,
             stack, col_c, col_s, col_h, bias, s_acc, q_acc, even, odd):
        k, at = pl.program_id(0), pl.program_id(1)
        length = info[1 + k]

        @pl.when((at == 0) & (k == 0))
        def _():
            stack[(taps + 1) * c_pad :, :] = jnp.zeros((extra, pooled), BF16)
            col_h[...] = column(table[1:2, :])
            bias[...] = column(table[2:3, :c_mid])
            st_ref[...] = jnp.zeros_like(st_ref)

        @pl.when(at == 0)
        def _():
            (centre, _, inverse), _, _ = first_rows(sums, k, c_in)
            col_c[...] = column(centre)
            col_s[...] = column(inverse * table[0:1, :])
            s_acc[...] = jnp.zeros_like(s_acc)
            q_acc[...] = jnp.zeros_like(q_acc)
            masks = pool_mask(length, pooled), odd_mask(length, pooled)

            def rows_body(rows, start):
                c, s, h = (wide(r[rows, :], TILE) for r in (col_c, col_s, col_h))
                here = lambda seg: pl.ds(aligned(seg * c_pad + start), 16)
                for half in range(2):
                    parts = []
                    for lane in range(0, pooled, TILE):
                        lanes = slice(lane, lane + TILE)
                        v = (x_ref[0, half, rows, lanes].astype(F32) - c) * s + h
                        parts.append((gelu(v) * masks[half][:, lanes]).astype(BF16))
                    a = jnp.concatenate(parts, axis=1)
                    act[0, half, rows, :] = a
                    stack[here(half), :] = before(a)
                    stack[here(2 + half), :] = a
                    stack[here(4 + half), :] = after(a)

            each_rows(c_pad, rows_body, 4)

        lanes = pl.ds(pl.multiple_of(at * TILE, TILE), TILE)
        even[...] = nn(weight[...], stack[:depth, lanes])
        odd[...] = nn(weight[...], stack[c_pad : c_pad + depth, lanes])
        mask = pool_mask(length, TILE, at * TILE)

        def rows_body(rows, start):
            b = wide(bias[rows, :], TILE)
            left, right = even[rows, :] + b, odd[rows, :] + b
            apart = left - right
            joined = jnp.maximum(left, right) + jnp.log1p(jnp.exp(-jnp.abs(apart)))
            rounded = (joined * mask).astype(BF16)
            diff[0, rows, :] = apart
            hid[0, rows, :] = rounded
            value = rounded.astype(F32)
            s_acc[rows, :] += fold(value)
            q_acc[rows, :] += fold(value * value)

        each_rows(c_mid, rows_body, 12)

        @pl.when(at == steps - 1)
        def _():
            put_rows(st_ref, k, as_row(s_acc[...]), as_row(q_acc[...]))

    return call(
        "forward_first",
        body,
        (micro, steps),
        [
            per_batch((2, c_pad, pooled)),
            whole((8, c_lane)),
            whole((8, c_lane)),
            whole((c_mid, depth), 1),
        ],
        [
            per_lanes((c_mid, TILE)),
            per_lanes((c_mid, TILE)),
            per_batch((2, c_pad, pooled)),
            whole((8, c_mid)),
        ],
        [
            shape_of((micro, c_mid, pooled), BF16),
            shape_of((micro, c_mid, pooled)),
            shape_of((micro, 2, c_pad, pooled), BF16),
            shape_of((8, c_mid)),
        ],
        [pltpu.VMEM((stack_rows, pooled), BF16)]
        + [pltpu.VMEM((c_lane, LANES), F32)] * 3
        + [pltpu.VMEM((c_mid, LANES), F32)] * 3
        + [pltpu.VMEM((c_mid, TILE), F32)] * 2,
    )


def forward_second(micro, c_in, c_mid, c_res, taps, pooled, c_lane):
    def body(info, hid, sums_a, sums, table, weight, conv, act, st_ref,
             stack, col_c, col_s, col_h, s_acc, q_acc):
        k = pl.program_id(0)
        length = info[1 + k]
        _, _, count = first_rows(sums_a, k, c_in)
        centre, _, inverse = finish_rows(row_pair(sums, k), count)
        col_c[...] = column(centre)
        col_s[...] = column(inverse * table[3:4, :c_mid])

        @pl.when(k == 0)
        def _():
            col_h[...] = column(table[4:5, :c_mid])
            st_ref[...] = jnp.zeros_like(st_ref)

        mask = pool_mask(length, pooled)

        def rows_body(rows, start):
            c, s, h = (wide(r[rows, :], TILE) for r in (col_c, col_s, col_h))
            here = lambda seg: pl.ds(aligned(seg * c_mid + start), 16)
            parts = []
            for lane in range(0, pooled, TILE):
                lanes = slice(lane, lane + TILE)
                v = (hid[0, rows, lanes].astype(F32) - c) * s + h
                parts.append((gelu(v) * mask[:, lanes]).astype(BF16))
            a = jnp.concatenate(parts, axis=1)
            act[0, rows, :] = a
            stack[here(0), :] = before(a)
            stack[here(1), :] = a
            stack[here(2), :] = after(a)

        each_rows(c_mid, rows_body, 8)
        for at in range(0, pooled, TILE):
            conv[0, :, at : at + TILE] = nn(weight[...], stack[:, at : at + TILE])

        def moments_body(rows, start):
            value = conv[0, rows, :] * mask
            s_acc[rows, :] = fold(value)
            q_acc[rows, :] = fold(value * value)

        each_rows(c_res, moments_body, 8)
        put_rows(st_ref, k, as_row(s_acc[...]), as_row(q_acc[...]))

    return call(
        "forward_second",
        body,
        (micro,),
        [
            per_batch((c_mid, pooled)),
            whole((8, c_lane)),
            whole((8, c_mid)),
            whole((8, c_lane)),
            whole((c_res, taps * c_mid), 1),
        ],
        [per_batch((c_res, pooled)), per_batch((c_mid, pooled)), whole((8, c_res))],
        [
            shape_of((micro, c_res, pooled)),
            shape_of((micro, c_mid, pooled), BF16),
            shape_of((8, c_res)),
        ],
        [pltpu.VMEM((taps * c_mid, pooled), BF16)]
        + [pltpu.VMEM((c_mid, LANES), F32)] * 3
        + [pltpu.VMEM((c_res, LANES), F32)] * 2,
    )


def turn_point(micro, c_in, c_mid, c_res, pooled, c_lane):
    half = c_mid // 2

    def body(info, conv, sums_a, sums, table, hid, cot, point_t, point,
             own, send, go, d_out, st_ref, point_own, point_send, grad_bias,
             act, up_grad, branch, flat, bias, col_c, col_s, col_h, s_acc, q_acc, product):
        k = pl.program_id(0)
        section, length = info[0], info[1 + k]
        first = section == 0
        _, _, count = first_rows(sums_a, k, c_in)
        centre, _, inverse = finish_rows(row_pair(sums, k), count)
        col_c[...] = column(centre)
        col_s[...] = column(inverse * table[5:6, :c_res])

        @pl.when(k == 0)
        def _():
            col_h[...] = column(table[6:7, :c_res])
            bias[...] = column(table[7:8, :c_mid])
            product[...] = jnp.zeros_like(product)
            grad_bias[...] = jnp.zeros_like(grad_bias)
            st_ref[...] = jnp.zeros_like(st_ref)

        mask = pool_mask(length, pooled)
        up_grad[...] = nt(point[...], cot[0, 0])

        def rows_body(rows, start):
            c, s, h = (wide(r[rows, :], TILE) for r in (col_c, col_s, col_h))
            total_s, total_q = [], []
            for lane in range(0, pooled, TILE):
                lanes = slice(lane, lane + TILE)
                apart = conv[0, rows, lanes] - c
                a, slope = gelu_slope(apart * s + h)
                act[rows, lanes] = (a * mask[:, lanes]).astype(BF16)
                d = mask[:, lanes] * slope * up_grad[rows, lanes]
                d_out[0, rows, lanes] = d
                total_s.append(fold(d))
                total_q.append(fold(d * apart))
            s_acc[rows, :] = sum(total_s)
            q_acc[rows, :] = sum(total_q)

        each_rows(c_res, rows_body, 4)
        put_rows(st_ref, k, as_row(s_acc[...]), as_row(q_acc[...]) * inverse)
        branch[...] = nn(point_t[...], act[...])

        def out_body(rows, start):
            b = wide(bias[rows, :], pooled)
            total = hid[0, rows, :].astype(F32) + (branch[rows, :] + b)
            flat[rows, :] = (total * mask).astype(BF16)

        each_rows(c_mid, out_body, 8)
        eye = identity()
        for at in range(0, pooled, TILE):
            turned = nt(eye, flat[:, at : at + TILE]).astype(BF16)
            low, high = turned[:, :half], turned[:, half:]
            own[0, at : at + TILE, :] = jnp.where(first, low, high)
            send[0, at : at + TILE, :] = jnp.where(first, high, low)
        for at in range(0, c_mid, TILE):
            go[0, at : at + TILE, :] = (nt(eye, cot[0, 0, :, at : at + TILE]) * mask).astype(BF16)
        product[...] += nn(act[...], cot[0, 0])
        ones = jnp.broadcast_to(mask, (16, pooled)).astype(BF16)
        grad_bias[...] += nn(ones, cot[0, 0])[:8]

        @pl.when(k == micro - 1)
        def _():
            low, high = product[:, :half], product[:, half:]
            point_own[...] = jnp.where(first, low, high)
            point_send[...] = jnp.where(first, high, low).astype(BF16)

    in_specs = [
        per_batch((c_res, pooled)),
        whole((8, c_lane)),
        whole((8, c_res)),
        whole((8, c_lane)),
        per_batch((c_mid, pooled)),
        pl.BlockSpec((1, 1, pooled, c_mid), lambda k, info: (k, info[0], 0, 0)),
        whole((c_mid, c_res), 1),
        whole((c_res, c_mid), 1),
    ]
    return call(
        "turn_point",
        body,
        (micro,),
        in_specs,
        [
            per_batch((pooled, half)),
            per_batch((pooled, half)),
            per_batch((c_mid, pooled)),
            per_batch((c_res, pooled)),
            whole((8, c_res)),
            whole((c_res, half)),
            whole((c_res, half)),
            whole((8, c_mid)),
        ],
        [
            shape_of((micro, pooled, half), BF16),
            shape_of((micro, pooled, half), BF16),
            shape_of((micro, c_mid, pooled), BF16),
            shape_of((micro, c_res, pooled)),
            shape_of((8, c_res)),
            shape_of((c_res, half)),
            shape_of((c_res, half), BF16),
            shape_of((8, c_mid)),
        ],
        [
            pltpu.VMEM((c_res, pooled), BF16),
            pltpu.VMEM((c_res, pooled), F32),
            pltpu.VMEM((c_mid, pooled), F32),
            pltpu.VMEM((c_mid, pooled), BF16),
            pltpu.VMEM((c_mid, LANES), F32),
        ]
        + [pltpu.VMEM((c_res, LANES), F32)] * 5
        + [pltpu.VMEM((c_res, c_mid), F32)],
    )


def backward_second(micro, c_in, c_mid, c_res, taps, pooled, c_lane):
    half = c_mid // 2

    def body(info, d_in, conv, sums_a, sums_b, sums_c, back, table, hid, act, weight,
             d_out, st_ref, conv_own, conv_send,
             stack, up_grad, product, col_a, col_b, col_0, col_r, col_c, col_s, col_h, s_acc, q_acc):
        k = pl.program_id(0)
        length = info[1 + k]
        first = info[0] == 0
        _, _, count = first_rows(sums_a, k, c_in)
        centre, _, inverse = finish_rows(row_pair(sums_c, k), count)
        outer, slant, level = back_rows(row_pair(back, k), count, table[5:6, :c_res], inverse)
        col_a[...] = column(outer)
        col_b[...] = column(slant)
        col_0[...] = column(level)
        col_r[...] = column(centre)
        centre, _, inverse = finish_rows(row_pair(sums_b, k), count)
        col_c[...] = column(centre)
        col_s[...] = column(inverse * table[3:4, :c_mid])

        @pl.when(k == 0)
        def _():
            col_h[...] = column(table[4:5, :c_mid])
            product[...] = jnp.zeros_like(product)
            st_ref[...] = jnp.zeros_like(st_ref)

        mask = pool_mask(length, pooled)

        def rows_body(rows, start):
            a, b, z, c = (wide(r[rows, :], pooled) for r in (col_a, col_b, col_0, col_r))
            g = (a * d_in[0, rows, :] - b * (conv[0, rows, :] - c) - z) * mask
            g = g.astype(BF16)
            here = lambda seg: pl.ds(aligned(seg * c_res + start), 16)
            stack[here(0), :] = after(g)
            stack[here(1), :] = g
            stack[here(2), :] = before(g)

        each_rows(c_res, rows_body, 8)
        for at in range(0, pooled, TILE):
            up_grad[:, at : at + TILE] = nn(weight[...], stack[:, at : at + TILE])

        def slope_body(rows, start):
            c, s, h = (wide(r[rows, :], TILE) for r in (col_c, col_s, col_h))
            total_s, total_q = [], []
            for lane in range(0, pooled, TILE):
                lanes = slice(lane, lane + TILE)
                apart = hid[0, rows, lanes].astype(F32) - c
                _, slope = gelu_slope(apart * s + h)
                d = mask[:, lanes] * slope * up_grad[rows, lanes]
                d_out[0, rows, lanes] = d
                total_s.append(fold(d))
                total_q.append(fold(d * apart))
            s_acc[rows, :] = sum(total_s)
            q_acc[rows, :] = sum(total_q)

        each_rows(c_mid, slope_body, 4)
        put_rows(st_ref, k, as_row(s_acc[...]), as_row(q_acc[...]) * inverse)
        for tap in range(taps):
            product[tap] += nt(act[0], stack[tap * c_res : (tap + 1) * c_res, :])

        @pl.when(k == micro - 1)
        def _():
            for tap in range(taps):
                low, high = product[tap, :half, :], product[tap, half:, :]
                conv_own[tap] = jnp.where(first, low, high)
                conv_send[tap] = jnp.where(first, high, low).astype(BF16)

    in_specs = [
        per_batch((c_res, pooled)),
        per_batch((c_res, pooled)),
        whole((8, c_lane)),
        whole((8, c_mid)),
        whole((8, c_res)),
        whole((8, c_res)),
        whole((8, c_lane)),
        per_batch((c_mid, pooled)),
        per_batch((c_mid, pooled)),
        whole((c_mid, taps * c_res), 1),
    ]
    return call(
        "backward_second",
        body,
        (micro,),
        in_specs,
        [
            per_batch((c_mid, pooled)),
            whole((8, c_mid)),
            whole((taps, half, c_res)),
            whole((taps, half, c_res)),
        ],
        [
            shape_of((micro, c_mid, pooled)),
            shape_of((8, c_mid)),
            shape_of((taps, half, c_res)),
            shape_of((taps, half, c_res), BF16),
        ],
        [
            pltpu.VMEM((taps * c_res, pooled), BF16),
            pltpu.VMEM((c_mid, pooled), F32),
            pltpu.VMEM((taps, c_mid, c_res), F32),
        ]
        + [pltpu.VMEM((c_res, LANES), F32)] * 4
        + [pltpu.VMEM((c_mid, LANES), F32)] * 5,
    )


def stack_gradient(stack, half, here, gradient):
    order = 3 - half
    stack[here(order - 2), :] = after(gradient)
    stack[here(order), :] = gradient
    stack[here(order + 2), :] = before(gradient)


def weights_first(micro, c_in, c_mid, taps, pooled, c_lane):
    c_pad = up(c_in, 16)
    half = c_mid // 2

    def body(info, d_in, hid, go, diff, sums_a, sums_b, back, table, act,
             g_out, bias_out, conv_own, conv_send,
             stack, product, col_a, col_b, col_0, col_c, s_acc):
        k, at = pl.program_id(0), pl.program_id(1)
        length = info[1 + k]
        first = info[0] == 0

        @pl.when((at == 0) & (k == 0))
        def _():
            bias_out[...] = jnp.zeros_like(bias_out)

        @pl.when(at == 0)
        def _():
            _, _, count = first_rows(sums_a, k, c_in)
            centre, _, inverse = finish_rows(row_pair(sums_b, k), count)
            outer, slant, level = back_rows(row_pair(back, k), count, table[3:4, :c_mid], inverse)
            col_a[...] = column(outer)
            col_b[...] = column(slant)
            col_0[...] = column(level)
            col_c[...] = column(centre)
            mask = pool_mask(length, pooled)

            def rows_body(rows, start):
                a, b, z, c = (wide(r[rows, :], TILE) for r in (col_a, col_b, col_0, col_c))
                lefts, rights, totals = [], [], []
                for lane in range(0, pooled, TILE):
                    lanes = slice(lane, lane + TILE)
                    field = a * d_in[0, rows, lanes] - b * (hid[0, rows, lanes].astype(F32) - c) - z
                    g = field * mask[:, lanes] + go[0, rows, lanes].astype(F32)
                    g = g.astype(BF16).astype(F32)
                    apart = diff[0, rows, lanes]
                    small = jnp.exp(-jnp.abs(apart))
                    large = 1.0 / (1.0 + small)
                    small = small * large
                    positive = apart >= 0.0
                    left = (g * jnp.where(positive, large, small)).astype(BF16)
                    right = (g * jnp.where(positive, small, large)).astype(BF16)
                    lefts.append(left)
                    rights.append(right)
                    totals.append(fold(left.astype(F32) + right.astype(F32)))
                s_acc[rows, :] = sum(totals)
                here = lambda seg: pl.ds(aligned(seg * c_mid + start), 16)
                for side, parts in enumerate((lefts, rights)):
                    joined = jnp.concatenate(parts, axis=1)
                    g_out[0, side, rows, :] = joined
                    stack_gradient(stack, side, here, joined)

            each_rows(c_mid, rows_body, 4)
            bias_out[...] += as_row(s_acc[...])

        even = pl.ds(pl.multiple_of((at + 1) * c_mid, c_mid), c_mid)
        odd = pl.ds(pl.multiple_of(at * c_mid, c_mid), c_mid)
        value = nt(act[0, 0], stack[even, :]) + nt(act[0, 1], stack[odd, :])

        @pl.when(k == 0)
        def _():
            product[at] = value

        @pl.when((k > 0) & (k < micro - 1))
        def _():
            product[at] += value

        @pl.when(k == micro - 1)
        def _():
            total = (product[at] + value)[:c_in]
            low, high = total[:, :half], total[:, half:]
            conv_own[0] = jnp.where(first, low, high)
            conv_send[0] = jnp.where(first, high, low).astype(BF16)

    block = pl.BlockSpec(
        (1, c_in, half), lambda k, j, _: (jnp.where(k == micro - 1, j, 0), 0, 0)
    )
    in_specs = [
        per_batch((c_mid, pooled)),
        per_batch((c_mid, pooled)),
        per_batch((c_mid, pooled)),
        per_batch((c_mid, pooled)),
        whole((8, c_lane)),
        whole((8, c_mid)),
        whole((8, c_mid)),
        whole((8, c_lane)),
        per_batch((2, c_pad, pooled)),
    ]
    return call(
        "weights_first",
        body,
        (micro, taps),
        in_specs,
        [per_batch((2, c_mid, pooled)), whole((8, c_mid)), block, block],
        [
            shape_of((micro, 2, c_mid, pooled), BF16),
            shape_of((8, c_mid)),
            shape_of((taps, c_in, half)),
            shape_of((taps, c_in, half), BF16),
        ],
        [pltpu.VMEM(((taps + 1) * c_mid, pooled), BF16), pltpu.VMEM((taps, c_pad, c_mid), F32)]
        + [pltpu.VMEM((c_mid, LANES), F32)] * 5,
    )


def backward_first(micro, c_in, c_mid, taps, pooled, c_lane):
    c_pad = up(c_in, 16)
    steps = pooled // TILE

    def body(info, g_in, x_ref, sums_a, table, weight, bias_first, bias_point, d_out, st_ref,
             stack, even, odd, col_c, col_s, col_h, s_acc, q_acc):
        k, at = pl.program_id(0), pl.program_id(1)
        length = info[1 + k]
        (centre, _, inverse), _, _ = first_rows(sums_a, k, c_in)

        @pl.when((at == 0) & (k == 0))
        def _():
            col_h[...] = column(table[1:2, :])
            st_ref[2 * micro : 2 * micro + 1, :] = bias_first[0:1, :]
            st_ref[2 * micro + 1 : 2 * micro + 2, :] = bias_point[0:1, :]

        @pl.when(at == 0)
        def _():
            col_c[...] = column(centre)
            col_s[...] = column(inverse * table[0:1, :])
            s_acc[...] = jnp.zeros_like(s_acc)
            q_acc[...] = jnp.zeros_like(q_acc)

            def rows_body(rows, start):
                here = lambda seg: pl.ds(aligned(seg * c_mid + start), 16)
                stack_gradient(stack, 0, here, g_in[0, 0, rows, :])
                stack_gradient(stack, 1, here, g_in[0, 1, rows, :])

            each_rows(c_mid, rows_body, 8)

        lanes = pl.ds(pl.multiple_of(at * TILE, TILE), TILE)
        depth = taps * c_mid
        even[...] = nn(weight[...], stack[c_mid : c_mid + depth, lanes])
        odd[...] = nn(weight[...], stack[:depth, lanes])
        masks = pool_mask(length, TILE, at * TILE), odd_mask(length, TILE, at * TILE)

        def rows_body(rows, start):
            c, s, h = (wide(r[rows, :], TILE) for r in (col_c, col_s, col_h))
            for half, upstream in enumerate((even, odd)):
                apart = x_ref[0, half, rows, :].astype(F32) - c
                _, slope = gelu_slope(apart * s + h)
                d = masks[half] * slope * upstream[rows, :]
                d_out[0, half, rows, :] = d
                s_acc[rows, :] += fold(d)
                q_acc[rows, :] += fold(d * apart)

        each_rows(c_pad, rows_body, 10)

        @pl.when(at == steps - 1)
        def _():
            put_rows(st_ref, k, as_row(s_acc[...]), as_row(q_acc[...]) * inverse)

    return call(
        "backward_first",
        body,
        (micro, steps),
        [
            per_batch((2, c_mid, pooled)),
            per_lanes((2, c_pad, TILE)),
            whole((8, c_lane)),
            whole((8, c_lane)),
            whole((c_pad, taps * c_mid), 1),
            whole((8, c_mid)),
            whole((8, c_mid)),
        ],
        [per_lanes((2, c_pad, TILE)), whole((8, c_lane))],
        [shape_of((micro, 2, c_pad, pooled)), shape_of((8, c_lane))],
        [
            pltpu.VMEM(((taps + 1) * c_mid, pooled), BF16),
            pltpu.VMEM((c_pad, TILE), F32),
            pltpu.VMEM((c_pad, TILE), F32),
        ]
        + [pltpu.VMEM((c_lane, LANES), F32)] * 5,
    )


def finish_first(micro, c_in, pooled, c_lane):
    c_pad = up(c_in, 16)
    half_in = c_in // 2
    steps = pooled // TILE

    def body(info, d_in, x_ref, sums_a, back, table, own, send, flat, col_a, col_b, col_0, col_c):
        k, at = pl.program_id(0), pl.program_id(1)
        section, length = info[0], info[1 + k]

        @pl.when(at == 0)
        def _():
            (centre, _, inverse), count, _ = first_rows(sums_a, k, c_in)
            outer, slant, level = back_rows(row_pair(back, k), count, table[0:1, :], inverse)
            col_a[...] = column(outer)
            col_b[...] = column(slant)
            col_0[...] = column(level)
            col_c[...] = column(centre)

        masks = pool_mask(length, TILE, at * TILE), odd_mask(length, TILE, at * TILE)

        def rows_body(rows, start):
            a, b, z, c = (wide(r[rows, :], TILE) for r in (col_a, col_b, col_0, col_c))
            parts = []
            for half in range(2):
                apart = x_ref[0, half, rows, :].astype(F32) - c
                field = (a * d_in[0, half, rows, :] - b * apart - z) * masks[half]
                parts.append(field.astype(BF16))
            for side in range(0, TILE, LANES):
                flat[rows, 2 * side : 2 * side + LANES] = parts[0][:, side : side + LANES]
                flat[rows, 2 * side + LANES : 2 * side + TILE] = parts[1][:, side : side + LANES]

        each_rows(c_pad, rows_body, 10)
        spot = iota((TILE, TILE), 0)
        source = jnp.where(spot < LANES, 2 * spot, 2 * spot - (TILE - 1))
        join = choose(iota((TILE, TILE), 1) == source).astype(BF16)
        for side in range(0, 2 * TILE, TILE):
            natural = nn(flat[:, side : side + TILE], join)
            low, high = natural[:half_in], natural[half_in : 2 * half_in]
            first = section == 0
            own[0, :, side : side + TILE] = jnp.where(first, low, high).astype(BF16)
            send[0, :, side : side + TILE] = jnp.where(first, high, low).astype(BF16)

    half_block = pl.BlockSpec((1, half_in, 2 * TILE), lambda k, j, _: (k, 0, j))
    return call(
        "finish_first",
        body,
        (micro, steps),
        [
            per_lanes((2, c_pad, TILE)),
            per_lanes((2, c_pad, TILE)),
            whole((8, c_lane)),
            whole((8, c_lane)),
            whole((8, c_lane)),
        ],
        [half_block, half_block],
        [shape_of((micro, half_in, 2 * pooled), BF16)] * 2,
        [pltpu.VMEM((c_pad, 2 * TILE), BF16)] + [pltpu.VMEM((c_lane, LANES), F32)] * 4,
    )


def pair_windows(micro, half_in, bins):
    step = 2 * TILE
    steps = bins // step

    def body(info, own, got, out):
        section = info[0]
        for row in range(0, half_in, LANES):
            count = min(LANES, half_in - row)
            at = iota((2 * count, count), 0) - 2 * iota((2 * count, count), 1)
            joined = nn(choose(at == section).astype(BF16), own[0, row : row + count, :])
            joined += nn(choose(at == 1 - section).astype(BF16), got[0, row : row + count, :])
            out[0, row : row + count] = joined.astype(BF16).reshape(count, 2, step)

    block = pl.BlockSpec((1, half_in, step), lambda k, j, _: (k, 0, j))
    return call(
        "pair_windows",
        body,
        (micro, steps),
        [block, block],
        pl.BlockSpec((1, half_in, 2, step), lambda k, j, _: (k, 0, 0, j)),
        shape_of((micro, half_in, 2, bins), BF16),
    )


def small_outputs(micro, c_in, c_mid, c_res, c_lane):
    def body(info, sums_a, sums_b, sums_c, back_a, back_b, back_c, *rest):
        running = rest[:6]
        outs = rest[6:]

        def put(ref, row):
            ref[...] = row.reshape(row.shape[1])[: ref.shape[0]]

        for at, back in enumerate((back_a, back_b, back_c)):
            put(outs[2 * at], sum(back[2 * k + 1 : 2 * k + 2, :] for k in range(micro)))
            put(outs[2 * at + 1], sum(back[2 * k : 2 * k + 1, :] for k in range(micro)))
        put(outs[6], back_a[2 * micro : 2 * micro + 1, :c_mid])
        put(outs[7], back_a[2 * micro + 1 : 2 * micro + 2, :c_mid])
        firsts = [first_rows(sums_a, k, c_in) for k in range(micro)]
        stats = [[f[0] for f in firsts]]
        for sums in (sums_b, sums_c):
            stats.append(
                [finish_rows(sums[2 * k : 2 * k + 2, :], firsts[k][2]) for k in range(micro)]
            )
        for at, history in enumerate(stats):
            for part in range(2):
                lanes = history[0][part].shape[1]
                value = running[2 * at + part][...]
                if value.shape[0] < lanes:
                    value = jnp.pad(value, (0, lanes - value.shape[0]))
                value = value.reshape(1, lanes)
                for k in range(micro):
                    value = (1.0 - MOMENTUM) * value + MOMENTUM * history[k][part]
                put(outs[8 + 2 * at + part], value)

    widths = [c_in] * 2 + [c_mid] * 2 + [c_res] * 2
    shapes = widths + [c_mid, c_mid] + widths
    tables = [(8, c_lane), (8, c_mid), (8, c_res)] * 2
    return call(
        "small_outputs",
        body,
        (1,),
        [whole(s) for s in tables] + [whole((n,)) for n in widths],
        [whole((n,)) for n in shapes],
        [shape_of((n,)) for n in shapes],
    )


def partner(array):
    return lax.ppermute(array, "section", [(0, 1), (1, 0)])


def share(rows):
    devices = lax.axis_size("section") * lax.axis_size("dp")
    bits = [1 << at for at in range(devices.bit_length() - 1)]
    groups = [[bits[-1], bits[0]]]
    rest = bits[1:-1]
    while rest:
        groups.append(rest[:3])
        rest = rest[3:]
    for group in groups:
        masks = [0]
        for bit in group:
            masks += [mask + bit for mask in masks]
        parts = [
            lax.ppermute(rows, BOTH, [(i, i ^ mask) for i in range(devices)]) if mask else rows
            for mask in masks
        ]
        while len(parts) > 1:
            parts = [a + b for a, b in zip(parts[::2], parts[1::2])]
        rows = parts[0]
    return rows


def share_at_once(rows):
    devices = lax.axis_size("section") * lax.axis_size("dp")
    copies = jnp.broadcast_to(rows[None], (devices,) + rows.shape)
    return jnp.sum(lax.all_to_all(copies, BOTH, 0, 0), axis=0)


def shards(
    features,
    lengths,
    gain_first,
    shift_first,
    conv_first,
    bias_first,
    gain_second,
    shift_second,
    conv_second,
    gain_third,
    shift_third,
    conv_point,
    bias_point,
    mean_first,
    variance_first,
    mean_second,
    variance_second,
    mean_third,
    variance_third,
    cotangent,
):
    micro, _, bins, c_in = features.shape
    pooled = bins // 2
    taps, _, c_mid = conv_first.shape
    taps_b, _, c_res = conv_second.shape
    c_lane = up(c_in, LANES)
    section = lax.axis_index("section").astype(jnp.int32)
    lead = section == 0
    own_lengths = jnp.where(lead, lengths[:, 0], lengths[:, 1]).astype(jnp.int32)
    info = jnp.concatenate([section[None], own_lengths])
    feats = features.transpose(0, 3, 1, 2)

    loaded, part = load_features(micro, bins, c_in)(info, feats)
    sums_a = share_at_once(part)
    vectors = (
        gain_first, shift_first, bias_first, gain_second, shift_second, gain_third, shift_third,
        bias_point,
    )
    first_t, first_b, second_t, second_b, point_t, table = prepare_weights(
        conv_first, conv_second, conv_point, vectors, c_lane
    )(info, conv_first, conv_second, conv_point, *vectors)
    hid, diff, act_a, part = forward_first(micro, c_in, c_mid, taps, pooled)(
        info, loaded, sums_a, table, first_t
    )
    sums_b = share(part)
    conv_b, act_b, part = forward_second(micro, c_in, c_mid, c_res, taps_b, pooled, c_lane)(
        info, hid, sums_a, sums_b, table, second_t
    )
    sums_c = share(part)
    own_out, send_out, go, d_c, part, point_own, point_send, grad_bias = turn_point(
        micro, c_in, c_mid, c_res, pooled, c_lane
    )(info, conv_b, sums_a, sums_c, table, hid, cotangent, point_t, conv_point)
    back_c = share(part)
    got_out = partner(send_out)
    d_b, part, second_own, second_send = backward_second(
        micro, c_in, c_mid, c_res, taps_b, pooled, c_lane
    )(info, d_c, conv_b, sums_a, sums_b, sums_c, back_c, table, hid, act_b, second_b)
    back_b = share(part)
    halves = [
        (mine + partner(other)).astype(BF16)
        for mine, other in ((second_own, second_send), (point_own, point_send))
    ]
    half_second, half_point = lax.psum(tuple(halves), "dp")
    g_a, bias_sum, first_own, first_send = weights_first(micro, c_in, c_mid, taps, pooled, c_lane)(
        info, d_b, hid, go, diff, sums_a, sums_b, back_b, table, act_a
    )
    half_first = lax.psum((first_own + partner(first_send)).astype(BF16), "dp")
    d_a, part = backward_first(micro, c_in, c_mid, taps, pooled, c_lane)(
        info, g_a, loaded, sums_a, table, first_b, bias_sum, grad_bias
    )
    back_a = share(part)
    own_in, send_in = finish_first(micro, c_in, pooled, c_lane)(
        info, d_a, loaded, sums_a, back_a, table
    )
    paired = pair_windows(micro, c_in // 2, bins)(info, own_in, partner(send_in))
    input_grad = paired.transpose(0, 2, 3, 1)
    block_output = jnp.stack(
        [jnp.where(lead, own_out, got_out), jnp.where(lead, got_out, own_out)], axis=1
    )
    small = small_outputs(micro, c_in, c_mid, c_res, c_lane)(
        info, sums_a, sums_b, sums_c, back_a, back_b, back_c,
        mean_first, variance_first, mean_second, variance_second, mean_third, variance_third,
    )

    def join(half, axis):
        other = partner(half)
        low, high = jnp.where(lead, half, other), jnp.where(lead, other, half)
        return jnp.concatenate([low, high], axis=axis).astype(F32)

    return (
        block_output,
        input_grad,
        small[0],
        small[1],
        join(half_first, 2),
        small[6],
        small[2],
        small[3],
        join(half_second, 1),
        small[4],
        small[5],
        join(half_point, 1),
        small[7],
        *small[8:],
    )


def solution(mesh):
    wide_spec = P(None, "dp", None, None)
    split_spec = P(None, "dp", None, "section")
    return jax.shard_map(
        shards,
        mesh=mesh,
        in_specs=(wide_spec, P(None, "dp")) + (P(),) * 17 + (wide_spec,),
        out_specs=(split_spec, split_spec) + (P(),) * 17,
        check_vma=False,
    )
```

profile of v0, /device:TPU:0, one launch (start us, length us, event | category | flops | bytes accessed | tf_op | source)
XLA Modules:
  0.0 557.7 jit_solution(8411407559990569531)
XLA Ops:
  8.6 16.8 %load_features.1 = (bf16[3,2,656,1024]{3,2,1,0:T(8,128)(2,1)}, f32[8,768]{1,0:T(8,128)}) custom-call(s32[4]{0:T(128)} %pad_add_fusion.info, bf16[3,652,2,2048]{3,2,1,0:T(2,128)(2,1)} %bitcast.9), custom_call_target="tpu_custom_call" | custom-call | tf_op jit(solution)/shard_map/load_features/pallas_call | solution.py:1067
  27.1 7.3 %all-to-all-start = ((f32[32,8,768]{2,1,0:T(8,128)}), f32[32,8,768]{2,1,0:T(8,128)S(1)}, u32[]{:S(2)}, u32[]{:S(2)}) async-start(f32[32,8,768]{2,1,0:T(8,128)} %broadcast_in_dim.10), calls=%async_computation | async-start | bytes 1572864 | tf_op jit(solution)/shard_map/all_to_all | solution.py:1031
  34.5 12.8 %prepare_weights.1 = (bf16[768,3328]{1,0:T(8,128)(2,1)}, bf16[656,3840]{1,0:T(8,128)(2,1)}, bf16[384,2304]{1,0:T(8,128)(2,1)}, bf16[768,1152]{1,0:T(8,128)(2,1)}...) custom-call(s32[4]{0:T(128)} %pad_add_fusion.info, bf16[5,652,768]{2,1,0:T(8,128)(2,1)} %first.1, ...), custom_call_target="tpu_custom_call" | custom-call | tf_op jit(solution)/shard_map/prepare_weights/pallas_call | solution.py:1073
  47.3 9.6 %all-to-all-done = f32[32,8,768]{2,1,0:T(8,128)S(1)} async-done(((f32[32,8,768]{2,1,0:T(8,128)}), f32[32,8,768]{2,1,0:T(8,128)S(1)}, u32[]{:S(2)}, u32[]{:S(2)}) %all-to-all-start) | async-done | bytes 786464 | tf_op jit(solution)/shard_map/all_to_all | solution.py:1031
  57.6 61.9 %forward_first.1 = (bf16[3,768,1024]{2,1,0:T(8,128)(2,1)}, f32[3,768,1024]{2,1,0:T(8,128)}, bf16[3,2,656,1024]{3,2,1,0:T(8,128)(2,1)}, f32[8,768]{1,0:T(8,128)}) custom-call(s32[4]{0:T(128)} %pad_add_fusion.info, bf16[3,2,656,1024]{3,2,1,0:T(8,128)(2,1)} %get-tuple-element.68.x_ref, f32[8,768]{1,0:T(8,128)} %reduce_sum.9.sums.sums_a, ...), custom_call_target="tpu_custom_call" | custom-call | tf_op jit(solution)/shard_map/forward_first/pallas_call | solution.py:1076
  119.6 1.8 collective-permute-start.2
  121.4 2.2 collective-permute-done.1
  124.9 3.0 collective-permute-start.5
  128.4 2.1 collective-permute-start.7
  131.2 4.3 collective-permute-start.9
  138.3 19.1 %forward_second.1 = (f32[3,384,1024]{2,1,0:T(8,128)}, bf16[3,768,1024]{2,1,0:T(8,128)(2,1)}, f32[8,384]{1,0:T(8,128)}) custom-call(s32[4]{0:T(128)} %pad_add_fusion.info, bf16[3,768,1024]{2,1,0:T(8,128)(2,1)} %get-tuple-element.72.hid, f32[8,768]{1,0:T(8,128)} %reduce_sum.9.sums.sums_a, f32[8,768]{1,0:T(8,128)} %add_add_fusion.4.sums.sums_b, ...), custom_call_target="tpu_custom_call" | custom-call | tf_op jit(solution)/shard_map/forward_second/pallas_call | solution.py:1080
  159.3 2.1 collective-permute-done.11
  163.0 2.0 collective-permute-start.13
  166.4 2.0 collective-permute-start.16
  168.4 2.3 collective-permute-start.17
  170.8 2.9 collective-permute-start.18
  174.1 2.1 collective-permute-done.18
  176.3 3.8 collective-permute-done.19
  180.7 24.8 %turn_point.1 = (bf16[3,1024,384]{2,1,0:T(8,128)(2,1)}, bf16[3,1024,384]{2,1,0:T(8,128)(2,1)}, bf16[3,768,1024]{2,1,0:T(8,128)(2,1)}, f32[3,384,1024]{2,1,0:T(8,...) custom-call(s32[4]{0:T(128)} %pad_add_fusion.info, ...), custom_call_target="tpu_custom_call" | custom-call | tf_op jit(solution)/shard_map/turn_point/pallas_call | solution.py:1084
  207.5 2.1 collective-permute-done.22
  210.6 3.3 collective-permute-start.26
  213.9 2.5 collective-permute-start.28
  217.2 4.3 collective-permute-start.30
  221.9 1.7 collective-permute-done.30
  224.2 34.1 %backward_second.1 = (f32[3,768,1024]{2,1,0:T(8,128)}, f32[8,768]{1,0:T(8,128)}, f32[3,384,384]{2,1,0:T(8,128)}, bf16[3,384,384]{2,1,0:T(8,128)(2,1)}) custom-call(s32[4]{0:T(128)} %pad_add_fusion.info, f32[3,384,1024]{2,1,0:T(8,128)} %get-tuple-element.80.d_in, f32[3,384,1024]{2,1,0:T(8,128)} %get-tuple-element.75.conv, f32[8,768]{1,0:T(8,128)} %reduce_sum.9.sums.sums_a, ...), custom_call_target="tpu_custom_call" | custom-call | tf_op jit(solution)/shard_map/backward_second/pallas_call | solution.py:1089
  260.3 2.2 collective-permute-done.32
  264.0 2.0 collective-permute-start.34
  267.5 2.0 collective-permute-start.37
  269.5 2.3 collective-permute-start.38
  271.8 2.9 collective-permute-start.39
  275.3 2.2 collective-permute-done.39
  277.4 3.8 collective-permute-done.40
  281.9 67.9 %weights_first.1 = (bf16[3,2,768,1024]{3,2,1,0:T(8,128)(2,1)}, f32[8,768]{1,0:T(8,128)}, f32[5,652,384]{2,1,0:T(8,128)}, bf16[5,652,384]{2,1,0:T(8,128)(2,1)}) custom-call(s32[4]{0:T(128)} %pad_add_fusion.info, f32[3,768,1024]{2,1,0:T(8,128)} %get-tuple-element.84.d_in, bf16[3,768,1024]{2,1,0:T(8,128)(2,1)} %get-tuple-element.72.hid, ...), custom_call_target="tpu_custom_call" | custom-call | tf_op jit(solution)/shard_map/weights_first/pallas_call | solution.py:1098
  350.4 5.5 collective-permute-done.56
  357.8 4.6 add_convert_fusion
  362.5 63.2 %backward_first.1 = (f32[3,2,656,1024]{3,2,1,0:T(8,128)}, f32[8,768]{1,0:T(8,128)}) custom-call(s32[4]{0:T(128)} %pad_add_fusion.info, bf16[3,2,768,1024]{3,2,1,0:T(8,128)(2,1)} %get-tuple-element.89.g_in, bf16[3,2,656,1024]{3,2,1,0:T(8,128)(2,1)} %get-tuple-element.68.x_ref, f32[8,768]{1,0:T(8,128)} %reduce_sum.9.sums.sums_a, ...), custom_call_target="tpu_custom_call" | custom-call | tf_op jit(solution)/shard_map/backward_first/pallas_call | solution.py:1102
  427.5 2.5 collective-permute-done.42
  431.5 3.4 collective-permute-start.46
  434.9 2.4 collective-permute-start.48
  437.6 4.9 collective-permute-start.50
  445.2 20.1 %finish_first.1 = (bf16[3,326,2048]{2,1,0:T(8,128)(2,1)}, bf16[3,326,2048]{2,1,0:T(8,128)(2,1)}) custom-call(s32[4]{0:T(128)} %pad_add_fusion.info, f32[3,2,656,1024]{3,2,1,0:T(8,128)} %get-tuple-element.93.d_in, bf16[3,2,656,1024]{3,2,1,0:T(8,128)(2,1)} %get-tuple-element.68.x_ref, f32[8,768]{1,0:T(8,128)} %reduce_sum.9.sums.sums_a, ...), custom_call_target="tpu_custom_call" | custom-call | tf_op jit(solution)/shard_map/finish_first/pallas_call | solution.py:1106
  465.8 53.7 %all-reduce.3.cloned.1.call-done = (bf16[5,652,384]{2,1,0:T(8,128)(2,1)}, bf16[3,384,384]{2,1,0:T(8,128)(2,1)}, bf16[384,384]{1,0:T(8,128)(2,1)}) async-done(((bf16[5,652,384]{2,1,0:T(8,128)(2,1)}, bf16[3,384,384]{2,1,0:T(8,128)(2,1)}, bf16[384,384]{1,0:T(8,128)(2,1)}), (bf16[5,652,384]{2,1,0:T(8,128)(2,1)}, bf16[3,384,384]{2,1,0:T(8,128)(2,1)}, bf16[384,384]{1,0:T(8,128)(2,1)})) %all-reduce.3.cloned.1.call-update) | async-done | bytes 3683344 | tf_op jit(solution)/shard_map/psum | solution.py:1101
  519.5 2.3 small_outputs.1
  522.4 2.1 select_bitcast_fusion.1
  525.1 2.7 copy.40
  527.8 13.2 %pair_windows.1 = bf16[3,326,2,2048]{3,2,1,0:T(2,128)(2,1)} custom-call(s32[4]{0:T(128)} %pad_add_fusion.info, bf16[3,326,2048]{2,1,0:T(8,128)(2,1)} %get-tuple-element.95.own, bf16[3,326,2048]{2,1,0:T(8,128)(2,1)} %collective-permute-done.51.got), custom_call_target="tpu_custom_call" | custom-call | tf_op jit(solution)/shard_map/pair_windows/pallas_call | solution.py:1109
  542.5 2.0 maximum_convert_fusion.1
  546.0 4.8 maximum_convert_fusion
  (126 shorter events, 39.5 us)
Async XLA Ops:
  27.1 29.8 %all-to-all-start = ((f32[32,8,768]{2,1,0:T(8,128)}), f32[32,8,768]{2,1,0:T(8,128)S(1)}, u32[]{:S(2)}, u32[]{:S(2)}) async-start(f32[32,8,768]{2,1,0:T(8,128)} %broadcast_in_dim.10), calls=%async_computation | async-start | bytes 1572864 | tf_op jit(solution)/shard_map/all_to_all | solution.py:1031
  34.4 485.0 %all-reduce.3.cloned.1.call-start = ((), (), s32[]{:S(2)}) async-start(), calls=%async_computation.1 | async-start | bytes 7397376 | tf_op jit(solution)/shard_map/psum | solution.py:1101
  119.5 4.1 collective-permute-start.1
  124.3 6.1 %collective-permute-start.3 = (f32[8,768]{1,0:T(8,128)S(1)}, f32[8,768]{1,0:T(8,128)S(1)}, u32[]{:S(2)}, u32[]{:S(2)}) collective-permute-start(f32[8,768]{1,0:T(8,128)S(1)} %add_add_fusion.5), channel_id=1, source_target_pairs={{0,2},{1,3},{2,0},{3,1},{4,6},{5,7},{6,4},{7,5},{8,10},{9,11},{10,... | collective-permute-start | bytes 73736 | tf_op jit(solution)/shard_map/ppermute | solution.py:1019
  124.6 6.6 %collective-permute-start.4 = (f32[8,768]{1,0:T(8,128)S(1)}, f32[8,768]{1,0:T(8,128)S(1)}, u32[]{:S(2)}, u32[]{:S(2)}) collective-permute-start(f32[8,768]{1,0:T(8,128)S(1)} %add_add_fusion.5), channel_id=1, source_target_pairs={{0,4},{1,5},{2,6},{3,7},{4,0},{5,1},{6,2},{7,3},{8,12},{9,13},{10,... | collective-permute-start | bytes 73736 | tf_op jit(solution)/shard_map/ppermute | solution.py:1019
  124.9 10.6 %collective-permute-start.5 = (f32[8,768]{1,0:T(8,128)S(1)}, f32[8,768]{1,0:T(8,128)S(1)}, u32[]{:S(2)}, u32[]{:S(2)}) collective-permute-start(f32[8,768]{1,0:T(8,128)S(1)} %add_add_fusion.5), channel_id=1, source_target_pairs={{0,6},{1,7},{2,4},{3,5},{4,2},{5,3},{6,0},{7,1},{8,14},{9,15},{10,... | collective-permute-start | bytes 73736 | tf_op jit(solution)/shard_map/ppermute | solution.py:1019
  127.8 7.7 %collective-permute-start.6 = (f32[8,768]{1,0:T(8,128)S(1)}, f32[8,768]{1,0:T(8,128)S(1)}, u32[]{:S(2)}, u32[]{:S(2)}) collective-permute-start(f32[8,768]{1,0:T(8,128)S(1)} %add_add_fusion.5), channel_id=1, source_target_pairs={{0,8},{1,9},{2,10},{3,11},{4,12},{5,13},{6,14},{7,15},{8,0},{9,1},... | collective-permute-start | bytes 73736 | tf_op jit(solution)/shard_map/ppermute | solution.py:1019
  128.4 7.1 %collective-permute-start.7 = (f32[8,768]{1,0:T(8,128)S(1)}, f32[8,768]{1,0:T(8,128)S(1)}, u32[]{:S(2)}, u32[]{:S(2)}) collective-permute-start(f32[8,768]{1,0:T(8,128)S(1)} %add_add_fusion.5), channel_id=1, source_target_pairs={{0,10},{1,11},{2,8},{3,9},{4,14},{5,15},{6,12},{7,13},{8,2},{9,3},... | collective-permute-start | bytes 73736 | tf_op jit(solution)/shard_map/ppermute | solution.py:1019
  130.5 5.7 %collective-permute-start.8 = (f32[8,768]{1,0:T(8,128)S(1)}, f32[8,768]{1,0:T(8,128)S(1)}, u32[]{:S(2)}, u32[]{:S(2)}) collective-permute-start(f32[8,768]{1,0:T(8,128)S(1)} %add_add_fusion.5), channel_id=1, source_target_pairs={{0,12},{1,13},{2,14},{3,15},{4,8},{5,9},{6,10},{7,11},{8,4},{9,5},... | collective-permute-start | bytes 73736 | tf_op jit(solution)/shard_map/ppermute | solution.py:1019
  131.2 6.5 %collective-permute-start.9 = (f32[8,768]{1,0:T(8,128)S(1)}, f32[8,768]{1,0:T(8,128)S(1)}, u32[]{:S(2)}, u32[]{:S(2)}) collective-permute-start(f32[8,768]{1,0:T(8,128)S(1)} %add_add_fusion.5), channel_id=1, source_target_pairs={{0,14},{1,15},{2,12},{3,13},{4,10},{5,11},{6,8},{7,9},{8,6},{9,7},... | collective-permute-start | bytes 73736 | tf_op jit(solution)/shard_map/ppermute | solution.py:1019
  163.0 7.8 %collective-permute-start.13 = (f32[8,384]{1,0:T(8,128)S(1)}, f32[8,384]{1,0:T(8,128)S(1)}, u32[]{:S(2)}, u32[]{:S(2)}) collective-permute-start(f32[8,384]{1,0:T(8,128)S(1)} %add_add_fusion.9), channel_id=1, source_target_pairs={{0,2},{1,3},{2,0},{3,1},{4,6},{5,7},{6,4},{7,5},{8,10},{9,11},{10,... | collective-permute-start | bytes 36872 | tf_op jit(solution)/shard_map/ppermute | solution.py:1019
  164.9 8.8 %collective-permute-start.14 = (f32[8,384]{1,0:T(8,128)S(1)}, f32[8,384]{1,0:T(8,128)S(1)}, u32[]{:S(2)}, u32[]{:S(2)}) collective-permute-start(f32[8,384]{1,0:T(8,128)S(1)} %add_add_fusion.9), channel_id=1, source_target_pairs={{0,4},{1,5},{2,6},{3,7},{4,0},{5,1},{6,2},{7,3},{8,12},{9,13},{10,... | collective-permute-start | bytes 36872 | tf_op jit(solution)/shard_map/ppermute | solution.py:1019
  164.9 9.2 %collective-permute-start.15 = (f32[8,384]{1,0:T(8,128)S(1)}, f32[8,384]{1,0:T(8,128)S(1)}, u32[]{:S(2)}, u32[]{:S(2)}) collective-permute-start(f32[8,384]{1,0:T(8,128)S(1)} %add_add_fusion.9), channel_id=1, source_target_pairs={{0,6},{1,7},{2,4},{3,5},{4,2},{5,3},{6,0},{7,1},{8,14},{9,15},{10,... | collective-permute-start | bytes 36872 | tf_op jit(solution)/shard_map/ppermute | solution.py:1019
  166.4 7.7 %collective-permute-start.16 = (f32[8,384]{1,0:T(8,128)S(1)}, f32[8,384]{1,0:T(8,128)S(1)}, u32[]{:S(2)}, u32[]{:S(2)}) collective-permute-start(f32[8,384]{1,0:T(8,128)S(1)} %add_add_fusion.9), channel_id=1, source_target_pairs={{0,8},{1,9},{2,10},{3,11},{4,12},{5,13},{6,14},{7,15},{8,0},{9,1},... | collective-permute-start | bytes 36872 | tf_op jit(solution)/shard_map/ppermute | solution.py:1019
  168.4 5.7 %collective-permute-start.17 = (f32[8,384]{1,0:T(8,128)S(1)}, f32[8,384]{1,0:T(8,128)S(1)}, u32[]{:S(2)}, u32[]{:S(2)}) collective-permute-start(f32[8,384]{1,0:T(8,128)S(1)} %add_add_fusion.9), channel_id=1, source_target_pairs={{0,10},{1,11},{2,8},{3,9},{4,14},{5,15},{6,12},{7,13},{8,2},{9,3},... | collective-permute-start | bytes 36872 | tf_op jit(solution)/shard_map/ppermute | solution.py:1019
  170.8 5.5 collective-permute-start.18
  173.7 6.4 %collective-permute-start.19 = (f32[8,384]{1,0:T(8,128)S(1)}, f32[8,384]{1,0:T(8,128)S(1)}, u32[]{:S(2)}, u32[]{:S(2)}) collective-permute-start(f32[8,384]{1,0:T(8,128)S(1)} %add_add_fusion.9), channel_id=1, source_target_pairs={{0,14},{1,15},{2,12},{3,13},{4,10},{5,11},{6,8},{7,9},{8,6},{9,7},... | collective-permute-start | bytes 36872 | tf_op jit(solution)/shard_map/ppermute | solution.py:1019
  210.4 6.0 %collective-permute-start.24 = (f32[8,384]{1,0:T(8,128)S(1)}, f32[8,384]{1,0:T(8,128)S(1)}, u32[]{:S(2)}, u32[]{:S(2)}) collective-permute-start(f32[8,384]{1,0:T(8,128)S(1)} %add_add_fusion.7), channel_id=1, source_target_pairs={{0,2},{1,3},{2,0},{3,1},{4,6},{5,7},{6,4},{7,5},{8,10},{9,11},{10,... | collective-permute-start | bytes 36872 | tf_op jit(solution)/shard_map/ppermute | solution.py:1019
  210.6 6.7 %collective-permute-start.25 = (f32[8,384]{1,0:T(8,128)S(1)}, f32[8,384]{1,0:T(8,128)S(1)}, u32[]{:S(2)}, u32[]{:S(2)}) collective-permute-start(f32[8,384]{1,0:T(8,128)S(1)} %add_add_fusion.7), channel_id=1, source_target_pairs={{0,4},{1,5},{2,6},{3,7},{4,0},{5,1},{6,2},{7,3},{8,12},{9,13},{10,... | collective-permute-start | bytes 36872 | tf_op jit(solution)/shard_map/ppermute | solution.py:1019
  210.6 11.0 %collective-permute-start.26 = (f32[8,384]{1,0:T(8,128)S(1)}, f32[8,384]{1,0:T(8,128)S(1)}, u32[]{:S(2)}, u32[]{:S(2)}) collective-permute-start(f32[8,384]{1,0:T(8,128)S(1)} %add_add_fusion.7), channel_id=1, source_target_pairs={{0,6},{1,7},{2,4},{3,5},{4,2},{5,3},{6,0},{7,1},{8,14},{9,15},{10,... | collective-permute-start | bytes 36872 | tf_op jit(solution)/shard_map/ppermute | solution.py:1019
  213.9 7.7 %collective-permute-start.27 = (f32[8,384]{1,0:T(8,128)S(1)}, f32[8,384]{1,0:T(8,128)S(1)}, u32[]{:S(2)}, u32[]{:S(2)}) collective-permute-start(f32[8,384]{1,0:T(8,128)S(1)} %add_add_fusion.7), channel_id=1, source_target_pairs={{0,8},{1,9},{2,10},{3,11},{4,12},{5,13},{6,14},{7,15},{8,0},{9,1},... | collective-permute-start | bytes 36872 | tf_op jit(solution)/shard_map/ppermute | solution.py:1019
  213.9 7.7 %collective-permute-start.28 = (f32[8,384]{1,0:T(8,128)S(1)}, f32[8,384]{1,0:T(8,128)S(1)}, u32[]{:S(2)}, u32[]{:S(2)}) collective-permute-start(f32[8,384]{1,0:T(8,128)S(1)} %add_add_fusion.7), channel_id=1, source_target_pairs={{0,10},{1,11},{2,8},{3,9},{4,14},{5,15},{6,12},{7,13},{8,2},{9,3},... | collective-permute-start | bytes 36872 | tf_op jit(solution)/shard_map/ppermute | solution.py:1019
  216.4 5.5 collective-permute-start.29
  217.2 6.4 %collective-permute-start.30 = (f32[8,384]{1,0:T(8,128)S(1)}, f32[8,384]{1,0:T(8,128)S(1)}, u32[]{:S(2)}, u32[]{:S(2)}) collective-permute-start(f32[8,384]{1,0:T(8,128)S(1)} %add_add_fusion.7), channel_id=1, source_target_pairs={{0,14},{1,15},{2,12},{3,13},{4,10},{5,11},{6,8},{7,9},{8,6},{9,7},... | collective-permute-start | bytes 36872 | tf_op jit(solution)/shard_map/ppermute | solution.py:1019
  258.4 4.1 collective-permute-start.32
  264.0 7.8 %collective-permute-start.34 = (f32[8,768]{1,0:T(8,128)S(1)}, f32[8,768]{1,0:T(8,128)S(1)}, u32[]{:S(2)}, u32[]{:S(2)}) collective-permute-start(f32[8,768]{1,0:T(8,128)S(1)} %add_add_fusion.3), channel_id=1, source_target_pairs={{0,2},{1,3},{2,0},{3,1},{4,6},{5,7},{6,4},{7,5},{8,10},{9,11},{10,... | collective-permute-start | bytes 73736 | tf_op jit(solution)/shard_map/ppermute | solution.py:1019
  266.0 8.8 %collective-permute-start.35 = (f32[8,768]{1,0:T(8,128)S(1)}, f32[8,768]{1,0:T(8,128)S(1)}, u32[]{:S(2)}, u32[]{:S(2)}) collective-permute-start(f32[8,768]{1,0:T(8,128)S(1)} %add_add_fusion.3), channel_id=1, source_target_pairs={{0,4},{1,5},{2,6},{3,7},{4,0},{5,1},{6,2},{7,3},{8,12},{9,13},{10,... | collective-permute-start | bytes 73736 | tf_op jit(solution)/shard_map/ppermute | solution.py:1019
  266.0 9.2 %collective-permute-start.36 = (f32[8,768]{1,0:T(8,128)S(1)}, f32[8,768]{1,0:T(8,128)S(1)}, u32[]{:S(2)}, u32[]{:S(2)}) collective-permute-start(f32[8,768]{1,0:T(8,128)S(1)} %add_add_fusion.3), channel_id=1, source_target_pairs={{0,6},{1,7},{2,4},{3,5},{4,2},{5,3},{6,0},{7,1},{8,14},{9,15},{10,... | collective-permute-start | bytes 73736 | tf_op jit(solution)/shard_map/ppermute | solution.py:1019
  267.5 7.7 %collective-permute-start.37 = (f32[8,768]{1,0:T(8,128)S(1)}, f32[8,768]{1,0:T(8,128)S(1)}, u32[]{:S(2)}, u32[]{:S(2)}) collective-permute-start(f32[8,768]{1,0:T(8,128)S(1)} %add_add_fusion.3), channel_id=1, source_target_pairs={{0,8},{1,9},{2,10},{3,11},{4,12},{5,13},{6,14},{7,15},{8,0},{9,1},... | collective-permute-start | bytes 73736 | tf_op jit(solution)/shard_map/ppermute | solution.py:1019
  269.5 5.8 %collective-permute-start.38 = (f32[8,768]{1,0:T(8,128)S(1)}, f32[8,768]{1,0:T(8,128)S(1)}, u32[]{:S(2)}, u32[]{:S(2)}) collective-permute-start(f32[8,768]{1,0:T(8,128)S(1)} %add_add_fusion.3), channel_id=1, source_target_pairs={{0,10},{1,11},{2,8},{3,9},{4,14},{5,15},{6,12},{7,13},{8,2},{9,3},... | collective-permute-start | bytes 73736 | tf_op jit(solution)/shard_map/ppermute | solution.py:1019
  271.8 5.6 %collective-permute-start.39 = (f32[8,768]{1,0:T(8,128)S(1)}, f32[8,768]{1,0:T(8,128)S(1)}, u32[]{:S(2)}, u32[]{:S(2)}) collective-permute-start(f32[8,768]{1,0:T(8,128)S(1)} %add_add_fusion.3), channel_id=1, source_target_pairs={{0,12},{1,13},{2,14},{3,15},{4,8},{5,9},{6,10},{7,11},{8,4},{9,5},... | collective-permute-start | bytes 73736 | tf_op jit(solution)/shard_map/ppermute | solution.py:1019
  274.8 6.5 %collective-permute-start.40 = (f32[8,768]{1,0:T(8,128)S(1)}, f32[8,768]{1,0:T(8,128)S(1)}, u32[]{:S(2)}, u32[]{:S(2)}) collective-permute-start(f32[8,768]{1,0:T(8,128)S(1)} %add_add_fusion.3), channel_id=1, source_target_pairs={{0,14},{1,15},{2,12},{3,13},{4,10},{5,11},{6,8},{7,9},{8,6},{9,7},... | collective-permute-start | bytes 73736 | tf_op jit(solution)/shard_map/ppermute | solution.py:1019
  349.8 8.0 %collective-permute-start.52 = (bf16[5,652,384]{2,1,0:T(8,128)(2,1)}, bf16[5,652,384]{2,1,0:T(8,128)(2,1)S(1)}, u32[]{:S(2)}, u32[]{:S(2)}) collective-permute-start(bf16[5,652,384]{2,1,0:T(8,128)(2,1)} %get-tuple-element.100), channel_id=1, source_target_pairs={{0,16},{16,0},{1,17},{17,1},{2,18},{18,2},{3,19},{19,3},{4,20},{20... | collective-permute-start | bytes 7511048 | tf_op jit(solution)/shard_map/ppermute | solution.py:1003
  349.8 6.9 %collective-permute-start.54 = (bf16[3,384,384]{2,1,0:T(8,128)(2,1)S(1)}, bf16[3,384,384]{2,1,0:T(8,128)(2,1)S(1)}, u32[]{:S(2)}, u32[]{:S(2)}) collective-permute-start(bf16[3,384,384]{2,1,0:T(8,128)(2,1)S(1)} %copy-done.6), channel_id=1, source_target_pairs={{0,16},{16,0},{1,17},{17,1},{2,18},{18,2},{3,19},{19,3},{4,20},{20... | collective-permute-start | bytes 2654216 | tf_op jit(solution)/shard_map/ppermute | solution.py:1003
  350.3 5.6 collective-permute-start.56
  426.0 4.0 collective-permute-start.42
  431.4 5.9 %collective-permute-start.44 = (f32[8,768]{1,0:T(8,128)S(1)}, f32[8,768]{1,0:T(8,128)S(1)}, u32[]{:S(2)}, u32[]{:S(2)}) collective-permute-start(f32[8,768]{1,0:T(8,128)S(1)} %add_add_fusion.1), channel_id=1, source_target_pairs={{0,2},{1,3},{2,0},{3,1},{4,6},{5,7},{6,4},{7,5},{8,10},{9,11},{10,... | collective-permute-start | bytes 73736 | tf_op jit(solution)/shard_map/ppermute | solution.py:1019
  431.4 6.2 %collective-permute-start.45 = (f32[8,768]{1,0:T(8,128)S(1)}, f32[8,768]{1,0:T(8,128)S(1)}, u32[]{:S(2)}, u32[]{:S(2)}) collective-permute-start(f32[8,768]{1,0:T(8,128)S(1)} %add_add_fusion.1), channel_id=1, source_target_pairs={{0,4},{1,5},{2,6},{3,7},{4,0},{5,1},{6,2},{7,3},{8,12},{9,13},{10,... | collective-permute-start | bytes 73736 | tf_op jit(solution)/shard_map/ppermute | solution.py:1019
  431.5 11.1 %collective-permute-start.46 = (f32[8,768]{1,0:T(8,128)S(1)}, f32[8,768]{1,0:T(8,128)S(1)}, u32[]{:S(2)}, u32[]{:S(2)}) collective-permute-start(f32[8,768]{1,0:T(8,128)S(1)} %add_add_fusion.1), channel_id=1, source_target_pairs={{0,6},{1,7},{2,4},{3,5},{4,2},{5,3},{6,0},{7,1},{8,14},{9,15},{10,... | collective-permute-start | bytes 73736 | tf_op jit(solution)/shard_map/ppermute | solution.py:1019
  434.9 7.7 %collective-permute-start.47 = (f32[8,768]{1,0:T(8,128)S(1)}, f32[8,768]{1,0:T(8,128)S(1)}, u32[]{:S(2)}, u32[]{:S(2)}) collective-permute-start(f32[8,768]{1,0:T(8,128)S(1)} %add_add_fusion.1), channel_id=1, source_target_pairs={{0,8},{1,9},{2,10},{3,11},{4,12},{5,13},{6,14},{7,15},{8,0},{9,1},... | collective-permute-start | bytes 73736 | tf_op jit(solution)/shard_map/ppermute | solution.py:1019
  434.9 7.7 %collective-permute-start.48 = (f32[8,768]{1,0:T(8,128)S(1)}, f32[8,768]{1,0:T(8,128)S(1)}, u32[]{:S(2)}, u32[]{:S(2)}) collective-permute-start(f32[8,768]{1,0:T(8,128)S(1)} %add_add_fusion.1), channel_id=1, source_target_pairs={{0,10},{1,11},{2,8},{3,9},{4,14},{5,15},{6,12},{7,13},{8,2},{9,3},... | collective-permute-start | bytes 73736 | tf_op jit(solution)/shard_map/ppermute | solution.py:1019
  437.3 5.6 %collective-permute-start.49 = (f32[8,768]{1,0:T(8,128)S(1)}, f32[8,768]{1,0:T(8,128)S(1)}, u32[]{:S(2)}, u32[]{:S(2)}) collective-permute-start(f32[8,768]{1,0:T(8,128)S(1)} %add_add_fusion.1), channel_id=1, source_target_pairs={{0,12},{1,13},{2,14},{3,15},{4,8},{5,9},{6,10},{7,11},{8,4},{9,5},... | collective-permute-start | bytes 73736 | tf_op jit(solution)/shard_map/ppermute | solution.py:1019
  437.6 7.0 %collective-permute-start.50 = (f32[8,768]{1,0:T(8,128)S(1)}, f32[8,768]{1,0:T(8,128)S(1)}, u32[]{:S(2)}, u32[]{:S(2)}) collective-permute-start(f32[8,768]{1,0:T(8,128)S(1)} %add_add_fusion.1), channel_id=1, source_target_pairs={{0,14},{1,15},{2,12},{3,13},{4,10},{5,11},{6,8},{7,9},{8,6},{9,7},... | collective-permute-start | bytes 73736 | tf_op jit(solution)/shard_map/ppermute | solution.py:1019
  465.3 62.5 %collective-permute-start.51 = (bf16[3,326,2048]{2,1,0:T(8,128)(2,1)}, bf16[3,326,2048]{2,1,0:T(8,128)(2,1)}, u32[]{:S(2)}, u32[]{:S(2)}) collective-permute-start(bf16[3,326,2048]{2,1,0:T(8,128)(2,1)} %get-tuple-element.96), channel_id=1, source_target_pairs={{0,16},{16,0},{1,17},{17,1},{2,18},{18,2},{3,19},{19,3},{4,20},{20... | collective-permute-start | bytes 12017672 | tf_op jit(solution)/shard_map/ppermute | solution.py:1003
  465.3 57.1 %collective-permute-start.20 = (bf16[3,1024,384]{2,1,0:T(8,128)(2,1)}, bf16[3,1024,384]{2,1,0:T(8,128)(2,1)}, u32[]{:S(2)}, u32[]{:S(2)}) collective-permute-start(bf16[3,1024,384]{2,1,0:T(8,128)(2,1)} %get-tuple-element.79), channel_id=1, source_target_pairs={{0,16},{16,0},{1,17},{17,1},{2,18},{18,2},{3,19},{19,3},{4,20},{20... | collective-permute-start | bytes 7077896 | tf_op jit(solution)/shard_map/ppermute | solution.py:1003
  519.5 25.1 %collective-permute-start.53 = (bf16[5,652,384]{2,1,0:T(8,128)(2,1)}, bf16[5,652,384]{2,1,0:T(8,128)(2,1)S(1)}, u32[]{:S(2)}, u32[]{:S(2)}) collective-permute-start(bf16[5,652,384]{2,1,0:T(8,128)(2,1)} %get-tuple-element.155), channel_id=1, source_target_pairs={{0,16},{16,0},{1,17},{17,1},{2,18},{18,2},{3,19},{19,3},{4,20},{20... | collective-permute-start | bytes 7511048 | tf_op jit(solution)/shard_map/ppermute | solution.py:1003
  521.8 19.2 %collective-permute-start.57 = (bf16[384,384]{1,0:T(8,128)(2,1)}, bf16[384,384]{1,0:T(8,128)(2,1)S(1)}, u32[]{:S(2)}, u32[]{:S(2)}) collective-permute-start(bf16[384,384]{1,0:T(8,128)(2,1)} %get-tuple-element.157), channel_id=1, source_target_pairs={{0,16},{16,0},{1,17},{17,1},{2,18},{18,2},{3,19},{19,3},{4,20},{20... | collective-permute-start | bytes 884744 | tf_op jit(solution)/shard_map/ppermute | solution.py:1003
  522.3 19.8 %collective-permute-start.55 = (bf16[3,384,384]{2,1,0:T(8,128)(2,1)}, bf16[3,384,384]{2,1,0:T(8,128)(2,1)S(1)}, u32[]{:S(2)}, u32[]{:S(2)}) collective-permute-start(bf16[3,384,384]{2,1,0:T(8,128)(2,1)} %get-tuple-element.156), channel_id=1, source_target_pairs={{0,16},{16,0},{1,17},{17,1},{2,18},{18,2},{3,19},{19,3},{4,20},{20... | collective-permute-start | bytes 2654216 | tf_op jit(solution)/shard_map/ppermute | solution.py:1003
  (20 other events, 415.3 us)
Sparse Core Ops, SparseCore 0:
  362.6 156.8 all-reduce.2
where the time goes:
time: 559 us; the launch traced here: 558 us
  Pallas kernels  336 us (60%)
  waiting for transfers between devices  101 us (18%)
  starting transfers between devices  74.3 us (13%)
  other arithmetic  26.6 us (5%)
  between operations  14.3 us (3%)
    pallas_call x1, Pallas kernels, shards(): weights_first(micro, c_in, c_mid, taps, pooled, c_lane)  67.9 us
    ppermute x50, starting transfers between devices, share(): lax.ppermute(rows, BOTH, [(i, i ^ mask) for i in range(devices)])  65.2 us
    pallas_call x1, Pallas kernels, shards(): backward_first(micro, c_in, c_mid, taps, pooled, c_lane)  63.2 us
    pallas_call x1, Pallas kernels, shards(): forward_first(micro, c_in, c_mid, taps, pooled)  61.9 us
    psum x1, waiting for transfers between devices, shards(): half_first = lax.psum((first_own + partner(first_send)).astype(BF16), 'dp')  53.7 us
    pallas_call x1, Pallas kernels, shards(): backward_second(micro, c_in, c_mid, c_res, taps_b, pooled, c_lane)  34.1 us
    ppermute x50, waiting for transfers between devices, share(): lax.ppermute(rows, BOTH, [(i, i ^ mask) for i in range(devices)])  32 us
    pallas_call x1, Pallas kernels, shards(): turn_point(micro, c_in, c_mid, c_res, pooled, c_lane)  24.8 us
  transfers between devices with their start and end apart: 60, of which 23 were waited for; matrix products, arithmetic and copies ran while one was open for 2% of the time, Pallas kernels for 20%

commit v1 on v0

--- a/solution.py
+++ b/solution.py
@@ -133,9 +133,15 @@
     return jax.ShapeDtypeStruct(shape, dtype)
 
 
-def call(name, body, grid, in_specs, out_specs, out_shape, scratch=(), limit=58):
+def call(name, body, grid, in_specs, out_specs, out_shape, scratch=(), limit=58, after=0):
+    real = len(in_specs) + 1
+
+    def ordered(*refs):
+        body(*refs[:real], *refs[real + after :])
+
+    in_specs = list(in_specs) + [pl.BlockSpec(memory_space=pl.ANY)] * after
     return pl.pallas_call(
-        body,
+        ordered,
         grid_spec=pltpu.PrefetchScalarGridSpec(
             num_scalar_prefetch=1,
             grid=grid,
@@ -300,70 +306,108 @@
     )
 
 
+def activate(micro, c_in, taps, pooled):
+    c_pad = up(c_in, 16)
+    c_lane = up(c_in, LANES)
+    extra = up(taps * c_pad, TILE) - taps * c_pad
+    stack_rows = (taps + 1) * c_pad + extra
+
+    def body(info, x_ref, sums, table, stack, col_c, col_s, col_h):
+        k = pl.program_id(0)
+        length = info[1 + k]
+        (centre, _, inverse), _, _ = first_rows(sums, k, c_in)
+        col_c[...] = column(centre)
+        col_s[...] = column(inverse * table[0:1, :])
+
+        @pl.when(k == 0)
+        def _():
+            col_h[...] = column(table[1:2, :])
+
+        stack[0, (taps + 1) * c_pad :, :] = jnp.zeros((extra, pooled), BF16)
+        masks = pool_mask(length, pooled), odd_mask(length, pooled)
+
+        def rows_body(rows, start):
+            c, s, h = (wide(r[rows, :], TILE) for r in (col_c, col_s, col_h))
+            here = lambda seg: pl.ds(aligned(seg * c_pad + start), 16)
+            for half in range(2):
+                parts = []
+                for lane in range(0, pooled, TILE):
+                    lanes = slice(lane, lane + TILE)
+                    v = (x_ref[0, half, rows, lanes].astype(F32) - c) * s + h
+                    parts.append((gelu(v) * masks[half][:, lanes]).astype(BF16))
+                a = jnp.concatenate(parts, axis=1)
+                stack[0, here(half), :] = before(a)
+                stack[0, here(2 + half), :] = a
+                stack[0, here(4 + half), :] = after(a)
+
+        each_rows(c_pad, rows_body, 8)
+
+    return call(
+        "activate",
+        body,
+        (micro,),
+        [per_batch((2, c_pad, pooled)), whole((8, c_lane)), whole((8, c_lane))],
+        per_batch((stack_rows, pooled)),
+        shape_of((micro, stack_rows, pooled), BF16),
+        [pltpu.VMEM((c_lane, LANES), F32)] * 3,
+    )
+
+
+def lane_blocks(shape, steps, last, late):
+    def place(s, _):
+        s = jnp.maximum(s - 1, 0) if late else jnp.minimum(s, last)
+        return (s // steps,) + (0,) * (len(shape) - 1) + (s % steps,)
+
+    return pl.BlockSpec((1,) + shape, place)
+
+
 def forward_first(micro, c_in, c_mid, taps, pooled):
     c_pad = up(c_in, 16)
     c_lane = up(c_in, LANES)
     depth = up(taps * c_pad, TILE)
-    extra = depth - taps * c_pad
     steps = pooled // TILE
-    stack_rows = (taps + 1) * c_pad + extra
-
-    def body(info, x_ref, sums, table, weight, hid, diff, act, st_ref,
-             stack, col_c, col_s, col_h, bias, s_acc, q_acc, even, odd):
-        k, at = pl.program_id(0), pl.program_id(1)
-        length = info[1 + k]
-
-        @pl.when((at == 0) & (k == 0))
-        def _():
-            stack[(taps + 1) * c_pad :, :] = jnp.zeros((extra, pooled), BF16)
-            col_h[...] = column(table[1:2, :])
+    total = micro * steps
+    stack_rows = c_pad + depth
+
+    def body(info, stack, table, weight, hid, diff, st_ref, bias, s_acc, q_acc, even, odd):
+        step = pl.program_id(0)
+        late = jnp.maximum(step - 1, 0)
+        k, at = late // steps, late % steps
+        mask = pool_mask(info[1 + k], TILE, at * TILE)
+
+        @pl.when(step == 0)
+        def _():
             bias[...] = column(table[2:3, :c_mid])
             st_ref[...] = jnp.zeros_like(st_ref)
 
         @pl.when(at == 0)
         def _():
-            (centre, _, inverse), _, _ = first_rows(sums, k, c_in)
-            col_c[...] = column(centre)
-            col_s[...] = column(inverse * table[0:1, :])
             s_acc[...] = jnp.zeros_like(s_acc)
             q_acc[...] = jnp.zeros_like(q_acc)
-            masks = pool_mask(length, pooled), odd_mask(length, pooled)
-
-            def rows_body(rows, start):
-                c, s, h = (wide(r[rows, :], TILE) for r in (col_c, col_s, col_h))
-                here = lambda seg: pl.ds(aligned(seg * c_pad + start), 16)
-                for half in range(2):
-                    parts = []
-                    for lane in range(0, pooled, TILE):
-                        lanes = slice(lane, lane + TILE)
-                        v = (x_ref[0, half, rows, lanes].astype(F32) - c) * s + h
-                        parts.append((gelu(v) * masks[half][:, lanes]).astype(BF16))
-                    a = jnp.concatenate(parts, axis=1)
-                    act[0, half, rows, :] = a
-                    stack[here(half), :] = before(a)
-                    stack[here(2 + half), :] = a
-                    stack[here(4 + half), :] = after(a)
-
-            each_rows(c_pad, rows_body, 4)
-
-        lanes = pl.ds(pl.multiple_of(at * TILE, TILE), TILE)
-        even[...] = nn(weight[...], stack[:depth, lanes])
-        odd[...] = nn(weight[...], stack[c_pad : c_pad + depth, lanes])
-        mask = pool_mask(length, TILE, at * TILE)
-
-        def rows_body(rows, start):
-            b = wide(bias[rows, :], TILE)
-            left, right = even[rows, :] + b, odd[rows, :] + b
-            apart = left - right
-            joined = jnp.maximum(left, right) + jnp.log1p(jnp.exp(-jnp.abs(apart)))
-            rounded = (joined * mask).astype(BF16)
-            diff[0, rows, :] = apart
-            hid[0, rows, :] = rounded
-            value = rounded.astype(F32)
-            s_acc[rows, :] += fold(value)
-            q_acc[rows, :] += fold(value * value)
-
-        each_rows(c_mid, rows_body, 12)
+
+        def finish():
+            for start in range(0, c_mid, 16):
+                rows = slice(start, start + 16)
+                b = wide(bias[rows, :], TILE)
+                left, right = even[rows, :] + b, odd[rows, :] + b
+                apart = left - right
+                joined = jnp.maximum(left, right) + jnp.log1p(jnp.exp(-jnp.abs(apart)))
+                rounded = (joined * mask).astype(BF16)
+                diff[0, rows, :] = apart
+                hid[0, rows, :] = rounded
+                value = rounded.astype(F32)
+                s_acc[rows, :] += fold(value)
+                q_acc[rows, :] += fold(value * value)
+
+        @pl.when(step < total)
+        def _():
+            finish()
+            even[...] = nn(weight[...], stack[0, :depth, :])
+            odd[...] = nn(weight[...], stack[0, c_pad : c_pad + depth, :])
+
+        @pl.when(step == total)
+        def _():
+            finish()
 
         @pl.when(at == steps - 1)
         def _():
@@ -372,29 +416,23 @@
     return call(
         "forward_first",
         body,
-        (micro, steps),
-        [
-            per_batch((2, c_pad, pooled)),
-            whole((8, c_lane)),
+        (total + 1,),
+        [
+            lane_blocks((stack_rows, TILE), steps, total - 1, False),
             whole((8, c_lane)),
             whole((c_mid, depth), 1),
         ],
         [
-            per_lanes((c_mid, TILE)),
-            per_lanes((c_mid, TILE)),
-            per_batch((2, c_pad, pooled)),
+            lane_blocks((c_mid, TILE), steps, total - 1, True),
+            lane_blocks((c_mid, TILE), steps, total - 1, True),
             whole((8, c_mid)),
         ],
         [
             shape_of((micro, c_mid, pooled), BF16),
             shape_of((micro, c_mid, pooled)),
-            shape_of((micro, 2, c_pad, pooled), BF16),
             shape_of((8, c_mid)),
         ],
-        [pltpu.VMEM((stack_rows, pooled), BF16)]
-        + [pltpu.VMEM((c_lane, LANES), F32)] * 3
-        + [pltpu.VMEM((c_mid, LANES), F32)] * 3
-        + [pltpu.VMEM((c_mid, TILE), F32)] * 2,
+        [pltpu.VMEM((c_mid, LANES), F32)] * 3 + [pltpu.VMEM((c_mid, TILE), F32)] * 2,
     )
 
 
@@ -461,18 +499,44 @@
         [pltpu.VMEM((taps * c_mid, pooled), BF16)]
         + [pltpu.VMEM((c_mid, LANES), F32)] * 3
         + [pltpu.VMEM((c_res, LANES), F32)] * 2,
-    )
-
-
-def turn_point(micro, c_in, c_mid, c_res, pooled, c_lane):
-    half = c_mid // 2
-
-    def body(info, conv, sums_a, sums, table, hid, cot, point_t, point,
-             own, send, go, d_out, st_ref, point_own, point_send, grad_bias,
-             act, up_grad, branch, flat, bias, col_c, col_s, col_h, s_acc, q_acc, product):
+        after=1,
+    )
+
+
+def turn_cotangent(micro, c_mid, c_res, pooled):
+    def body(info, cot, point, go, up_grad, grad_bias):
         k = pl.program_id(0)
-        section, length = info[0], info[1 + k]
-        first = section == 0
+        mask = pool_mask(info[1 + k], pooled)
+        eye = identity()
+        up_grad[0] = nt(point[...], cot[0, 0])
+        for at in range(0, c_mid, TILE):
+            go[0, at : at + TILE, :] = (nt(eye, cot[0, 0, :, at : at + TILE]) * mask).astype(BF16)
+        ones = jnp.broadcast_to(mask, (16, pooled)).astype(BF16)
+        total = nn(ones, cot[0, 0])[:8]
+        grad_bias[...] = total + jnp.where(k == 0, 0.0, grad_bias[...])
+
+    return call(
+        "turn_cotangent",
+        body,
+        (micro,),
+        [
+            pl.BlockSpec((1, 1, pooled, c_mid), lambda k, info: (k, info[0], 0, 0)),
+            whole((c_res, c_mid), 1),
+        ],
+        [per_batch((c_mid, pooled)), per_batch((c_res, pooled)), whole((8, c_mid))],
+        [
+            shape_of((micro, c_mid, pooled), BF16),
+            shape_of((micro, c_res, pooled)),
+            shape_of((8, c_mid)),
+        ],
+    )
+
+
+def norm_third(micro, c_in, c_res, pooled, c_lane):
+    def body(info, conv, up_grad, sums_a, sums, table, act, d_out, st_ref,
+             col_c, col_s, col_h, s_acc, q_acc):
+        k = pl.program_id(0)
+        length = info[1 + k]
         _, _, count = first_rows(sums_a, k, c_in)
         centre, _, inverse = finish_rows(row_pair(sums, k), count)
         col_c[...] = column(centre)
@@ -481,13 +545,9 @@
         @pl.when(k == 0)
         def _():
             col_h[...] = column(table[6:7, :c_res])
-            bias[...] = column(table[7:8, :c_mid])
-            product[...] = jnp.zeros_like(product)
-            grad_bias[...] = jnp.zeros_like(grad_bias)
             st_ref[...] = jnp.zeros_like(st_ref)
 
         mask = pool_mask(length, pooled)
-        up_grad[...] = nt(point[...], cot[0, 0])
 
         def rows_body(rows, start):
             c, s, h = (wide(r[rows, :], TILE) for r in (col_c, col_s, col_h))
@@ -496,22 +556,60 @@
                 lanes = slice(lane, lane + TILE)
                 apart = conv[0, rows, lanes] - c
                 a, slope = gelu_slope(apart * s + h)
-                act[rows, lanes] = (a * mask[:, lanes]).astype(BF16)
-                d = mask[:, lanes] * slope * up_grad[rows, lanes]
+                act[0, rows, lanes] = (a * mask[:, lanes]).astype(BF16)
+                d = mask[:, lanes] * slope * up_grad[0, rows, lanes]
                 d_out[0, rows, lanes] = d
                 total_s.append(fold(d))
                 total_q.append(fold(d * apart))
             s_acc[rows, :] = sum(total_s)
             q_acc[rows, :] = sum(total_q)
 
-        each_rows(c_res, rows_body, 4)
+        each_rows(c_res, rows_body, 8)
         put_rows(st_ref, k, as_row(s_acc[...]), as_row(q_acc[...]) * inverse)
-        branch[...] = nn(point_t[...], act[...])
+
+    return call(
+        "norm_third",
+        body,
+        (micro,),
+        [
+            per_batch((c_res, pooled)),
+            per_batch((c_res, pooled)),
+            whole((8, c_lane)),
+            whole((8, c_res)),
+            whole((8, c_lane)),
+        ],
+        [per_batch((c_res, pooled)), per_batch((c_res, pooled)), whole((8, c_res))],
+        [
+            shape_of((micro, c_res, pooled), BF16),
+            shape_of((micro, c_res, pooled)),
+            shape_of((8, c_res)),
+        ],
+        [pltpu.VMEM((c_res, LANES), F32)] * 5,
+    )
+
+
+def point_output(micro, c_mid, c_res, pooled, c_lane):
+    half = c_mid // 2
+
+    def body(info, act, hid, cot, table, point_t, own, send, grad_point,
+             branch, flat, bias, product):
+        k = pl.program_id(0)
+        first = info[0] == 0
+        mask = pool_mask(info[1 + k], pooled)
+
+        @pl.when(k == 0)
+        def _():
+            bias[...] = column(table[7:8, :c_mid])
+
+        branch[...] = nn(point_t[...], act[0])
+        total = nn(act[0], cot[0, 0]) + jnp.where(k == 0, 0.0, product[...])
+        product[...] = total
+        grad_point[...] = total.astype(BF16)
 
         def out_body(rows, start):
             b = wide(bias[rows, :], pooled)
-            total = hid[0, rows, :].astype(F32) + (branch[rows, :] + b)
-            flat[rows, :] = (total * mask).astype(BF16)
+            value = hid[0, rows, :].astype(F32) + (branch[rows, :] + b)
+            flat[rows, :] = (value * mask).astype(BF16)
 
         each_rows(c_mid, out_body, 8)
         eye = identity()
@@ -520,74 +618,39 @@
             low, high = turned[:, :half], turned[:, half:]
             own[0, at : at + TILE, :] = jnp.where(first, low, high)
             send[0, at : at + TILE, :] = jnp.where(first, high, low)
-        for at in range(0, c_mid, TILE):
-            go[0, at : at + TILE, :] = (nt(eye, cot[0, 0, :, at : at + TILE]) * mask).astype(BF16)
-        product[...] += nn(act[...], cot[0, 0])
-        ones = jnp.broadcast_to(mask, (16, pooled)).astype(BF16)
-        grad_bias[...] += nn(ones, cot[0, 0])[:8]
-
-        @pl.when(k == micro - 1)
-        def _():
-            low, high = product[:, :half], product[:, half:]
-            point_own[...] = jnp.where(first, low, high)
-            point_send[...] = jnp.where(first, high, low).astype(BF16)
-
-    in_specs = [
-        per_batch((c_res, pooled)),
-        whole((8, c_lane)),
-        whole((8, c_res)),
-        whole((8, c_lane)),
-        per_batch((c_mid, pooled)),
-        pl.BlockSpec((1, 1, pooled, c_mid), lambda k, info: (k, info[0], 0, 0)),
-        whole((c_mid, c_res), 1),
-        whole((c_res, c_mid), 1),
-    ]
-    return call(
-        "turn_point",
+
+    return call(
+        "point_output",
         body,
         (micro,),
-        in_specs,
-        [
-            per_batch((pooled, half)),
-            per_batch((pooled, half)),
+        [
+            per_batch((c_res, pooled)),
             per_batch((c_mid, pooled)),
-            per_batch((c_res, pooled)),
-            whole((8, c_res)),
-            whole((c_res, half)),
-            whole((c_res, half)),
-            whole((8, c_mid)),
-        ],
+            pl.BlockSpec((1, 1, pooled, c_mid), lambda k, info: (k, info[0], 0, 0)),
+            whole((8, c_lane)),
+            whole((c_mid, c_res), 1),
+        ],
+        [per_batch((pooled, half)), per_batch((pooled, half)), whole((c_res, c_mid))],
         [
             shape_of((micro, pooled, half), BF16),
             shape_of((micro, pooled, half), BF16),
-            shape_of((micro, c_mid, pooled), BF16),
-            shape_of((micro, c_res, pooled)),
-            shape_of((8, c_res)),
-            shape_of((c_res, half)),
-            shape_of((c_res, half), BF16),
-            shape_of((8, c_mid)),
-        ],
-        [
-            pltpu.VMEM((c_res, pooled), BF16),
-            pltpu.VMEM((c_res, pooled), F32),
+            shape_of((c_res, c_mid), BF16),
+        ],
+        [
             pltpu.VMEM((c_mid, pooled), F32),
             pltpu.VMEM((c_mid, pooled), BF16),
             pltpu.VMEM((c_mid, LANES), F32),
-        ]
-        + [pltpu.VMEM((c_res, LANES), F32)] * 5
-        + [pltpu.VMEM((c_res, c_mid), F32)],
+            pltpu.VMEM((c_res, c_mid), F32),
+        ],
     )
 
 
 def backward_second(micro, c_in, c_mid, c_res, taps, pooled, c_lane):
-    half = c_mid // 2
-
-    def body(info, d_in, conv, sums_a, sums_b, sums_c, back, table, hid, act, weight,
-             d_out, st_ref, conv_own, conv_send,
-             stack, up_grad, product, col_a, col_b, col_0, col_r, col_c, col_s, col_h, s_acc, q_acc):
+    def body(info, d_in, conv, sums_a, sums_b, sums_c, back, table, hid, weight,
+             d_out, st_ref, stack,
+             up_grad, col_a, col_b, col_0, col_r, col_c, col_s, col_h, s_acc, q_acc):
         k = pl.program_id(0)
         length = info[1 + k]
-        first = info[0] == 0
         _, _, count = first_rows(sums_a, k, c_in)
         centre, _, inverse = finish_rows(row_pair(sums_c, k), count)
         outer, slant, level = back_rows(row_pair(back, k), count, table[5:6, :c_res], inverse)
@@ -602,7 +665,6 @@
         @pl.when(k == 0)
         def _():
             col_h[...] = column(table[4:5, :c_mid])
-            product[...] = jnp.zeros_like(product)
             st_ref[...] = jnp.zeros_like(st_ref)
 
         mask = pool_mask(length, pooled)
@@ -612,13 +674,13 @@
             g = (a * d_in[0, rows, :] - b * (conv[0, rows, :] - c) - z) * mask
             g = g.astype(BF16)
             here = lambda seg: pl.ds(aligned(seg * c_res + start), 16)
-            stack[here(0), :] = after(g)
-            stack[here(1), :] = g
-            stack[here(2), :] = before(g)
+            stack[0, here(0), :] = after(g)
+            stack[0, here(1), :] = g
+            stack[0, here(2), :] = before(g)
 
         each_rows(c_res, rows_body, 8)
         for at in range(0, pooled, TILE):
-            up_grad[:, at : at + TILE] = nn(weight[...], stack[:, at : at + TILE])
+            up_grad[:, at : at + TILE] = nn(weight[...], stack[0, :, at : at + TILE])
 
         def slope_body(rows, start):
             c, s, h = (wide(r[rows, :], TILE) for r in (col_c, col_s, col_h))
@@ -634,17 +696,8 @@
             s_acc[rows, :] = sum(total_s)
             q_acc[rows, :] = sum(total_q)
 
-        each_rows(c_mid, slope_body, 4)
+        each_rows(c_mid, slope_body, 8)
         put_rows(st_ref, k, as_row(s_acc[...]), as_row(q_acc[...]) * inverse)
-        for tap in range(taps):
-            product[tap] += nt(act[0], stack[tap * c_res : (tap + 1) * c_res, :])
-
-        @pl.when(k == micro - 1)
-        def _():
-            for tap in range(taps):
-                low, high = product[tap, :half, :], product[tap, half:, :]
-                conv_own[tap] = jnp.where(first, low, high)
-                conv_send[tap] = jnp.where(first, high, low).astype(BF16)
 
     in_specs = [
         per_batch((c_res, pooled)),
@@ -655,7 +708,6 @@
         whole((8, c_res)),
         whole((8, c_lane)),
         per_batch((c_mid, pooled)),
-        per_batch((c_mid, pooled)),
         whole((c_mid, taps * c_res), 1),
     ]
     return call(
@@ -663,111 +715,84 @@
         body,
         (micro,),
         in_specs,
-        [
-            per_batch((c_mid, pooled)),
-            whole((8, c_mid)),
-            whole((taps, half, c_res)),
-            whole((taps, half, c_res)),
-        ],
+        [per_batch((c_mid, pooled)), whole((8, c_mid)), per_batch((taps * c_res, pooled))],
         [
             shape_of((micro, c_mid, pooled)),
             shape_of((8, c_mid)),
-            shape_of((taps, half, c_res)),
-            shape_of((taps, half, c_res), BF16),
-        ],
-        [
-            pltpu.VMEM((taps * c_res, pooled), BF16),
-            pltpu.VMEM((c_mid, pooled), F32),
-            pltpu.VMEM((taps, c_mid, c_res), F32),
-        ]
+            shape_of((micro, taps * c_res, pooled), BF16),
+        ],
+        [pltpu.VMEM((c_mid, pooled), F32)]
         + [pltpu.VMEM((c_res, LANES), F32)] * 4
         + [pltpu.VMEM((c_mid, LANES), F32)] * 5,
-    )
-
-
-def stack_gradient(stack, half, here, gradient):
-    order = 3 - half
-    stack[here(order - 2), :] = after(gradient)
-    stack[here(order), :] = gradient
-    stack[here(order + 2), :] = before(gradient)
-
-
-def weights_first(micro, c_in, c_mid, taps, pooled, c_lane):
-    c_pad = up(c_in, 16)
-    half = c_mid // 2
-
-    def body(info, d_in, hid, go, diff, sums_a, sums_b, back, table, act,
-             g_out, bias_out, conv_own, conv_send,
-             stack, product, col_a, col_b, col_0, col_c, s_acc):
-        k, at = pl.program_id(0), pl.program_id(1)
+        after=1,
+    )
+
+
+def weights_second(micro, c_mid, c_res, taps, pooled):
+    def body(info, act, stack, grad_conv, product):
+        k = pl.program_id(0)
+        for tap in range(taps):
+            value = nt(act[0], stack[0, tap * c_res : (tap + 1) * c_res, :])
+            value += jnp.where(k == 0, 0.0, product[tap])
+            product[tap] = value
+            grad_conv[tap] = value.astype(BF16)
+
+    return call(
+        "weights_second",
+        body,
+        (micro,),
+        [per_batch((c_mid, pooled)), per_batch((taps * c_res, pooled))],
+        whole((taps, c_mid, c_res)),
+        shape_of((taps, c_mid, c_res), BF16),
+        [pltpu.VMEM((taps, c_mid, c_res), F32)],
+    )
+
+
+def gradient_first(micro, c_in, c_mid, taps, pooled, c_lane):
+    def body(info, d_in, hid, go, diff, sums_a, sums_b, back, table,
+             stack, bias_out, col_a, col_b, col_0, col_c, s_acc):
+        k = pl.program_id(0)
         length = info[1 + k]
-        first = info[0] == 0
-
-        @pl.when((at == 0) & (k == 0))
-        def _():
-            bias_out[...] = jnp.zeros_like(bias_out)
-
-        @pl.when(at == 0)
-        def _():
-            _, _, count = first_rows(sums_a, k, c_in)
-            centre, _, inverse = finish_rows(row_pair(sums_b, k), count)
-            outer, slant, level = back_rows(row_pair(back, k), count, table[3:4, :c_mid], inverse)
-            col_a[...] = column(outer)
-            col_b[...] = column(slant)
-            col_0[...] = column(level)
-            col_c[...] = column(centre)
-            mask = pool_mask(length, pooled)
-
-            def rows_body(rows, start):
-                a, b, z, c = (wide(r[rows, :], TILE) for r in (col_a, col_b, col_0, col_c))
-                lefts, rights, totals = [], [], []
-                for lane in range(0, pooled, TILE):
-                    lanes = slice(lane, lane + TILE)
-                    field = a * d_in[0, rows, lanes] - b * (hid[0, rows, lanes].astype(F32) - c) - z
-                    g = field * mask[:, lanes] + go[0, rows, lanes].astype(F32)
-                    g = g.astype(BF16).astype(F32)
-                    apart = diff[0, rows, lanes]
-                    small = jnp.exp(-jnp.abs(apart))
-                    large = 1.0 / (1.0 + small)
-                    small = small * large
-                    positive = apart >= 0.0
-                    left = (g * jnp.where(positive, large, small)).astype(BF16)
-                    right = (g * jnp.where(positive, small, large)).astype(BF16)
-                    lefts.append(left)
-                    rights.append(right)
-                    totals.append(fold(left.astype(F32) + right.astype(F32)))
-                s_acc[rows, :] = sum(totals)
-                here = lambda seg: pl.ds(aligned(seg * c_mid + start), 16)
-                for side, parts in enumerate((lefts, rights)):
-                    joined = jnp.concatenate(parts, axis=1)
-                    g_out[0, side, rows, :] = joined
-                    stack_gradient(stack, side, here, joined)
-
-            each_rows(c_mid, rows_body, 4)
-            bias_out[...] += as_row(s_acc[...])
-
-        even = pl.ds(pl.multiple_of((at + 1) * c_mid, c_mid), c_mid)
-        odd = pl.ds(pl.multiple_of(at * c_mid, c_mid), c_mid)
-        value = nt(act[0, 0], stack[even, :]) + nt(act[0, 1], stack[odd, :])
-
-        @pl.when(k == 0)
-        def _():
-            product[at] = value
-
-        @pl.when((k > 0) & (k < micro - 1))
-        def _():
-            product[at] += value
-
-        @pl.when(k == micro - 1)
-        def _():
-            total = (product[at] + value)[:c_in]
-            low, high = total[:, :half], total[:, half:]
-            conv_own[0] = jnp.where(first, low, high)
-            conv_send[0] = jnp.where(first, high, low).astype(BF16)
-
-    block = pl.BlockSpec(
-        (1, c_in, half), lambda k, j, _: (jnp.where(k == micro - 1, j, 0), 0, 0)
-    )
+        _, _, count = first_rows(sums_a, k, c_in)
+        centre, _, inverse = finish_rows(row_pair(sums_b, k), count)
+        outer, slant, level = back_rows(row_pair(back, k), count, table[3:4, :c_mid], inverse)
+        col_a[...] = column(outer)
+        col_b[...] = column(slant)
+        col_0[...] = column(level)
+        col_c[...] = column(centre)
+        mask = pool_mask(length, pooled)
+
+        def rows_body(rows, start):
+            a, b, z, c = (wide(r[rows, :], TILE) for r in (col_a, col_b, col_0, col_c))
+            lefts, rights, totals = [], [], []
+            for lane in range(0, pooled, TILE):
+                lanes = slice(lane, lane + TILE)
+                field = a * d_in[0, rows, lanes] - b * (hid[0, rows, lanes].astype(F32) - c) - z
+                g = field * mask[:, lanes] + go[0, rows, lanes].astype(F32)
+                g = g.astype(BF16).astype(F32)
+                apart = diff[0, rows, lanes]
+                small = jnp.exp(-jnp.abs(apart))
+                large = 1.0 / (1.0 + small)
+                small = small * large
+                positive = apart >= 0.0
+                left = (g * jnp.where(positive, large, small)).astype(BF16)
+                right = (g * jnp.where(positive, small, large)).astype(BF16)
+                lefts.append(left)
+                rights.append(right)
+                totals.append(fold(left.astype(F32) + right.astype(F32)))
+            s_acc[rows, :] = sum(totals)
+            here = lambda seg: pl.ds(aligned(seg * c_mid + start), 16)
+            for side, parts in enumerate((lefts, rights)):
+                joined = jnp.concatenate(parts, axis=1)
+                order = 3 - side
+                stack[0, here(order - 2), :] = after(joined)
+                stack[0, here(order), :] = joined
+                stack[0, here(order + 2), :] = before(joined)
+
+        each_rows(c_mid, rows_body, 6)
+        bias_out[...] = as_row(s_acc[...]) + jnp.where(k == 0, 0.0, bias_out[...])
+
+    rows = (taps + 1) * c_mid
     in_specs = [
         per_batch((c_mid, pooled)),
         per_batch((c_mid, pooled)),
@@ -777,38 +802,69 @@
         whole((8, c_mid)),
         whole((8, c_mid)),
         whole((8, c_lane)),
-        per_batch((2, c_pad, pooled)),
     ]
     return call(
+        "gradient_first",
+        body,
+        (micro,),
+        in_specs,
+        [per_batch((rows, pooled)), whole((8, c_mid))],
+        [shape_of((micro, rows, pooled), BF16), shape_of((8, c_mid))],
+        [pltpu.VMEM((c_mid, LANES), F32)] * 5,
+        after=1,
+    )
+
+
+def weights_first(micro, c_in, c_mid, pooled, tap_from, tap_to):
+    c_pad = up(c_in, 16)
+    count = tap_to - tap_from
+
+    def body(info, act_left, act_right, left, right, grad_conv, product):
+        k, at = pl.program_id(0), pl.program_id(1)
+        value = nt(act_left[0], left[0]) + nt(act_right[0], right[0])
+        value += jnp.where(k == 0, 0.0, product[at])
+        product[at] = value
+        grad_conv[0] = value[:c_in].astype(BF16)
+
+    def act_block(shift):
+        return pl.BlockSpec((1, c_pad, pooled), lambda k, j, _: (k, j + tap_from + shift, 0))
+
+    def grad_block(segment):
+        return pl.BlockSpec((1, c_mid, pooled), lambda k, j, _: (k, segment, 0))
+
+    return call(
         "weights_first",
         body,
-        (micro, taps),
-        in_specs,
-        [per_batch((2, c_mid, pooled)), whole((8, c_mid)), block, block],
-        [
-            shape_of((micro, 2, c_mid, pooled), BF16),
-            shape_of((8, c_mid)),
-            shape_of((taps, c_in, half)),
-            shape_of((taps, c_in, half), BF16),
-        ],
-        [pltpu.VMEM(((taps + 1) * c_mid, pooled), BF16), pltpu.VMEM((taps, c_pad, c_mid), F32)]
-        + [pltpu.VMEM((c_mid, LANES), F32)] * 5,
+        (micro, count),
+        [act_block(0), act_block(1), grad_block(3), grad_block(2)],
+        pl.BlockSpec(
+            (1, c_in, c_mid), lambda k, j, _: (jnp.where(k == micro - 1, j, 0), 0, 0)
+        ),
+        shape_of((count, c_in, c_mid), BF16),
+        [pltpu.VMEM((count, c_pad, c_mid), F32)],
+        after=1,
     )
 
 
 def backward_first(micro, c_in, c_mid, taps, pooled, c_lane):
     c_pad = up(c_in, 16)
     steps = pooled // TILE
-
-    def body(info, g_in, x_ref, sums_a, table, weight, bias_first, bias_point, d_out, st_ref,
-             stack, even, odd, col_c, col_s, col_h, s_acc, q_acc):
-        k, at = pl.program_id(0), pl.program_id(1)
+    total = micro * steps
+    depth = taps * c_mid
+
+    def body(info, stack, x_ref, sums_a, table, weight, bias_first, bias_point, d_out, st_ref,
+             even, odd, col_c, col_s, col_h, s_acc, q_acc):
+        step = pl.program_id(0)
+        late = jnp.maximum(step - 1, 0)
+        k, at = late // steps, late % steps
         length = info[1 + k]
         (centre, _, inverse), _, _ = first_rows(sums_a, k, c_in)
-
-        @pl.when((at == 0) & (k == 0))
+        masks = pool_mask(length, TILE, at * TILE), odd_mask(length, TILE, at * TILE)
+
+        @pl.when(step == 0)
         def _():
             col_h[...] = column(table[1:2, :])
+            st_ref[...] = jnp.zeros_like(st_ref)
             st_ref[2 * micro : 2 * micro + 1, :] = bias_first[0:1, :]
             st_ref[2 * micro + 1 : 2 * micro + 2, :] = bias_point[0:1, :]
 
@@ -819,30 +875,27 @@
             s_acc[...] = jnp.zeros_like(s_acc)
             q_acc[...] = jnp.zeros_like(q_acc)
 
-            def rows_body(rows, start):
-                here = lambda seg: pl.ds(aligned(seg * c_mid + start), 16)
-                stack_gradient(stack, 0, here, g_in[0, 0, rows, :])
-                stack_gradient(stack, 1, here, g_in[0, 1, rows, :])
-
-            each_rows(c_mid, rows_body, 8)
-
-        lanes = pl.ds(pl.multiple_of(at * TILE, TILE), TILE)
-        depth = taps * c_mid
-        even[...] = nn(weight[...], stack[c_mid : c_mid + depth, lanes])
-        odd[...] = nn(weight[...], stack[:depth, lanes])
-        masks = pool_mask(length, TILE, at * TILE), odd_mask(length, TILE, at * TILE)
-
-        def rows_body(rows, start):
-            c, s, h = (wide(r[rows, :], TILE) for r in (col_c, col_s, col_h))
-            for half, upstream in enumerate((even, odd)):
-                apart = x_ref[0, half, rows, :].astype(F32) - c
-                _, slope = gelu_slope(apart * s + h)
-                d = masks[half] * slope * upstream[rows, :]
-                d_out[0, half, rows, :] = d
-                s_acc[rows, :] += fold(d)
-                q_acc[rows, :] += fold(d * apart)
-
-        each_rows(c_pad, rows_body, 10)
+        def finish():
+            for start in range(0, c_pad, 16):
+                rows = slice(start, start + 16)
+                c, s, h = (wide(r[rows, :], TILE) for r in (col_c, col_s, col_h))
+                for half, upstream in enumerate((even, odd)):
+                    apart = x_ref[0, half, rows, :].astype(F32) - c
+                    _, slope = gelu_slope(apart * s + h)
+                    d = masks[half] * slope * upstream[rows, :]
+                    d_out[0, half, rows, :] = d
+                    s_acc[rows, :] += fold(d)
+                    q_acc[rows, :] += fold(d * apart)
+
+        @pl.when(step < total)
+        def _():
+            finish()
+            even[...] = nn(weight[...], stack[0, c_mid : c_mid + depth, :])
+            odd[...] = nn(weight[...], stack[0, :depth, :])
+
+        @pl.when(step == total)
+        def _():
+            finish()
 
         @pl.when(at == steps - 1)
         def _():
@@ -851,24 +904,20 @@
     return call(
         "backward_first",
         body,
-        (micro, steps),
-        [
-            per_batch((2, c_mid, pooled)),
-            per_lanes((2, c_pad, TILE)),
+        (total + 1,),
+        [
+            lane_blocks((depth + c_mid, TILE), steps, total - 1, False),
+            lane_blocks((2, c_pad, TILE), steps, total - 1, True),
             whole((8, c_lane)),
             whole((8, c_lane)),
             whole((c_pad, taps * c_mid), 1),
             whole((8, c_mid)),
             whole((8, c_mid)),
         ],
-        [per_lanes((2, c_pad, TILE)), whole((8, c_lane))],
+        [lane_blocks((2, c_pad, TILE), steps, total - 1, True), whole((8, c_lane))],
         [shape_of((micro, 2, c_pad, pooled)), shape_of((8, c_lane))],
-        [
-            pltpu.VMEM(((taps + 1) * c_mid, pooled), BF16),
-            pltpu.VMEM((c_pad, TILE), F32),
-            pltpu.VMEM((c_pad, TILE), F32),
-        ]
-        + [pltpu.VMEM((c_lane, LANES), F32)] * 5,
+        [pltpu.VMEM((c_pad, TILE), F32)] * 2 + [pltpu.VMEM((c_lane, LANES), F32)] * 5,
+        after=1,
     )
 
 
@@ -1009,8 +1058,8 @@
     groups = [[bits[-1], bits[0]]]
     rest = bits[1:-1]
     while rest:
-        groups.append(rest[:3])
-        rest = rest[3:]
+        groups.append(rest[:2])
+        rest = rest[2:]
     for group in groups:
         masks = [0]
         for bit in group:
@@ -1023,12 +1072,6 @@
             parts = [a + b for a, b in zip(parts[::2], parts[1::2])]
         rows = parts[0]
     return rows
-
-
-def share_at_once(rows):
-    devices = lax.axis_size("section") * lax.axis_size("dp")
-    copies = jnp.broadcast_to(rows[None], (devices,) + rows.shape)
-    return jnp.sum(lax.all_to_all(copies, BOTH, 0, 0), axis=0)
 
 
 def shards(
@@ -1065,7 +1108,7 @@
     feats = features.transpose(0, 3, 1, 2)
 
     loaded, part = load_features(micro, bins, c_in)(info, feats)
-    sums_a = share_at_once(part)
+    sums_a = share(part)
     vectors = (
         gain_first, shift_first, bias_first, gain_second, shift_second, gain_third, shift_third,
         bias_point,
@@ -1073,34 +1116,43 @@
     first_t, first_b, second_t, second_b, point_t, table = prepare_weights(
         conv_first, conv_second, conv_point, vectors, c_lane
     )(info, conv_first, conv_second, conv_point, *vectors)
-    hid, diff, act_a, part = forward_first(micro, c_in, c_mid, taps, pooled)(
-        info, loaded, sums_a, table, first_t
-    )
+    act_a = activate(micro, c_in, taps, pooled)(info, loaded, sums_a, table)
+    hid, diff, part = forward_first(micro, c_in, c_mid, taps, pooled)(info, act_a, table, first_t)
     sums_b = share(part)
+    go, up_c, grad_bias = turn_cotangent(micro, c_mid, c_res, pooled)(info, cotangent, conv_point)
     conv_b, act_b, part = forward_second(micro, c_in, c_mid, c_res, taps_b, pooled, c_lane)(
-        info, hid, sums_a, sums_b, table, second_t
+        info, hid, sums_a, sums_b, table, second_t, grad_bias
     )
     sums_c = share(part)
-    own_out, send_out, go, d_c, part, point_own, point_send, grad_bias = turn_point(
-        micro, c_in, c_mid, c_res, pooled, c_lane
-    )(info, conv_b, sums_a, sums_c, table, hid, cotangent, point_t, conv_point)
+    act_c, d_c, part = norm_third(micro, c_in, c_res, pooled, c_lane)(
+        info, conv_b, up_c, sums_a, sums_c, table
+    )
     back_c = share(part)
+    own_out, send_out, grad_point = point_output(micro, c_mid, c_res, pooled, c_lane)(
+        info, act_c, hid, cotangent, table, point_t
+    )
     got_out = partner(send_out)
-    d_b, part, second_own, second_send = backward_second(
-        micro, c_in, c_mid, c_res, taps_b, pooled, c_lane
-    )(info, d_c, conv_b, sums_a, sums_b, sums_c, back_c, table, hid, act_b, second_b)
+    d_b, part, stack_b = backward_second(micro, c_in, c_mid, c_res, taps_b, pooled, c_lane)(
+        info, d_c, conv_b, sums_a, sums_b, sums_c, back_c, table, hid, second_b, grad_point
+    )
     back_b = share(part)
-    halves = [
-        (mine + partner(other)).astype(BF16)
-        for mine, other in ((second_own, second_send), (point_own, point_send))
-    ]
-    half_second, half_point = lax.psum(tuple(halves), "dp")
-    g_a, bias_sum, first_own, first_send = weights_first(micro, c_in, c_mid, taps, pooled, c_lane)(
-        info, d_b, hid, go, diff, sums_a, sums_b, back_b, table, act_a
-    )
-    half_first = lax.psum((first_own + partner(first_send)).astype(BF16), "dp")
+    grad_second = weights_second(micro, c_mid, c_res, taps_b, pooled)(info, act_b, stack_b)
+    sum_second, sum_point = lax.psum((grad_second, grad_point), BOTH)
+    stack_a, bias_sum = gradient_first(micro, c_in, c_mid, taps, pooled, c_lane)(
+        info, d_b, hid, go, diff, sums_a, sums_b, back_b, table, grad_second
+    )
+    cut = taps - taps // 2
+    lower = weights_first(micro, c_in, c_mid, pooled, 0, cut)(
+        info, act_a, act_a, stack_a, stack_a, bias_sum
+    )
+    upper = weights_first(micro, c_in, c_mid, pooled, cut, taps)(
+        info, act_a, act_a, stack_a, stack_a, lower
+    )
+    lower, _, _ = lax.optimization_barrier((lower, sum_second, sum_point))
+    sum_lower = lax.psum(lower, BOTH)
+    sum_upper = lax.psum(upper, BOTH[::-1])
     d_a, part = backward_first(micro, c_in, c_mid, taps, pooled, c_lane)(
-        info, g_a, loaded, sums_a, table, first_b, bias_sum, grad_bias
+        info, stack_a, loaded, sums_a, table, first_b, bias_sum, grad_bias, upper
     )
     back_a = share(part)
     own_in, send_in = finish_first(micro, c_in, pooled, c_lane)(
@@ -1115,25 +1167,20 @@
         info, sums_a, sums_b, sums_c, back_a, back_b, back_c,
         mean_first, variance_first, mean_second, variance_second, mean_third, variance_third,
     )
-
-    def join(half, axis):
-        other = partner(half)
-        low, high = jnp.where(lead, half, other), jnp.where(lead, other, half)
-        return jnp.concatenate([low, high], axis=axis).astype(F32)
 
     return (
         block_output,
         input_grad,
         small[0],
         small[1],
-        join(half_first, 2),
+        jnp.concatenate([sum_lower, sum_upper]).astype(F32),
         small[6],
         small[2],
         small[3],
-        join(half_second, 1),
+        sum_second.astype(F32),
         small[4],
         small[5],
-        join(half_point, 1),
+        sum_point.astype(F32),
         small[7],
         *small[8:],
     )

time: 559 us -> 853 us (1.53)
  waiting for transfers between devices: 101 us -> 410 us
  starting transfers between devices: 74.3 us -> 45.7 us
  Pallas kernels: 336 us -> 346 us
    psum x1 -> x3, waiting for transfers between devices: 53.7 us -> 375 us  [the longest x1 143 us: shards(): sum_lower = lax.psum(lower, BOTH)]
    pallas_call x3 -> x9, Pallas kernels: 155 us -> 182 us  [the longest x1 45.6 us: shards(): forward_first(micro, c_in, c_mid, taps, pooled)(info, act_a, table, first_t)]
    ppermute x50 -> x42, starting transfers between devices: 65.2 us -> 44.8 us  [share(): lax.ppermute(rows, BOTH, [(i, i ^ mask) for i in range(devices)])]
    all_to_all x1 -> x0, waiting for transfers between devices: 9.57 us -> none  [share_at_once(): return jnp.sum(lax.all_to_all(copies, BOTH, 0, 0), axis=0)]
    pallas_call x1, Pallas kernels: 63.2 us -> 54 us  [shards(): backward_first(micro, c_in, c_mid, taps, pooled, c_lane)]
    ppermute x50 -> x42, waiting for transfers between devices: 32 us -> 35.1 us  [share(): lax.ppermute(rows, BOTH, [(i, i ^ mask) for i in range(devices)])]
  transfers between devices with their start and end apart: 60 -> 47, of which waited for: 23 -> 35; matrix products, arithmetic and copies ran while one was open for 2% -> 2% of each run, Pallas kernels for 20% -> 8%
where the time goes in v1:
time: 853 us; the launch traced here: 844 us
  waiting for transfers between devices  410 us (48%)
  Pallas kernels  346 us (41%)
  starting transfers between devices  45.7 us (5%)
  other arithmetic  24.9 us (3%)
  between operations  14.3 us (2%)
    psum x1, waiting for transfers between devices, shards(): sum_lower = lax.psum(lower, BOTH)  143 us
    psum x1, waiting for transfers between devices, shards(): sum_upper = lax.psum(upper, BOTH[::-1])  125 us
    psum x1, waiting for transfers between devices, shards(): sum_second, sum_point = lax.psum((grad_second, grad_point), BOTH)  108 us
    pallas_call x1, Pallas kernels, shards(): backward_first(micro, c_in, c_mid, taps, pooled, c_lane)  54 us
    pallas_call x1, Pallas kernels, shards(): forward_first(micro, c_in, c_mid, taps, pooled)(info, act_a, table, first_t)  45.6 us
    ppermute x42, starting transfers between devices, share(): lax.ppermute(rows, BOTH, [(i, i ^ mask) for i in range(devices)])  44.8 us
    ppermute x42, waiting for transfers between devices, share(): lax.ppermute(rows, BOTH, [(i, i ^ mask) for i in range(devices)])  35.1 us
    pallas_call x1, Pallas kernels, shards(): gradient_first(micro, c_in, c_mid, taps, pooled, c_lane)  28.4 us
  transfers between devices with their start and end apart: 47, of which 35 were waited for; matrix products, arithmetic and copies ran while one was open for 2% of the time, Pallas kernels for 8%

profile of v1, /device:TPU:0, one launch (start us, length us, event | category | flops | bytes accessed | tf_op | source)
XLA Modules:
  0.0 844.0 jit_solution(16365057888483215224)
XLA Ops:
  8.6 16.9 %load_features.1 = (bf16[3,2,656,1024]{3,2,1,0:T(8,128)(2,1)}, f32[8,768]{1,0:T(8,128)}) custom-call(s32[4]{0:T(128)} %pad_add_fusion.refs_0_, bf16[3,652,2,2048]{3,2,1,0:T(2,128)(2,1)} %bitcast.9), custom_call_target="tpu_custom_call" | custom-call | tf_op jit(solution)/shard_map/load_features/pallas_call | solution.py:1110
  25.5 2.4 collective-permute-start.2
  29.7 2.2 collective-permute-done.1
  32.7 2.5 collective-permute-start.5
  39.5 2.7 collective-permute-start.6
  42.2 12.8 %prepare_weights.1 = (bf16[768,3328]{1,0:T(8,128)(2,1)}, bf16[656,3840]{1,0:T(8,128)(2,1)}, bf16[384,2304]{1,0:T(8,128)(2,1)}, bf16[768,1152]{1,0:T(8,128)(2,1)}...) custom-call(s32[4]{0:T(128)} %pad_add_fusion.refs_0_, bf16[5,652,768]{2,1,0:T(8,128)(2,1)} %refs_1_.2, ...), custom_call_target="tpu_custom_call" | custom-call | tf_op jit(solution)/shard_map/prepare_weights/pallas_call | solution.py:1116
  55.6 17.1 %activate.1.refs_1_.refs_2_ = bf16[3,3984,1024]{2,1,0:T(8,128)(2,1)} custom-call(s32[4]{0:T(128)} %pad_add_fusion.refs_0_, bf16[3,2,656,1024]{3,2,1,0:T(8,128)(2,1)} %get-tuple-element.66.refs_1_.refs_2_, f32[8,768]{1,0:T(8,128)} %add.140.refs_2_.refs_3_.refs_5_.refs_1_, f32[8,768]{1,0:T(8,128)} %get-tuple-element.68.refs_3_.refs_2_.refs_4_.refs_5_.refs_7_.refs_8_), custom_call_target="tpu_custom_call" | custom-call | tf_op jit(solution)/shard_map/activate/pallas_call | solution.py:1119
  72.7 45.6 %forward_first.1 = (bf16[3,768,1024]{2,1,0:T(8,128)(2,1)}, f32[3,768,1024]{2,1,0:T(8,128)}, f32[8,768]{1,0:T(8,128)}) custom-call(s32[4]{0:T(128)} %pad_add_fusion.refs_0_, bf16[3,3984,1024]{2,1,0:T(8,128)(2,1)} %activate.1.refs_1_.refs_2_, f32[8,768]{1,0:T(8,128)} %get-tuple-element.68.refs_3_.refs_2_.refs_4_.refs_5_.refs_7_.refs_8_, ...), custom_call_target="tpu_custom_call" | custom-call | tf_op jit(solution)/shard_map/forward_first/pallas_call | solution.py:1120
  120.2 1.6 collective-permute-done.9
  123.3 1.5 collective-permute-start.12
  125.2 1.5 collective-permute-start.10
  129.5 9.1 %turn_cotangent.1 = (bf16[3,768,1024]{2,1,0:T(8,128)(2,1)}, f32[3,384,1024]{2,1,0:T(8,128)}, f32[8,768]{1,0:T(8,128)}) custom-call(s32[4]{0:T(128)} %pad_add_fusion.refs_0_, bf16[3,2,1024,768]{3,2,1,0:T(8,128)(2,1)} %refs_3_.3, bf16[384,768]{1,0:T(8,128)(2,1)} %refs_2_.3), custom_call_target="tpu_custom_call" | custom-call | tf_op jit(solution)/shard_map/turn_cotangent/pallas_call | solution.py:1122
  139.2 19.3 %forward_second.1 = (f32[3,384,1024]{2,1,0:T(8,128)}, bf16[3,768,1024]{2,1,0:T(8,128)(2,1)}, f32[8,384]{1,0:T(8,128)}) custom-call(s32[4]{0:T(128)} %pad_add_fusion.refs_0_, bf16[3,768,1024]{2,1,0:T(8,128)(2,1)} %get-tuple-element.70.refs_1_.refs_2_.refs_8_, f32[8,768]{1,0:T(8,128)} %add.140.refs_2_.refs_3_.refs_5_.refs_1_, ...), custom_call_target="tpu_custom_call" | custom-call | tf_op jit(solution)/shard_map/forward_second/pallas_call | solution.py:1123
  160.4 1.5 collective-permute-done.16
  163.2 2.5 collective-permute-start.19
  167.8 1.6 collective-permute-done.18
  169.9 2.6 collective-permute-start.20
  172.5 2.0 collective-permute-done.20
  175.1 10.4 %norm_third.1 = (bf16[3,384,1024]{2,1,0:T(8,128)(2,1)}, f32[3,384,1024]{2,1,0:T(8,128)}, f32[8,384]{1,0:T(8,128)}) custom-call(s32[4]{0:T(128)} %pad_add_fusion.refs_0_, f32[3,384,1024]{2,1,0:T(8,128)} %get-tuple-element.74.refs_1_.refs_2_, f32[3,384,1024]{2,1,0:T(8,128)} %get-tuple-element.75.refs_2_, f32[8,768]{1,0:T(8,128)} %add.140.refs_2_.refs_3_.refs_5_.refs_1_, ...), custom_call_target="tpu_custom_call" | custom-call | tf_op jit(solution)/shard_map/norm_third/pallas_call | solution.py:1127
  190.3 1.5 collective-permute-start.27
  192.2 1.5 collective-permute-start.25
  195.9 2.6 collective-permute-start.28
  198.5 14.2 %point_output.1 = (bf16[3,1024,384]{2,1,0:T(8,128)(2,1)}, bf16[3,1024,384]{2,1,0:T(8,128)(2,1)}, bf16[384,768]{1,0:T(8,128)(2,1)}) custom-call(s32[4]{0:T(128)} %pad_add_fusion.refs_0_, bf16[3,384,1024]{2,1,0:T(8,128)(2,1)} %get-tuple-element.77.refs_1_, bf16[3,768,1024]{2,1,0:T(8,128)(2,1)} %get-tuple-element.70.refs_1_.refs_2_.refs_8_, ...), custom_call_target="tpu_custom_call" | custom-call | tf_op jit(solution)/shard_map/point_output/pallas_call | solution.py:1131
  213.4 25.7 %backward_second.1 = (f32[3,768,1024]{2,1,0:T(8,128)}, f32[8,768]{1,0:T(8,128)}, bf16[3,1152,1024]{2,1,0:T(8,128)(2,1)}) custom-call(s32[4]{0:T(128)} %pad_add_fusion.refs_0_, f32[3,384,1024]{2,1,0:T(8,128)} %get-tuple-element.81.refs_1_, f32[3,384,1024]{2,1,0:T(8,128)} %get-tuple-element.74.refs_1_.refs_2_, f32[8,768]{1,0:T(8,128)} %add.140.refs_2_.refs_3_.refs_5_.refs_1_, ...), custom_call_target="tpu_custom_call" | custom-call | tf_op jit(solution)/shard_map/backward_second/pallas_call | solution.py:1135
  240.9 1.6 collective-permute-done.31
  243.9 2.5 collective-permute-start.34
  247.4 1.5 collective-permute-done.34
  251.2 11.9 %weights_second.1.refs_9_ = bf16[3,768,384]{2,1,0:T(8,128)(2,1)} custom-call(s32[4]{0:T(128)} %pad_add_fusion.refs_0_, bf16[3,768,1024]{2,1,0:T(8,128)(2,1)} %get-tuple-element.89.refs_1_, bf16[3,1152,1024]{2,1,0:T(8,128)(2,1)} %get-tuple-element.90.refs_2_), custom_call_target="tpu_custom_call" | custom-call | tf_op jit(solution)/shard_map/weights_second/pallas_call | solution.py:1139
  263.7 28.4 %gradient_first.1 = (bf16[3,4608,1024]{2,1,0:T(8,128)(2,1)}, f32[8,768]{1,0:T(8,128)}) custom-call(s32[4]{0:T(128)} %pad_add_fusion.refs_0_, f32[3,768,1024]{2,1,0:T(8,128)} %get-tuple-element.85.refs_1_, bf16[3,768,1024]{2,1,0:T(8,128)(2,1)} %get-tuple-element.70.refs_1_.refs_2_.refs_8_, bf16[3,768,1024]{2,1,0:T(8,128)(2,1)} %get-tuple-element.86.refs_3_, ...), custom_call_target="tpu_custom_call" | custom-call | tf_op jit(solution)/shard_map/gradient_first/pallas_call | solution.py:1141
  292.1 26.1 %weights_first.2.refs_5_ = bf16[3,652,768]{2,1,0:T(8,128)(2,1)} custom-call(s32[4]{0:T(128)} %pad_add_fusion.refs_0_, bf16[3,3984,1024]{2,1,0:T(8,128)(2,1)} %activate.1.refs_1_.refs_2_, bf16[3,3984,1024]{2,1,0:T(8,128)(2,1)} %activate.1.refs_1_.refs_2_, bf16[3,4608,1024]{2,1,0:T(8,128)(2,1)} %get-tuple-element.91.refs_3_.refs_4_.refs_1_, ...), custom_call_target="tpu_custom_call" | custom-call | tf_op jit(solution)/shard_map/weights_first/pallas_call | solution.py:1145
  318.2 19.0 %weights_first.3.refs_8_ = bf16[2,652,768]{2,1,0:T(8,128)(2,1)} custom-call(s32[4]{0:T(128)} %pad_add_fusion.refs_0_, bf16[3,3984,1024]{2,1,0:T(8,128)(2,1)} %activate.1.refs_1_.refs_2_, bf16[3,3984,1024]{2,1,0:T(8,128)(2,1)} %activate.1.refs_1_.refs_2_, bf16[3,4608,1024]{2,1,0:T(8,128)(2,1)} %get-tuple-element.91.refs_3_.refs_4_.refs_1_, ...), custom_call_target="tpu_custom_call" | custom-call | tf_op jit(solution)/shard_map/weights_first/pallas_call | solution.py:1148
  337.2 54.0 %backward_first.1 = (f32[3,2,656,1024]{3,2,1,0:T(8,128)}, f32[8,768]{1,0:T(8,128)}) custom-call(s32[4]{0:T(128)} %pad_add_fusion.refs_0_, bf16[3,4608,1024]{2,1,0:T(8,128)(2,1)} %get-tuple-element.91.refs_3_.refs_4_.refs_1_, bf16[3,2,656,1024]{3,2,1,0:T(8,128)(2,1)} %get-tuple-element.66.refs_1_.refs_2_, f32[8,768]{1,0:T(8,128)} %add.140.refs_2_.refs_3_.refs_5_.refs_1_, ...), custom_call_target="tpu_custom_call" | custom-call | tf_op jit(solution)/shard_map/backward_first/pallas_call | solution.py:1154
  393.1 1.6 collective-permute-done.38
  396.1 1.5 collective-permute-start.41
  398.1 1.5 collective-permute-start.39
  401.9 2.7 collective-permute-start.42
  404.6 2.1 collective-permute-done.42
  407.3 20.1 %finish_first.1 = (bf16[3,326,2048]{2,1,0:T(8,128)(2,1)}, bf16[3,326,2048]{2,1,0:T(8,128)(2,1)}) custom-call(s32[4]{0:T(128)} %pad_add_fusion.refs_0_, f32[3,2,656,1024]{3,2,1,0:T(8,128)} %get-tuple-element.94.refs_1_, bf16[3,2,656,1024]{3,2,1,0:T(8,128)(2,1)} %get-tuple-element.66.refs_1_.refs_2_, f32[8,768]{1,0:T(8,128)} %add.140.refs_2_.refs_3_.refs_5_.refs_1_, ...), custom_call_target="tpu_custom_call" | custom-call | tf_op jit(solution)/shard_map/finish_first/pallas_call | solution.py:1158
  428.3 107.9 %all-reduce.9.cloned.1.call-done = (bf16[3,768,384]{2,1,0:T(8,128)(2,1)}, bf16[384,768]{1,0:T(8,128)(2,1)}) async-done(((bf16[3,768,384]{2,1,0:T(8,128)(2,1)}, bf16[384,768]{1,0:T(8,128)(2,1)}), (bf16[3,768,384]{2,1,0:T(8,128)(2,1)}, bf16[384,768]{1,0:T(8,128)(2,1)})) %all-reduce.9.cloned.1.call-update) | async-done | bytes 2359312 | tf_op jit(solution)/shard_map/psum | solution.py:1140
  536.3 2.4 small_outputs.1
  538.7 2.2 convert_element_type.11
  540.8 3.5 convert_element_type.10
  544.3 2.1 select_bitcast_fusion.1
  547.0 2.7 copy.39
  549.7 124.7 %all-reduce.7.cloned.1.call-done = bf16[2,652,768]{2,1,0:T(8,128)(2,1)} async-done(((bf16[2,652,768]{2,1,0:T(8,128)(2,1)}), bf16[2,652,768]{2,1,0:T(8,128)(2,1)}) %all-reduce.7.cloned.1.call-update) | async-done | bytes 2002960 | tf_op jit(solution)/shard_map/psum | solution.py:1153
  674.3 142.6 %all-reduce.5.cloned.1.call-done = bf16[3,652,768]{2,1,0:T(8,128)(2,1)} async-done(((bf16[3,652,768]{2,1,0:T(8,128)(2,1)}), bf16[3,652,768]{2,1,0:T(8,128)(2,1)}) %all-reduce.5.cloned.1.call-update) | async-done | bytes 3004432 | tf_op jit(solution)/shard_map/psum | solution.py:1152
  816.9 7.1 maximum_convert_fusion
  824.0 13.1 %pair_windows.1 = bf16[3,326,2,2048]{3,2,1,0:T(2,128)(2,1)} custom-call(s32[4]{0:T(128)} %pad_add_fusion.refs_0_, bf16[3,326,2048]{2,1,0:T(8,128)(2,1)} %get-tuple-element.96.refs_1_, bf16[3,326,2048]{2,1,0:T(8,128)(2,1)} %collective-permute-done.43.refs_2_), custom_call_target="tpu_custom_call" | custom-call | tf_op jit(solution)/shard_map/pair_windows/pallas_call | solution.py:1161
  (94 shorter events, 45.5 us)
Async XLA Ops:
  25.5 4.2 collective-permute-start.2
  27.9 4.0 collective-permute-start.1
  28.5 3.4 collective-permute-start
  32.7 4.9 collective-permute-start.5
  35.2 3.8 collective-permute-start.4
  35.7 3.8 collective-permute-start.3
  39.5 15.5 %collective-permute-start.6 = (f32[8,768]{1,0:T(8,128)S(1)}, f32[8,768]{1,0:T(8,128)S(1)}, u32[]{:S(2)}, u32[]{:S(2)}) collective-permute-start(f32[8,768]{1,0:T(8,128)S(1)} %add_add_fusion.6), channel_id=1, source_target_pairs={{0,8},{1,9},{2,10},{3,11},{4,12},{5,13},{6,14},{7,15},{8,0},{9,1},... | collective-permute-start | bytes 73736 | tf_op jit(solution)/shard_map/ppermute | solution.py:1068
  118.2 3.5 collective-permute-start.9
  118.3 4.2 collective-permute-start.8
  119.1 3.4 collective-permute-start.7
  123.3 4.7 collective-permute-start.12
  124.8 3.8 collective-permute-start.11
  125.2 3.8 collective-permute-start.10
  129.1 9.5 %collective-permute-start.13 = (f32[8,768]{1,0:T(8,128)S(1)}, f32[8,768]{1,0:T(8,128)S(1)}, u32[]{:S(2)}, u32[]{:S(2)}) collective-permute-start(f32[8,768]{1,0:T(8,128)S(1)} %add_add_fusion.4), channel_id=1, source_target_pairs={{0,8},{1,9},{2,10},{3,11},{4,12},{5,13},{6,14},{7,15},{8,0},{9,1},... | collective-permute-start | bytes 73736 | tf_op jit(solution)/shard_map/ppermute | solution.py:1068
  158.5 3.3 collective-permute-start.16
  158.5 4.0 collective-permute-start.15
  159.2 3.2 collective-permute-start.14
  163.2 4.6 collective-permute-start.19
  165.7 3.7 collective-permute-start.18
  166.2 3.7 collective-permute-start.17
  169.9 4.6 collective-permute-start.20
  185.5 3.4 collective-permute-start.24
  185.6 4.0 collective-permute-start.23
  186.3 3.2 collective-permute-start.22
  190.3 4.6 collective-permute-start.27
  191.8 3.7 collective-permute-start.26
  192.2 3.7 collective-permute-start.25
  195.9 16.8 %collective-permute-start.28 = (f32[8,384]{1,0:T(8,128)S(1)}, f32[8,384]{1,0:T(8,128)S(1)}, u32[]{:S(2)}, u32[]{:S(2)}) collective-permute-start(f32[8,384]{1,0:T(8,128)S(1)} %add_add_fusion.8), channel_id=1, source_target_pairs={{0,8},{1,9},{2,10},{3,11},{4,12},{5,13},{6,14},{7,15},{8,0},{9,1},... | collective-permute-start | bytes 36872 | tf_op jit(solution)/shard_map/ppermute | solution.py:1068
  239.0 3.5 collective-permute-start.31
  239.1 4.1 collective-permute-start.30
  239.8 3.4 collective-permute-start.29
  243.9 5.0 collective-permute-start.34
  246.5 3.8 collective-permute-start.33
  246.9 3.8 collective-permute-start.32
  250.8 12.3 %collective-permute-start.35 = (f32[8,768]{1,0:T(8,128)S(1)}, f32[8,768]{1,0:T(8,128)S(1)}, u32[]{:S(2)}, u32[]{:S(2)}) collective-permute-start(f32[8,768]{1,0:T(8,128)S(1)} %add_add_fusion.2), channel_id=1, source_target_pairs={{0,8},{1,9},{2,10},{3,11},{4,12},{5,13},{6,14},{7,15},{8,0},{9,1},... | collective-permute-start | bytes 73736 | tf_op jit(solution)/shard_map/ppermute | solution.py:1068
  292.0 244.2 %all-reduce.9.cloned.1.call-start = ((), (), s32[]{:S(2)}) async-start(), calls=%async_computation.2 | async-start | bytes 4718592 | tf_op jit(solution)/shard_map/psum | solution.py:1140
  391.2 3.5 collective-permute-start.38
  391.2 4.1 collective-permute-start.37
  392.0 3.4 collective-permute-start.36
  396.1 4.8 collective-permute-start.41
  397.6 3.8 collective-permute-start.40
  398.1 3.8 collective-permute-start.39
  399.6 274.7 %all-reduce.7.cloned.1.call-start = ((), (), s32[]{:S(2)}) async-start(), calls=%async_computation.1 | async-start | bytes 4030464 | tf_op jit(solution)/shard_map/psum | solution.py:1153
  401.9 4.8 collective-permute-start.42
  427.5 396.5 %collective-permute-start.43 = (bf16[3,326,2048]{2,1,0:T(8,128)(2,1)}, bf16[3,326,2048]{2,1,0:T(8,128)(2,1)}, u32[]{:S(2)}, u32[]{:S(2)}) collective-permute-start(bf16[3,326,2048]{2,1,0:T(8,128)(2,1)} %get-tuple-element.97), channel_id=1, source_target_pairs={{0,16},{16,0},{1,17},{17,1},{2,18},{18,2},{3,19},{19,3},{4,20},{20... | collective-permute-start | bytes 12017672 | tf_op jit(solution)/shard_map/ppermute | solution.py:1052
  427.5 116.9 %collective-permute-start.21 = (bf16[3,1024,384]{2,1,0:T(8,128)(2,1)}, bf16[3,1024,384]{2,1,0:T(8,128)(2,1)}, u32[]{:S(2)}, u32[]{:S(2)}) collective-permute-start(bf16[3,1024,384]{2,1,0:T(8,128)(2,1)} %get-tuple-element.80), channel_id=1, source_target_pairs={{0,16},{16,0},{1,17},{17,1},{2,18},{18,2},{3,19},{19,3},{4,20},{20... | collective-permute-start | bytes 7077896 | tf_op jit(solution)/shard_map/ppermute | solution.py:1052
  428.0 388.9 %all-reduce.5.cloned.1.call-start = ((), (), s32[]{:S(2)}) async-start(), calls=%async_computation | async-start | bytes 6045696 | tf_op jit(solution)/shard_map/psum | solution.py:1152
  536.2 8.1 copy-start
Sparse Core Ops, SparseCore 0:
  399.7 136.4 all-reduce.8
  542.5 131.8 all-reduce.6
  680.4 136.4 all-reduce.4

commit v2 on v1

--- a/solution.py
+++ b/solution.py
@@ -15,6 +15,7 @@
 F32 = jnp.float32
 LANES = 128
 TILE = 256
+STEP = 512
 BOTH = ("section", "dp")
 
 
@@ -134,6 +135,7 @@
 
 
 def call(name, body, grid, in_specs, out_specs, out_shape, scratch=(), limit=58, after=0):
+
     real = len(in_specs) + 1
 
     def ordered(*refs):
@@ -187,58 +189,24 @@
     return outer, outer * inverse * (total[1:2] / count), outer * (total[0:1] / count)
 
 
-def prepare_weights(conv_first, conv_second, conv_point, vectors, c_lane):
-    taps, c_in, c_mid = conv_first.shape
-    taps_b, _, c_res = conv_second.shape
-    c_pad = up(c_in, 16)
-    depth = up(taps * c_pad, TILE)
-    room = up(c_pad + (taps - 1) * (c_pad % LANES), LANES)
-    base = c_pad - c_pad % LANES
+def prepare_table(vectors, c_lane):
     many = len(vectors)
 
-    def body(info, first, second, point, *rest):
-        vector_refs = rest[:many]
-        first_out, back_out, second_out, second_back, point_out, table, wide_sum = rest[many:]
-        for index, ref in enumerate(vector_refs):
+    def body(info, *refs):
+        table = refs[many]
+        for index, ref in enumerate(refs[:many]):
             value = ref[...]
             if value.shape[0] < c_lane:
                 value = jnp.pad(value, (0, c_lane - value.shape[0]))
             table[index : index + 1, :] = value.reshape(1, c_lane)
-        eye = identity()
-        for row in range(0, c_mid, TILE):
-            wide_sum[...] = jnp.zeros_like(wide_sum)
-            for tap in range(taps):
-                turned = nt(eye, first[tap, :, row : row + TILE])
-                padded = jnp.concatenate([turned, jnp.zeros((TILE, room - c_in), F32)], axis=1)
-                moved = pltpu.roll(padded, tap * (c_pad % LANES), 1) if tap else padded
-                wide_sum[:, tap * base : tap * base + room] += moved
-            first_out[row : row + TILE, :] = wide_sum[:, :depth].astype(BF16)
-        for tap in range(taps):
-            back_out[:c_in, tap * c_mid : (tap + 1) * c_mid] = first[tap]
-        back_out[c_in:, :] = jnp.zeros((c_pad - c_in, taps * c_mid), BF16)
-        eye_res = choose(iota((c_res, c_res), 0) == iota((c_res, c_res), 1)).astype(BF16)
-        for tap in range(taps_b):
-            second_out[:, tap * c_mid : (tap + 1) * c_mid] = nt(eye_res, second[tap]).astype(BF16)
-            second_back[:, tap * c_res : (tap + 1) * c_res] = second[tap]
-        eye_mid = choose(iota((c_mid, c_mid), 0) == iota((c_mid, c_mid), 1)).astype(BF16)
-        point_out[...] = nt(eye_mid, point[...]).astype(BF16)
-
-    outs = [
-        ((c_mid, depth), BF16),
-        ((c_pad, taps * c_mid), BF16),
-        ((c_res, taps_b * c_mid), BF16),
-        ((c_mid, taps_b * c_res), BF16),
-        ((c_mid, c_res), BF16),
-        ((up(many, 8), c_lane), F32),
-    ]
-    return call(
-        "prepare_weights",
+
+    return call(
+        "prepare_table",
         body,
         (1,),
-        [whole(a.shape) for a in (conv_first, conv_second, conv_point, *vectors)],
-        [whole(s) for s, _ in outs],
-        [shape_of(s, t) for s, t in outs],
-        [pltpu.VMEM((TILE, max(depth, (taps - 1) * base + room)), F32)],
+        [whole(a.shape) for a in vectors],
+        whole((up(many, 8), c_lane)),
+        shape_of((up(many, 8), c_lane)),
     )
 
 
@@ -365,20 +333,32 @@
     c_pad = up(c_in, 16)
     c_lane = up(c_in, LANES)
     depth = up(taps * c_pad, TILE)
-    steps = pooled // TILE
+    steps = pooled // STEP
     total = micro * steps
     stack_rows = c_pad + depth
-
-    def body(info, stack, table, weight, hid, diff, st_ref, bias, s_acc, q_acc, even, odd):
+    room = up(c_pad + (taps - 1) * (c_pad % LANES), LANES)
+    base = c_pad - c_pad % LANES
+
+    def body(info, stack, table, weight, hid, diff, st_ref,
+             bias, s_acc, q_acc, even, odd, held, line):
         step = pl.program_id(0)
         late = jnp.maximum(step - 1, 0)
         k, at = late // steps, late % steps
-        mask = pool_mask(info[1 + k], TILE, at * TILE)
+        mask = pool_mask(info[1 + k], STEP, at * STEP)
 
         @pl.when(step == 0)
         def _():
             bias[...] = column(table[2:3, :c_mid])
             st_ref[...] = jnp.zeros_like(st_ref)
+            eye = identity()
+            for row in range(0, c_mid, TILE):
+                line[...] = jnp.zeros_like(line)
+                for tap in range(taps):
+                    turned = nt(eye, weight[tap, :, row : row + TILE])
+                    padded = jnp.concatenate([turned, jnp.zeros((TILE, room - c_in), F32)], axis=1)
+                    moved = pltpu.roll(padded, tap * (c_pad % LANES), 1) if tap else padded
+                    line[:, tap * base : tap * base + room] += moved
+                held[row : row + TILE, :] = line[:, :depth].astype(BF16)
 
         @pl.when(at == 0)
         def _():
@@ -388,7 +368,7 @@
         def finish():
             for start in range(0, c_mid, 16):
                 rows = slice(start, start + 16)
-                b = wide(bias[rows, :], TILE)
+                b = wide(bias[rows, :], STEP)
                 left, right = even[rows, :] + b, odd[rows, :] + b
                 apart = left - right
                 joined = jnp.maximum(left, right) + jnp.log1p(jnp.exp(-jnp.abs(apart)))
@@ -402,8 +382,8 @@
         @pl.when(step < total)
         def _():
             finish()
-            even[...] = nn(weight[...], stack[0, :depth, :])
-            odd[...] = nn(weight[...], stack[0, c_pad : c_pad + depth, :])
+            even[...] = nn(held[...], stack[0, :depth, :])
+            odd[...] = nn(held[...], stack[0, c_pad : c_pad + depth, :])
 
         @pl.when(step == total)
         def _():
@@ -418,13 +398,13 @@
         body,
         (total + 1,),
         [
-            lane_blocks((stack_rows, TILE), steps, total - 1, False),
+            lane_blocks((stack_rows, STEP), steps, total - 1, False),
             whole((8, c_lane)),
-            whole((c_mid, depth), 1),
-        ],
-        [
-            lane_blocks((c_mid, TILE), steps, total - 1, True),
-            lane_blocks((c_mid, TILE), steps, total - 1, True),
+            whole((taps, c_in, c_mid), 1),
+        ],
+        [
+            lane_blocks((c_mid, STEP), steps, total - 1, True),
+            lane_blocks((c_mid, STEP), steps, total - 1, True),
             whole((8, c_mid)),
         ],
         [
@@ -432,13 +412,18 @@
             shape_of((micro, c_mid, pooled)),
             shape_of((8, c_mid)),
         ],
-        [pltpu.VMEM((c_mid, LANES), F32)] * 3 + [pltpu.VMEM((c_mid, TILE), F32)] * 2,
+        [pltpu.VMEM((c_mid, LANES), F32)] * 3
+        + [pltpu.VMEM((c_mid, STEP), F32)] * 2
+        + [
+            pltpu.VMEM((c_mid, depth), BF16),
+            pltpu.VMEM((TILE, max(depth, (taps - 1) * base + room)), F32),
+        ],
     )
 
 
 def forward_second(micro, c_in, c_mid, c_res, taps, pooled, c_lane):
     def body(info, hid, sums_a, sums, table, weight, conv, act, st_ref,
-             stack, col_c, col_s, col_h, s_acc, q_acc):
+             stack, col_c, col_s, col_h, s_acc, q_acc, held):
         k = pl.program_id(0)
         length = info[1 + k]
         _, _, count = first_rows(sums_a, k, c_in)
@@ -450,6 +435,9 @@
         def _():
             col_h[...] = column(table[4:5, :c_mid])
             st_ref[...] = jnp.zeros_like(st_ref)
+            eye = choose(iota((c_res, c_res), 0) == iota((c_res, c_res), 1)).astype(BF16)
+            for tap in range(taps):
+                held[:, tap * c_mid : (tap + 1) * c_mid] = nt(eye, weight[tap]).astype(BF16)
 
         mask = pool_mask(length, pooled)
 
@@ -468,8 +456,7 @@
             stack[here(2), :] = after(a)
 
         each_rows(c_mid, rows_body, 8)
-        for at in range(0, pooled, TILE):
-            conv[0, :, at : at + TILE] = nn(weight[...], stack[:, at : at + TILE])
+        conv[0] = nn(held[...], stack[...])
 
         def moments_body(rows, start):
             value = conv[0, rows, :] * mask
@@ -488,7 +475,7 @@
             whole((8, c_lane)),
             whole((8, c_mid)),
             whole((8, c_lane)),
-            whole((c_res, taps * c_mid), 1),
+            whole((taps, c_mid, c_res), 1),
         ],
         [per_batch((c_res, pooled)), per_batch((c_mid, pooled)), whole((8, c_res))],
         [
@@ -498,7 +485,8 @@
         ],
         [pltpu.VMEM((taps * c_mid, pooled), BF16)]
         + [pltpu.VMEM((c_mid, LANES), F32)] * 3
-        + [pltpu.VMEM((c_res, LANES), F32)] * 2,
+        + [pltpu.VMEM((c_res, LANES), F32)] * 2
+        + [pltpu.VMEM((c_res, taps * c_mid), BF16)],
         after=1,
     )
 
@@ -591,8 +579,7 @@
 def point_output(micro, c_mid, c_res, pooled, c_lane):
     half = c_mid // 2
 
-    def body(info, act, hid, cot, table, point_t, own, send, grad_point,
-             branch, flat, bias, product):
+    def body(info, act, hid, table, point, own, send, branch, flat, bias, held):
         k = pl.program_id(0)
         first = info[0] == 0
         mask = pool_mask(info[1 + k], pooled)
@@ -600,11 +587,10 @@
         @pl.when(k == 0)
         def _():
             bias[...] = column(table[7:8, :c_mid])
-
-        branch[...] = nn(point_t[...], act[0])
-        total = nn(act[0], cot[0, 0]) + jnp.where(k == 0, 0.0, product[...])
-        product[...] = total
-        grad_point[...] = total.astype(BF16)
+            eye = choose(iota((c_mid, c_mid), 0) == iota((c_mid, c_mid), 1)).astype(BF16)
+            held[...] = nt(eye, point[...]).astype(BF16)
+
+        branch[...] = nn(held[...], act[0])
 
         def out_body(rows, start):
             b = wide(bias[rows, :], pooled)
@@ -626,21 +612,19 @@
         [
             per_batch((c_res, pooled)),
             per_batch((c_mid, pooled)),
-            pl.BlockSpec((1, 1, pooled, c_mid), lambda k, info: (k, info[0], 0, 0)),
             whole((8, c_lane)),
-            whole((c_mid, c_res), 1),
-        ],
-        [per_batch((pooled, half)), per_batch((pooled, half)), whole((c_res, c_mid))],
+            whole((c_res, c_mid), 1),
+        ],
+        [per_batch((pooled, half)), per_batch((pooled, half))],
         [
             shape_of((micro, pooled, half), BF16),
             shape_of((micro, pooled, half), BF16),
-            shape_of((c_res, c_mid), BF16),
         ],
         [
             pltpu.VMEM((c_mid, pooled), F32),
             pltpu.VMEM((c_mid, pooled), BF16),
             pltpu.VMEM((c_mid, LANES), F32),
-            pltpu.VMEM((c_res, c_mid), F32),
+            pltpu.VMEM((c_mid, c_res), BF16),
         ],
     )
 
@@ -648,7 +632,7 @@
 def backward_second(micro, c_in, c_mid, c_res, taps, pooled, c_lane):
     def body(info, d_in, conv, sums_a, sums_b, sums_c, back, table, hid, weight,
              d_out, st_ref, stack,
-             up_grad, col_a, col_b, col_0, col_r, col_c, col_s, col_h, s_acc, q_acc):
+             up_grad, col_a, col_b, col_0, col_r, col_c, col_s, col_h, s_acc, q_acc, held, kept):
         k = pl.program_id(0)
         length = info[1 + k]
         _, _, count = first_rows(sums_a, k, c_in)
@@ -666,6 +650,8 @@
         def _():
             col_h[...] = column(table[4:5, :c_mid])
             st_ref[...] = jnp.zeros_like(st_ref)
+            for tap in range(taps):
+                held[:, tap * c_res : (tap + 1) * c_res] = weight[tap]
 
         mask = pool_mask(length, pooled)
 
@@ -674,13 +660,12 @@
             g = (a * d_in[0, rows, :] - b * (conv[0, rows, :] - c) - z) * mask
             g = g.astype(BF16)
             here = lambda seg: pl.ds(aligned(seg * c_res + start), 16)
-            stack[0, here(0), :] = after(g)
-            stack[0, here(1), :] = g
-            stack[0, here(2), :] = before(g)
+            for order, value in enumerate((after(g), g, before(g))):
+                stack[0, here(order), :] = value
+                kept[here(order), :] = value
 
         each_rows(c_res, rows_body, 8)
-        for at in range(0, pooled, TILE):
-            up_grad[:, at : at + TILE] = nn(weight[...], stack[0, :, at : at + TILE])
+        up_grad[...] = nn(held[...], kept[...])
 
         def slope_body(rows, start):
             c, s, h = (wide(r[rows, :], TILE) for r in (col_c, col_s, col_h))
@@ -708,7 +693,7 @@
         whole((8, c_res)),
         whole((8, c_lane)),
         per_batch((c_mid, pooled)),
-        whole((c_mid, taps * c_res), 1),
+        whole((taps, c_mid, c_res), 1),
     ]
     return call(
         "backward_second",
@@ -723,34 +708,48 @@
         ],
         [pltpu.VMEM((c_mid, pooled), F32)]
         + [pltpu.VMEM((c_res, LANES), F32)] * 4
-        + [pltpu.VMEM((c_mid, LANES), F32)] * 5,
-        after=1,
+        + [pltpu.VMEM((c_mid, LANES), F32)] * 5
+        + [pltpu.VMEM((c_mid, taps * c_res), BF16), pltpu.VMEM((taps * c_res, pooled), BF16)],
     )
 
 
 def weights_second(micro, c_mid, c_res, taps, pooled):
-    def body(info, act, stack, grad_conv, product):
+    rows = taps * c_res
+
+    def body(info, act, stack, go, act_c, grad_conv, grad_point, product, product_point):
         k = pl.program_id(0)
-        for tap in range(taps):
-            value = nt(act[0], stack[0, tap * c_res : (tap + 1) * c_res, :])
-            value += jnp.where(k == 0, 0.0, product[tap])
-            product[tap] = value
-            grad_conv[tap] = value.astype(BF16)
+        product[...] = nt(stack[0], act[0]) + jnp.where(k == 0, 0.0, product[...])
+        product_point[...] = nt(act_c[0], go[0]) + jnp.where(k == 0, 0.0, product_point[...])
+
+        @pl.when(k == micro - 1)
+        def _():
+            grad_point[...] = product_point[...].astype(BF16)
+            eye = identity()
+            for tap in range(taps):
+                block = product[tap * c_res : (tap + 1) * c_res, :].astype(BF16)
+                for row in range(0, c_mid, TILE):
+                    turned = nt(eye, block[:, row : row + TILE])
+                    grad_conv[tap, row : row + TILE, :] = turned.astype(BF16)
 
     return call(
         "weights_second",
         body,
         (micro,),
-        [per_batch((c_mid, pooled)), per_batch((taps * c_res, pooled))],
-        whole((taps, c_mid, c_res)),
-        shape_of((taps, c_mid, c_res), BF16),
-        [pltpu.VMEM((taps, c_mid, c_res), F32)],
+        [
+            per_batch((c_mid, pooled)),
+            per_batch((rows, pooled)),
+            per_batch((c_mid, pooled)),
+            per_batch((c_res, pooled)),
+        ],
+        [whole((taps, c_mid, c_res)), whole((c_res, c_mid))],
+        [shape_of((taps, c_mid, c_res), BF16), shape_of((c_res, c_mid), BF16)],
+        [pltpu.VMEM((rows, c_mid), F32), pltpu.VMEM((c_res, c_mid), F32)],
     )
 
 
 def gradient_first(micro, c_in, c_mid, taps, pooled, c_lane):
     def body(info, d_in, hid, go, diff, sums_a, sums_b, back, table,
-             stack, bias_out, col_a, col_b, col_0, col_c, s_acc):
+             g_out, bias_out, col_a, col_b, col_0, col_c, s_acc):
         k = pl.program_id(0)
         length = info[1 + k]
         _, _, count = first_rows(sums_a, k, c_in)
@@ -781,18 +780,12 @@
                 rights.append(right)
                 totals.append(fold(left.astype(F32) + right.astype(F32)))
             s_acc[rows, :] = sum(totals)
-            here = lambda seg: pl.ds(aligned(seg * c_mid + start), 16)
             for side, parts in enumerate((lefts, rights)):
-                joined = jnp.concatenate(parts, axis=1)
-                order = 3 - side
-                stack[0, here(order - 2), :] = after(joined)
-                stack[0, here(order), :] = joined
-                stack[0, here(order + 2), :] = before(joined)
+                g_out[0, side, rows, :] = jnp.concatenate(parts, axis=1)
 
         each_rows(c_mid, rows_body, 6)
         bias_out[...] = as_row(s_acc[...]) + jnp.where(k == 0, 0.0, bias_out[...])
 
-    rows = (taps + 1) * c_mid
     in_specs = [
         per_batch((c_mid, pooled)),
         per_batch((c_mid, pooled)),
@@ -808,63 +801,73 @@
         body,
         (micro,),
         in_specs,
-        [per_batch((rows, pooled)), whole((8, c_mid))],
-        [shape_of((micro, rows, pooled), BF16), shape_of((8, c_mid))],
+        [per_batch((2, c_mid, pooled)), whole((8, c_mid))],
+        [shape_of((micro, 2, c_mid, pooled), BF16), shape_of((8, c_mid))],
         [pltpu.VMEM((c_mid, LANES), F32)] * 5,
         after=1,
     )
 
 
-def weights_first(micro, c_in, c_mid, pooled, tap_from, tap_to):
+def weights_first(micro, c_in, c_mid, taps, pooled):
     c_pad = up(c_in, 16)
-    count = tap_to - tap_from
-
-    def body(info, act_left, act_right, left, right, grad_conv, product):
+
+    def body(info, act_left, act_right, left, right, grad_conv, product, held_left, held_right):
         k, at = pl.program_id(0), pl.program_id(1)
-        value = nt(act_left[0], left[0]) + nt(act_right[0], right[0])
-        value += jnp.where(k == 0, 0.0, product[at])
-        product[at] = value
-        grad_conv[0] = value[:c_in].astype(BF16)
+
+        @pl.when(at == 0)
+        def _():
+            held_left[...] = left[0, 0]
+            held_right[...] = right[0, 0]
+
+        value = nt(act_left[0], held_left[...]) + nt(act_right[0], held_right[...])
+        product[at] = value + jnp.where(k == 0, 0.0, product[at])
+
+        @pl.when(k == micro - 1)
+        def _():
+            grad_conv[0] = product[at, :c_in, :].astype(BF16)
 
     def act_block(shift):
-        return pl.BlockSpec((1, c_pad, pooled), lambda k, j, _: (k, j + tap_from + shift, 0))
-
-    def grad_block(segment):
-        return pl.BlockSpec((1, c_mid, pooled), lambda k, j, _: (k, segment, 0))
+        return pl.BlockSpec((1, c_pad, pooled), lambda k, j, _: (k, j + shift, 0))
+
+    def grad_block(side):
+        return pl.BlockSpec((1, 1, c_mid, pooled), lambda k, j, _: (k, side, 0, 0))
 
     return call(
         "weights_first",
         body,
-        (micro, count),
-        [act_block(0), act_block(1), grad_block(3), grad_block(2)],
+        (micro, taps),
+        [act_block(0), act_block(1), grad_block(0), grad_block(1)],
         pl.BlockSpec(
             (1, c_in, c_mid), lambda k, j, _: (jnp.where(k == micro - 1, j, 0), 0, 0)
         ),
-        shape_of((count, c_in, c_mid), BF16),
-        [pltpu.VMEM((count, c_pad, c_mid), F32)],
+        shape_of((taps, c_in, c_mid), BF16),
+        [pltpu.VMEM((taps, c_pad, c_mid), F32)] + [pltpu.VMEM((c_mid, pooled), BF16)] * 2,
         after=1,
     )
 
 
 def backward_first(micro, c_in, c_mid, taps, pooled, c_lane):
     c_pad = up(c_in, 16)
-    steps = pooled // TILE
+    steps = pooled // STEP
     total = micro * steps
     depth = taps * c_mid
 
-    def body(info, stack, x_ref, sums_a, table, weight, bias_first, bias_point, d_out, st_ref,
-             even, odd, col_c, col_s, col_h, s_acc, q_acc):
+    def body(info, g_in, x_ref, sums_a, table, weight, bias_first, bias_point, d_out, st_ref,
+             even, odd, col_c, col_s, col_h, s_acc, q_acc, held, stack):
         step = pl.program_id(0)
         late = jnp.maximum(step - 1, 0)
         k, at = late // steps, late % steps
         length = info[1 + k]
         (centre, _, inverse), _, _ = first_rows(sums_a, k, c_in)
-        masks = pool_mask(length, TILE, at * TILE), odd_mask(length, TILE, at * TILE)
+        masks = pool_mask(length, STEP, at * STEP), odd_mask(length, STEP, at * STEP)
 
         @pl.when(step == 0)
         def _():
             col_h[...] = column(table[1:2, :])
             st_ref[...] = jnp.zeros_like(st_ref)
+            held[c_in:, :] = jnp.zeros((c_pad - c_in, depth), BF16)
+            for tap in range(taps):
+                held[:c_in, tap * c_mid : (tap + 1) * c_mid] = weight[tap]
             st_ref[2 * micro : 2 * micro + 1, :] = bias_first[0:1, :]
             st_ref[2 * micro + 1 : 2 * micro + 2, :] = bias_point[0:1, :]
 
@@ -875,10 +878,25 @@
             s_acc[...] = jnp.zeros_like(s_acc)
             q_acc[...] = jnp.zeros_like(q_acc)
 
+        @pl.when((step % steps == 0) & (step < total))
+        def _():
+            def rows_body(rows, start):
+                here = lambda seg: pl.ds(aligned(seg * c_mid + start), 16)
+                for side in range(2):
+                    value = g_in[0, side, rows, :]
+                    order = 3 - side
+                    stack[here(order - 2), :] = after(value)
+                    stack[here(order), :] = value
+                    stack[here(order + 2), :] = before(value)
+
+            each_rows(c_mid, rows_body, 8)
+
+        lanes = pl.ds(pl.multiple_of((step % steps) * STEP, STEP), STEP)
+
         def finish():
             for start in range(0, c_pad, 16):
                 rows = slice(start, start + 16)
-                c, s, h = (wide(r[rows, :], TILE) for r in (col_c, col_s, col_h))
+                c, s, h = (wide(r[rows, :], STEP) for r in (col_c, col_s, col_h))
                 for half, upstream in enumerate((even, odd)):
                     apart = x_ref[0, half, rows, :].astype(F32) - c
                     _, slope = gelu_slope(apart * s + h)
@@ -890,8 +908,8 @@
         @pl.when(step < total)
         def _():
             finish()
-            even[...] = nn(weight[...], stack[0, c_mid : c_mid + depth, :])
-            odd[...] = nn(weight[...], stack[0, :depth, :])
+            even[...] = nn(held[...], stack[c_mid : c_mid + depth, lanes])
+            odd[...] = nn(held[...], stack[:depth, lanes])
 
         @pl.when(step == total)
         def _():
@@ -906,18 +924,22 @@
         body,
         (total + 1,),
         [
-            lane_blocks((depth + c_mid, TILE), steps, total - 1, False),
-            lane_blocks((2, c_pad, TILE), steps, total - 1, True),
+            pl.BlockSpec(
+                (1, 2, c_mid, pooled),
+                lambda s, _: (jnp.minimum(s, total - 1) // steps, 0, 0, 0),
+            ),
+            lane_blocks((2, c_pad, STEP), steps, total - 1, True),
             whole((8, c_lane)),
             whole((8, c_lane)),
-            whole((c_pad, taps * c_mid), 1),
+            whole((taps, c_in, c_mid), 1),
             whole((8, c_mid)),
             whole((8, c_mid)),
         ],
-        [lane_blocks((2, c_pad, TILE), steps, total - 1, True), whole((8, c_lane))],
+        [lane_blocks((2, c_pad, STEP), steps, total - 1, True), whole((8, c_lane))],
         [shape_of((micro, 2, c_pad, pooled)), shape_of((8, c_lane))],
-        [pltpu.VMEM((c_pad, TILE), F32)] * 2 + [pltpu.VMEM((c_lane, LANES), F32)] * 5,
-        after=1,
+        [pltpu.VMEM((c_pad, STEP), F32)] * 2
+        + [pltpu.VMEM((c_lane, LANES), F32)] * 5
+        + [pltpu.VMEM((c_pad, depth), BF16), pltpu.VMEM((depth + c_mid, pooled), BF16)],
     )
 
 
@@ -1113,74 +1135,79 @@
         gain_first, shift_first, bias_first, gain_second, shift_second, gain_third, shift_third,
         bias_point,
     )
-    first_t, first_b, second_t, second_b, point_t, table = prepare_weights(
-        conv_first, conv_second, conv_point, vectors, c_lane
-    )(info, conv_first, conv_second, conv_point, *vectors)
+    table = prepare_table(vectors, c_lane)(info, *vectors)
     act_a = activate(micro, c_in, taps, pooled)(info, loaded, sums_a, table)
-    hid, diff, part = forward_first(micro, c_in, c_mid, taps, pooled)(info, act_a, table, first_t)
+    hid, diff, part = forward_first(micro, c_in, c_mid, taps, pooled)(info, act_a, table, conv_first)
     sums_b = share(part)
     go, up_c, grad_bias = turn_cotangent(micro, c_mid, c_res, pooled)(info, cotangent, conv_point)
     conv_b, act_b, part = forward_second(micro, c_in, c_mid, c_res, taps_b, pooled, c_lane)(
-        info, hid, sums_a, sums_b, table, second_t, grad_bias
+        info, hid, sums_a, sums_b, table, conv_second, grad_bias
     )
     sums_c = share(part)
     act_c, d_c, part = norm_third(micro, c_in, c_res, pooled, c_lane)(
         info, conv_b, up_c, sums_a, sums_c, table
     )
     back_c = share(part)
-    own_out, send_out, grad_point = point_output(micro, c_mid, c_res, pooled, c_lane)(
-        info, act_c, hid, cotangent, table, point_t
-    )
-    got_out = partner(send_out)
     d_b, part, stack_b = backward_second(micro, c_in, c_mid, c_res, taps_b, pooled, c_lane)(
-        info, d_c, conv_b, sums_a, sums_b, sums_c, back_c, table, hid, second_b, grad_point
+        info, d_c, conv_b, sums_a, sums_b, sums_c, back_c, table, hid, conv_second
     )
     back_b = share(part)
-    grad_second = weights_second(micro, c_mid, c_res, taps_b, pooled)(info, act_b, stack_b)
-    sum_second, sum_point = lax.psum((grad_second, grad_point), BOTH)
-    stack_a, bias_sum = gradient_first(micro, c_in, c_mid, taps, pooled, c_lane)(
+    grad_second, grad_point = weights_second(micro, c_mid, c_res, taps_b, pooled)(
+        info, act_b, stack_b, go, act_c
+    )
+    g_a, bias_sum = gradient_first(micro, c_in, c_mid, taps, pooled, c_lane)(
         info, d_b, hid, go, diff, sums_a, sums_b, back_b, table, grad_second
     )
-    cut = taps - taps // 2
-    lower = weights_first(micro, c_in, c_mid, pooled, 0, cut)(
-        info, act_a, act_a, stack_a, stack_a, bias_sum
-    )
-    upper = weights_first(micro, c_in, c_mid, pooled, cut, taps)(
-        info, act_a, act_a, stack_a, stack_a, lower
-    )
-    lower, _, _ = lax.optimization_barrier((lower, sum_second, sum_point))
-    sum_lower = lax.psum(lower, BOTH)
-    sum_upper = lax.psum(upper, BOTH[::-1])
-    d_a, part = backward_first(micro, c_in, c_mid, taps, pooled, c_lane)(
-        info, stack_a, loaded, sums_a, table, first_b, bias_sum, grad_bias, upper
-    )
-    back_a = share(part)
-    own_in, send_in = finish_first(micro, c_in, pooled, c_lane)(
-        info, d_a, loaded, sums_a, back_a, table
-    )
-    paired = pair_windows(micro, c_in // 2, bins)(info, own_in, partner(send_in))
+    grad_first = weights_first(micro, c_in, c_mid, taps, pooled)(
+        info, act_a, act_a, g_a, g_a, bias_sum
+    )
+    sums = lax.psum((grad_first, grad_second, grad_point), BOTH)
+    running = (
+        mean_first, variance_first, mean_second, variance_second, mean_third, variance_third,
+    )
+
+    def behind(_):
+        d_a, part = backward_first(micro, c_in, c_mid, taps, pooled, c_lane)(
+            info, g_a, loaded, sums_a, table, conv_first, bias_sum, grad_bias
+        )
+        back_a = share(part)
+        own_out, send_out = point_output(micro, c_mid, c_res, pooled, c_lane)(
+            info, act_c, hid, table, conv_point
+        )
+        got_out = partner(send_out)
+        own_in, send_in = finish_first(micro, c_in, pooled, c_lane)(
+            info, d_a, loaded, sums_a, back_a, table
+        )
+        got_in = partner(send_in)
+        small = small_outputs(micro, c_in, c_mid, c_res, c_lane)(
+            info, sums_a, sums_b, sums_c, back_a, back_b, back_c, *running
+        )
+        paired = pair_windows(micro, c_in // 2, bins)(info, own_in, got_in)
+        block_output = jnp.stack(
+            [jnp.where(lead, own_out, got_out), jnp.where(lead, got_out, own_out)], axis=1
+        )
+        return paired, block_output, tuple(small)
+
+    def nothing(_):
+        shapes = jax.eval_shape(behind, 0)
+        return jax.tree.map(lambda s: jnp.zeros(s.shape, s.dtype), shapes)
+
+    paired, block_output, small = lax.cond(info[1] > 0, behind, nothing, 0)
     input_grad = paired.transpose(0, 2, 3, 1)
-    block_output = jnp.stack(
-        [jnp.where(lead, own_out, got_out), jnp.where(lead, got_out, own_out)], axis=1
-    )
-    small = small_outputs(micro, c_in, c_mid, c_res, c_lane)(
-        info, sums_a, sums_b, sums_c, back_a, back_b, back_c,
-        mean_first, variance_first, mean_second, variance_second, mean_third, variance_third,
-    )
-
+    sum_first, sum_second, sum_point = (value.astype(F32) for value in sums)
     return (
         block_output,
         input_grad,
         small[0],
         small[1],
-        jnp.concatenate([sum_lower, sum_upper]).astype(F32),
+        sum_first,
         small[6],
         small[2],
         small[3],
-        sum_second.astype(F32),
+        sum_second,
         small[4],
         small[5],
-        sum_point.astype(F32),
+        sum_point,
         small[7],
         *small[8:],
     )

time: 853 us -> 509 us (0.60)
  waiting for transfers between devices: 410 us -> 85.6 us
    psum x3 -> x1, waiting for transfers between devices: 375 us -> 34.6 us  [shards(): sums = lax.psum((grad_first, grad_second, grad_point), BOTH)]
    ppermute x42, waiting for transfers between devices: 35.1 us -> 48.7 us  [share(): lax.ppermute(rows, BOTH, [(i, i ^ mask) for i in range(devices)])]
    pallas_call x1, Pallas kernels: 28.4 us -> 17.3 us  [shards(): gradient_first(micro, c_in, c_mid, taps, pooled, c_lane)]
    pallas_call x10 -> x9, Pallas kernels: 219 us -> 226 us  [the longest x1 62.3 us: behind(): backward_first(micro, c_in, c_mid, taps, pooled, c_lane)]
  transfers between devices with their start and end apart: 47 -> 45, of which waited for: 35 -> 35; matrix products, arithmetic and copies ran while one was open for 2% -> 1% of each run, Pallas kernels for 8% -> 26%
where the time goes in v2:
time: 509 us; the launch traced here: 505 us
  Pallas kernels  340 us (67%)
  waiting for transfers between devices  85.6 us (17%)
  starting transfers between devices  42.7 us (8%)
  other arithmetic  19.1 us (4%)
  between operations  14.5 us (3%)
    pallas_call x1, Pallas kernels, behind(): backward_first(micro, c_in, c_mid, taps, pooled, c_lane)  62.3 us
    pallas_call x1, Pallas kernels, shards(): weights_first(micro, c_in, c_mid, taps, pooled)  54 us
    pallas_call x1, Pallas kernels, shards(): forward_first(micro, c_in, c_mid, taps, pooled)  49.5 us
    ppermute x42, waiting for transfers between devices, share(): lax.ppermute(rows, BOTH, [(i, i ^ mask) for i in range(devices)])  48.7 us
    ppermute x42, starting transfers between devices, share(): lax.ppermute(rows, BOTH, [(i, i ^ mask) for i in range(devices)])  42.2 us
    psum x1, waiting for transfers between devices, shards(): sums = lax.psum((grad_first, grad_second, grad_point), BOTH)  34.6 us
    pallas_call x1, Pallas kernels, shards(): backward_second(micro, c_in, c_mid, c_res, taps_b, pooled, c_lane)  24.6 us
    pallas_call x1, Pallas kernels, behind(): finish_first(micro, c_in, pooled, c_lane)  19.9 us
  transfers between devices with their start and end apart: 45, of which 35 were waited for; matrix products, arithmetic and copies ran while one was open for 1% of the time, Pallas kernels for 26%

profile of v2, /device:TPU:0, one launch (start us, length us, event | category | flops | bytes accessed | tf_op | source)
XLA Modules:
  0.0 505.3 jit_solution(16624329902843032941)
XLA Ops:
  8.1 16.7 %load_features.1 = (bf16[3,2,656,1024]{3,2,1,0:T(8,128)(2,1)}, f32[8,768]{1,0:T(8,128)}) custom-call(s32[4]{0:T(128)S(1)} %pad_add_fusion.refs_0_, bf16[3,652,2,2048]{3,2,1,0:T(2,128)(2,1)} %bitcast.13), custom_call_target="tpu_custom_call" | custom-call | tf_op jit(solution)/shard_map/load_features/pallas_call | solution.py:1132
  24.8 2.9 collective-permute-start.10
  27.9 1.9 collective-permute-done.10
  32.0 1.5 collective-permute-start.12
  33.5 1.6 collective-permute-start.13
  35.8 1.5 collective-permute-done.13
  37.3 2.5 collective-permute-done.14
  39.8 2.7 collective-permute-start.15
  44.7 16.9 %activate.1.refs_1_.refs_2_ = bf16[3,3984,1024]{2,1,0:T(8,128)(2,1)} custom-call(s32[4]{0:T(128)S(1)} %pad_add_fusion.refs_0_, bf16[3,2,656,1024]{3,2,1,0:T(8,128)(2,1)} %get-tuple-element.142.refs_1_, f32[8,768]{1,0:T(8,128)S(1)} %add.138.refs_2_.refs_3_.refs_5_, f32[8,768]{1,0:T(8,128)S(1)} %prepare_table.1.refs_3_.refs_2_.refs_4_.refs_5_.refs_7_.refs_8_), custom_call_target="tpu_custom_call" | custom-call | tf_op jit(solution)/shard_map/activate/pallas_call | solution.py:1139
  61.7 49.5 %forward_first.1 = (bf16[3,768,1024]{2,1,0:T(8,128)(2,1)S(1)}, f32[3,768,1024]{2,1,0:T(8,128)}, f32[8,768]{1,0:T(8,128)}) custom-call(s32[4]{0:T(128)S(1)} %pad_add_fusion.refs_0_, bf16[3,3984,1024]{2,1,0:T(8,128)(2,1)} %activate.1.refs_1_.refs_2_, f32[8,768]{1,0:T(8,128)S(1)} %prepare_table.1.refs_3_.refs_2_.refs_4_.refs_5_.refs_7_.refs_8_, ...), custom_call_target="tpu_custom_call" | custom-call | tf_op jit(solution)/shard_map/forward_first/pallas_call | solution.py:1140
  113.0 2.3 collective-permute-done.17
  117.2 2.6 collective-permute-start.21
  121.9 2.6 collective-permute-start.22
  124.5 8.2 %turn_cotangent.1 = (bf16[3,768,1024]{2,1,0:T(8,128)(2,1)}, f32[3,384,1024]{2,1,0:T(8,128)}, f32[8,768]{1,0:T(8,128)S(1)}) custom-call(s32[4]{0:T(128)S(1)} %pad_add_fusion.refs_0_, bf16[3,2,1024,768]{3,2,1,0:T(8,128)(2,1)} %refs_1_.3, bf16[384,768]{1,0:T(8,128)(2,1)S(1)} %copy-done.1), custom_call_target="tpu_custom_call" | custom-call | tf_op jit(solution)/shard_map/turn_cotangent/pallas_call | solution.py:1142
  132.7 19.7 %forward_second.1 = (f32[3,384,1024]{2,1,0:T(8,128)}, bf16[3,768,1024]{2,1,0:T(8,128)(2,1)}, f32[8,384]{1,0:T(8,128)}) custom-call(s32[4]{0:T(128)S(1)} %pad_add_fusion.refs_0_, bf16[3,768,1024]{2,1,0:T(8,128)(2,1)S(1)} %get-tuple-element.144.refs_1_.refs_8_.refs_2_, f32[8,768]{1,0:T(8,128)S(1)} %add.138.refs_2_.refs_3_.refs_5_, ...), custom_call_target="tpu_custom_call" | custom-call | tf_op jit(solution)/shard_map/forward_second/pallas_call | solution.py:1143
  154.2 2.0 collective-permute-done.24
  159.1 1.6 collective-permute-start.27
  162.8 2.5 collective-permute-done.28
  165.8 4.1 collective-permute-done.29
  169.9 10.3 %norm_third.1 = (bf16[3,384,1024]{2,1,0:T(8,128)(2,1)}, f32[3,384,1024]{2,1,0:T(8,128)}, f32[8,384]{1,0:T(8,128)}) custom-call(s32[4]{0:T(128)S(1)} %pad_add_fusion.refs_0_, f32[3,384,1024]{2,1,0:T(8,128)} %get-tuple-element.147.refs_1_.refs_2_, f32[3,384,1024]{2,1,0:T(8,128)} %get-tuple-element.148.refs_2_, f32[8,768]{1,0:T(8,128)S(1)} %add.138.refs_2_.refs_3_.refs_5_, ...), custom_call_target="tpu_custom_call" | custom-call | tf_op jit(solution)/shard_map/norm_third/pallas_call | solution.py:1147
  182.1 2.1 collective-permute-done.31
  186.2 2.6 collective-permute-start.35
  191.2 4.2 collective-permute-done.36
  195.4 24.6 %backward_second.1 = (f32[3,768,1024]{2,1,0:T(8,128)}, f32[8,768]{1,0:T(8,128)}, bf16[3,1152,1024]{2,1,0:T(8,128)(2,1)}) custom-call(s32[4]{0:T(128)S(1)} %pad_add_fusion.refs_0_, f32[3,384,1024]{2,1,0:T(8,128)} %get-tuple-element.150.refs_1_, f32[3,384,1024]{2,1,0:T(8,128)} %get-tuple-element.147.refs_1_.refs_2_, ...), custom_call_target="tpu_custom_call" | custom-call | tf_op jit(solution)/shard_map/backward_second/pallas_call | solution.py:1151
  222.0 2.2 collective-permute-done.38
  227.1 1.7 collective-permute-start.41
  229.4 1.6 collective-permute-done.41
  230.9 2.5 collective-permute-done.42
  233.9 13.7 %weights_second.1 = (bf16[3,768,384]{2,1,0:T(8,128)(2,1)}, bf16[384,768]{1,0:T(8,128)(2,1)}) custom-call(s32[4]{0:T(128)S(1)} %pad_add_fusion.refs_0_, bf16[3,768,1024]{2,1,0:T(8,128)(2,1)} %get-tuple-element.156.refs_1_, bf16[3,1152,1024]{2,1,0:T(8,128)(2,1)} %get-tuple-element.157.refs_2_, bf16[3,768,1024]{2,1,0:T(8,128)(2,1)} %get-tuple-element.153.refs_3_, ...), custom_call_target="tpu_custom_call" | custom-call | tf_op jit(solution)/shard_map/weights_second/pallas_call | solution.py:1155
  247.6 17.3 %gradient_first.1 = (bf16[3,2,768,1024]{3,2,1,0:T(8,128)(2,1)}, f32[8,768]{1,0:T(8,128)S(1)}) custom-call(s32[4]{0:T(128)S(1)} %pad_add_fusion.refs_0_, f32[3,768,1024]{2,1,0:T(8,128)} %get-tuple-element.152.refs_1_, bf16[3,768,1024]{2,1,0:T(8,128)(2,1)S(1)} %get-tuple-element.144.refs_1_.refs_8_.refs_2_, bf16[3,768,1024]{2,1,0:T(8,128)(2,1)} %get-tuple-element.153.refs_3_, ...), custom_call_target="tpu_custom_call" | custom-call | tf_op jit(solution)/shard_map/gradient_first/pallas_call | solution.py:1158
  264.9 54.0 %weights_first.1 = bf16[5,652,768]{2,1,0:T(8,128)(2,1)} custom-call(s32[4]{0:T(128)S(1)} %pad_add_fusion.refs_0_, bf16[3,3984,1024]{2,1,0:T(8,128)(2,1)} %activate.1.refs_1_.refs_2_, bf16[3,3984,1024]{2,1,0:T(8,128)(2,1)} %activate.1.refs_1_.refs_2_, bf16[3,2,768,1024]{3,2,1,0:T(8,128)(2,1)} %get-tuple-element.160.refs_3_.refs_4_, ...), custom_call_target="tpu_custom_call" | custom-call | tf_op jit(solution)/shard_map/weights_first/pallas_call | solution.py:1161
  319.7 133.4 %conditional.1 = (bf16[3,326,2,2048]{3,2,1,0:T(2,128)(2,1)}, f32[652]{0:T(1024)S(1)}, f32[652]{0:T(1024)}, f32[768]{0:T(1024)}, f32[768]{0:T(1024)}, /*index=5*/...) conditional(s32[]{:T(128)} %bitcast.2, () %tuple.16, ...), branch_computations={%region_0.1_spmd, %region_1.2_spmd} | conditional | flops 4761600 | bytes 68936216 | solution.py:1195
  319.7 62.3 %backward_first.1 = (f32[3,2,656,1024]{3,2,1,0:T(8,128)}, f32[8,768]{1,0:T(8,128)}) custom-call(s32[4]{0:T(128)S(1)} %get-tuple-element.44.refs_0_, bf16[3,2,768,1024]{3,2,1,0:T(8,128)(2,1)} %get-tuple-element.45.refs_1_, bf16[3,2,656,1024]{3,2,1,0:T(8,128)(2,1)} %get-tuple-element.46.refs_2_, f32[8,768]{1,0:T(8,128)S(1)} %get-tuple-element.47.refs_3_.refs_1_, ...), custom_call_target="tpu_custom_call" | custom-call | tf_op jit(solution)/shard_map/cond/branch_1_fun/backward_first/pallas_call | solution.py:1170
  382.1 1.8 collective-permute-start.2
  383.9 2.2 collective-permute-done.1
  387.1 3.3 collective-permute-start.5
  393.4 2.1 collective-permute-start.6
  395.5 3.4 collective-permute-done.6
  399.6 19.9 %finish_first.1 = (bf16[3,326,2048]{2,1,0:T(8,128)(2,1)}, bf16[3,326,2048]{2,1,0:T(8,128)(2,1)}) custom-call(s32[4]{0:T(128)S(1)} %get-tuple-element.44.refs_0_, f32[3,2,656,1024]{3,2,1,0:T(8,128)} %get-tuple-element.52.refs_1_, bf16[3,2,656,1024]{3,2,1,0:T(8,128)(2,1)} %get-tuple-element.46.refs_2_, f32[8,768]{1,0:T(8,128)S(1)} %get-tuple-element.47.refs_3_.refs_1_, ...), custom_call_target="tpu_custom_call" | custom-call | tf_op jit(solution)/shard_map/cond/branch_1_fun/finish_first/pallas_call | solution.py:1178
  419.5 10.1 %point_output.1 = (bf16[3,1024,384]{2,1,0:T(8,128)(2,1)}, bf16[3,1024,384]{2,1,0:T(8,128)(2,1)}) custom-call(s32[4]{0:T(128)S(1)} %get-tuple-element.44.refs_0_, bf16[3,384,1024]{2,1,0:T(8,128)(2,1)} %get-tuple-element.57.refs_1_, bf16[3,768,1024]{2,1,0:T(8,128)(2,1)S(1)} %bitcast.12, f32[8,768]{1,0:T(8,128)S(1)} %get-tuple-element.48.refs_4_.refs_5_.refs_3_, ...), custom_call_target="tpu_custom_call" | custom-call | tf_op jit(solution)/shard_map/cond/branch_1_fun/point_output/pallas_call | solution.py:1174
  430.1 2.0 small_outputs.1
  432.2 2.3 collective-permute-done.8
  434.5 2.1 select_bitcast_fusion.1
  437.2 2.7 copy.47
  439.9 13.3 %pair_windows.1 = bf16[3,326,2,2048]{3,2,1,0:T(2,128)(2,1)} custom-call(s32[4]{0:T(128)S(1)} %get-tuple-element.44.refs_0_, bf16[3,326,2048]{2,1,0:T(8,128)(2,1)} %get-tuple-element.54.refs_1_, bf16[3,326,2048]{2,1,0:T(8,128)(2,1)} %collective-permute-done.7.refs_2_), custom_call_target="tpu_custom_call" | custom-call | tf_op jit(solution)/shard_map/cond/branch_1_fun/pair_windows/pallas_call | solution.py:1185
  453.1 34.6 %all-reduce.3.cloned.1.call-done = (bf16[5,652,768]{2,1,0:T(8,128)(2,1)}, bf16[3,768,384]{2,1,0:T(8,128)(2,1)}, bf16[384,768]{1,0:T(8,128)(2,1)}) async-done(((bf16[5,652,768]{2,1,0:T(8,128)(2,1)}, bf16[3,768,384]{2,1,0:T(8,128)(2,1)}, bf16[384,768]{1,0:T(8,128)(2,1)}), (bf16[5,652,768]{2,1,0:T(8,128)(2,1)}, bf16[3,768,384]{2,1,0:T(8,128)(2,1)}, bf16[384,768]{1,0:T(8,128)(2,1)})) %all-reduce.3.cloned.1.call-update) | async-done | bytes 7366672 | tf_op jit(solution)/shard_map/psum | solution.py:1164
  487.7 7.4 %convert_element_type.18 = f32[5,652,768]{2,1,0:T(8,128)} convert(bf16[5,652,768]{2,1,0:T(8,128)(2,1)} %get-tuple-element.211) | non-fusion elementwise | flops 2503680 | bytes 15022080 | tf_op jit(solution)/shard_map/convert_element_type | solution.py:1197
  495.1 2.0 convert_element_type.19
  (116 shorter events, 39.0 us)
Async XLA Ops:
  7.2 480.5 %all-reduce.3.cloned.1.call-start = ((), (), s32[]{:S(2)}) async-start(), calls=%async_computation | async-start | bytes 14794752 | tf_op jit(solution)/shard_map/psum | solution.py:1164
  24.8 5.0 collective-permute-start.10
  27.8 3.5 collective-permute-start.11
  27.8 3.5 collective-permute-start.9
  32.0 3.8 collective-permute-start.12
  33.5 3.8 collective-permute-start.13
  35.1 4.7 collective-permute-start.14
  39.8 4.9 collective-permute-start.15
  61.7 62.8 %copy-start.1 = (bf16[384,768]{1,0:T(8,128)(2,1)S(1)}, bf16[384,768]{1,0:T(8,128)(2,1)}, u32[]{:S(2)}) copy-start(bf16[384,768]{1,0:T(8,128)(2,1)} %refs_2_.3) | copy-start | bytes 1769476
  111.2 136.4 %copy-start = (bf16[3,768,1024]{2,1,0:T(8,128)(2,1)}, bf16[3,768,1024]{2,1,0:T(8,128)(2,1)S(1)}, u32[]{:S(2)}) copy-start(bf16[3,768,1024]{2,1,0:T(8,128)(2,1)S(1)} %get-tuple-element.144.refs_1_.refs_8_.refs_2_) | copy-start | bytes 14155780
  111.2 1.9 collective-permute-start.16
  111.2 4.1 collective-permute-start.17
  112.0 3.5 collective-permute-start.18
  116.3 3.8 collective-permute-start.19
  116.9 3.9 collective-permute-start.20
  117.2 4.7 collective-permute-start.21
  121.9 10.7 %collective-permute-start.22 = (f32[8,768]{1,0:T(8,128)S(1)}, f32[8,768]{1,0:T(8,128)S(1)}, u32[]{:S(2)}, u32[]{:S(2)}) collective-permute-start(f32[8,768]{1,0:T(8,128)S(1)} %add_add_fusion.4), channel_id=1, source_target_pairs={{0,8},{1,9},{2,10},{3,11},{4,12},{5,13},{6,14},{7,15},{8,0},{9,1},... | collective-permute-start | bytes 73736 | tf_op jit(solution)/shard_map/ppermute | solution.py:1090
  152.4 1.9 collective-permute-start.23
  152.4 3.9 collective-permute-start.24
  153.5 3.3 collective-permute-start.25
  157.6 3.7 collective-permute-start.26
  159.1 3.7 collective-permute-start.27
  160.7 4.6 collective-permute-start.28
  165.3 4.6 collective-permute-start.29
  180.2 1.9 collective-permute-start.30
  180.3 4.0 collective-permute-start.31
  181.2 3.3 collective-permute-start.32
  185.3 3.7 collective-permute-start.33
  185.7 3.8 collective-permute-start.34
  186.2 4.6 collective-permute-start.35
  190.8 4.6 collective-permute-start.36
  220.0 1.9 collective-permute-start.37
  220.1 4.1 collective-permute-start.38
  221.3 3.5 collective-permute-start.39
  225.6 3.8 collective-permute-start.40
  227.1 3.9 collective-permute-start.41
  228.7 4.7 collective-permute-start.42
  233.5 14.1 %collective-permute-start.43 = (f32[8,768]{1,0:T(8,128)S(1)}, f32[8,768]{1,0:T(8,128)S(1)}, u32[]{:S(2)}, u32[]{:S(2)}) collective-permute-start(f32[8,768]{1,0:T(8,128)S(1)} %add_add_fusion.2), channel_id=1, source_target_pairs={{0,8},{1,9},{2,10},{3,11},{4,12},{5,13},{6,14},{7,15},{8,0},{9,1},... | collective-permute-start | bytes 73736 | tf_op jit(solution)/shard_map/ppermute | solution.py:1090
  319.7 99.8 %slice-start = ((s8[4718592]{0:T(1024)(128)(4,1)}), s8[4194304]{0:T(1024)(128)(4,1)S(1)}, s32[]{:S(2)}) async-start(s8[4718592]{0:T(1024)(128)(4,1)} %bitcast.11), calls=%async_computation.1 | async-start | bytes 8388608 | tf_op jit(solution)/shard_map/cond
  382.1 1.9 collective-permute-start
  382.1 4.1 collective-permute-start.1
  382.1 4.0 collective-permute-start.2
  386.9 4.2 collective-permute-start.3
  386.9 5.0 collective-permute-start.4
  387.1 6.3 %collective-permute-start.5 = (f32[8,768]{1,0:T(8,128)S(1)}, f32[8,768]{1,0:T(8,128)S(1)}, u32[]{:S(2)}, u32[]{:S(2)}) collective-permute-start(f32[8,768]{1,0:T(8,128)S(1)} %add_add_fusion.1), channel_id=1, source_target_pairs={{0,6},{1,7},{2,4},{3,5},{4,2},{5,3},{6,0},{7,1},{8,14},{9,15},{10,... | collective-permute-start | bytes 73736 | tf_op jit(solution)/shard_map/cond/branch_1_fun/ppermute | solution.py:1090
  393.4 5.6 %collective-permute-start.6 = (f32[8,768]{1,0:T(8,128)S(1)}, f32[8,768]{1,0:T(8,128)S(1)}, u32[]{:S(2)}, u32[]{:S(2)}) collective-permute-start(f32[8,768]{1,0:T(8,128)S(1)} %add_add_fusion), channel_id=1, source_target_pairs={{0,8},{1,9},{2,10},{3,11},{4,12},{5,13},{6,14},{7,15},{8,0},{9,1},... | collective-permute-start | bytes 73736 | tf_op jit(solution)/shard_map/cond/branch_1_fun/ppermute | solution.py:1090
  419.5 20.3 %collective-permute-start.7 = (bf16[3,326,2048]{2,1,0:T(8,128)(2,1)}, bf16[3,326,2048]{2,1,0:T(8,128)(2,1)}, u32[]{:S(2)}, u32[]{:S(2)}) collective-permute-start(bf16[3,326,2048]{2,1,0:T(8,128)(2,1)} %get-tuple-element.55), channel_id=1, source_target_pairs={{0,16},{16,0},{1,17},{17,1},{2,18},{18,2},{3,19},{19,3},{4,20},{20... | collective-permute-start | bytes 12017672 | tf_op jit(solution)/shard_map/cond/branch_1_fun/ppermute | solution.py:1074
  429.7 4.9 collective-permute-start.8
  (11 other events, 76.5 us)
Sparse Core Ops, SparseCore 0:
  319.1 168.5 all-reduce.2

commit v3 on v2

--- a/solution.py
+++ b/solution.py
@@ -340,7 +340,7 @@
     base = c_pad - c_pad % LANES
 
     def body(info, stack, table, weight, hid, diff, st_ref,
-             bias, s_acc, q_acc, even, odd, held, line):
+             bias, s_acc, q_acc, even, odd, even_next, odd_next, held, line):
         step = pl.program_id(0)
         late = jnp.maximum(step - 1, 0)
         k, at = late // steps, late % steps
@@ -365,11 +365,11 @@
             s_acc[...] = jnp.zeros_like(s_acc)
             q_acc[...] = jnp.zeros_like(q_acc)
 
-        def finish():
-            for start in range(0, c_mid, 16):
+        def finish(old, first, last):
+            for start in range(first, last, 16):
                 rows = slice(start, start + 16)
                 b = wide(bias[rows, :], STEP)
-                left, right = even[rows, :] + b, odd[rows, :] + b
+                left, right = old[0][rows, :] + b, old[1][rows, :] + b
                 apart = left - right
                 joined = jnp.maximum(left, right) + jnp.log1p(jnp.exp(-jnp.abs(apart)))
                 rounded = (joined * mask).astype(BF16)
@@ -379,15 +379,25 @@
                 s_acc[rows, :] += fold(value)
                 q_acc[rows, :] += fold(value * value)
 
-        @pl.when(step < total)
-        def _():
-            finish()
-            even[...] = nn(held[...], stack[0, :depth, :])
-            odd[...] = nn(held[...], stack[0, c_pad : c_pad + depth, :])
+        def both(new, old):
+            parts = [(side, lane) for side in range(2) for lane in range(0, STEP, TILE)]
+            share_of = c_mid // len(parts)
+            for part, (side, lane) in enumerate(parts):
+                lanes = slice(lane, lane + TILE)
+                taken = slice(side * c_pad, side * c_pad + depth)
+                new[side][:, lanes] = nn(held[...], stack[0, taken, lanes])
+                finish(old, part * share_of, (part + 1) * share_of)
+
+        pairs = (even, odd), (even_next, odd_next)
+        for turn in range(2):
+
+            @pl.when((step < total) & (step % 2 == turn))
+            def _(turn=turn):
+                both(pairs[turn], pairs[1 - turn])
 
         @pl.when(step == total)
         def _():
-            finish()
+            finish(pairs[(total - 1) % 2], 0, c_mid)
 
         @pl.when(at == steps - 1)
         def _():
@@ -413,7 +423,7 @@
             shape_of((8, c_mid)),
         ],
         [pltpu.VMEM((c_mid, LANES), F32)] * 3
-        + [pltpu.VMEM((c_mid, STEP), F32)] * 2
+        + [pltpu.VMEM((c_mid, STEP), F32)] * 4
         + [
             pltpu.VMEM((c_mid, depth), BF16),
             pltpu.VMEM((TILE, max(depth, (taps - 1) * base + room)), F32),
@@ -810,39 +820,68 @@
 
 def weights_first(micro, c_in, c_mid, taps, pooled):
     c_pad = up(c_in, 16)
-
-    def body(info, act_left, act_right, left, right, grad_conv, product, held_left, held_right):
+    rows = taps * c_pad
+    steps = c_mid // TILE
+
+    def body(info, act, left, right, grad_conv, product):
         k, at = pl.program_id(0), pl.program_id(1)
-
-        @pl.when(at == 0)
-        def _():
-            held_left[...] = left[0, 0]
-            held_right[...] = right[0, 0]
-
-        value = nt(act_left[0], held_left[...]) + nt(act_right[0], held_right[...])
+        value = nt(act[0, :rows, :], left[0, 0]) + nt(act[0, c_pad : c_pad + rows, :], right[0, 0])
         product[at] = value + jnp.where(k == 0, 0.0, product[at])
 
         @pl.when(k == micro - 1)
         def _():
-            grad_conv[0] = product[at, :c_in, :].astype(BF16)
-
-    def act_block(shift):
-        return pl.BlockSpec((1, c_pad, pooled), lambda k, j, _: (k, j + shift, 0))
+            for tap in range(taps):
+                own = product[at, tap * c_pad : tap * c_pad + c_in, :]
+                grad_conv[tap] = own.astype(BF16)
 
     def grad_block(side):
-        return pl.BlockSpec((1, 1, c_mid, pooled), lambda k, j, _: (k, side, 0, 0))
+        return pl.BlockSpec((1, 1, TILE, pooled), lambda k, j, _: (k, side, j, 0))
 
     return call(
         "weights_first",
         body,
-        (micro, taps),
-        [act_block(0), act_block(1), grad_block(0), grad_block(1)],
+        (micro, steps),
+        [
+            per_batch((rows + c_pad, pooled)),
+            grad_block(0),
+            grad_block(1),
+        ],
         pl.BlockSpec(
-            (1, c_in, c_mid), lambda k, j, _: (jnp.where(k == micro - 1, j, 0), 0, 0)
+            (taps, c_in, TILE), lambda k, j, _: (0, 0, jnp.where(k == micro - 1, j, 0))
         ),
         shape_of((taps, c_in, c_mid), BF16),
-        [pltpu.VMEM((taps, c_pad, c_mid), F32)] + [pltpu.VMEM((c_mid, pooled), BF16)] * 2,
+        [pltpu.VMEM((steps, rows, TILE), F32)],
         after=1,
+    )
+
+
+def widen(first, second, third):
+    steps = first[0]
+    most = second[0] - 1
+
+    def body(info, first_in, second_in, third_in, first_out, second_out, third_out):
+        first_out[...] = first_in[...].astype(F32)
+
+        @pl.when(pl.program_id(0) <= most)
+        def _():
+            second_out[...] = second_in[...].astype(F32)
+
+        @pl.when(pl.program_id(0) == 0)
+        def _():
+            third_out[...] = third_in[...].astype(F32)
+
+    specs = [
+        pl.BlockSpec((1,) + first[1:], lambda i, _: (i, 0, 0)),
+        pl.BlockSpec((1,) + second[1:], lambda i, _: (jnp.minimum(i, most), 0, 0)),
+        whole(third),
+    ]
+    return call(
+        "widen",
+        body,
+        (steps,),
+        specs,
+        specs,
+        [shape_of(s) for s in (first, second, third)],
     )
 
 
@@ -1159,7 +1198,7 @@
         info, d_b, hid, go, diff, sums_a, sums_b, back_b, table, grad_second
     )
     grad_first = weights_first(micro, c_in, c_mid, taps, pooled)(
-        info, act_a, act_a, g_a, g_a, bias_sum
+        info, act_a, g_a, g_a, bias_sum
     )
     sums = lax.psum((grad_first, grad_second, grad_point), BOTH)
     running = (
@@ -1194,7 +1233,7 @@
 
     paired, block_output, small = lax.cond(info[1] > 0, behind, nothing, 0)
     input_grad = paired.transpose(0, 2, 3, 1)
-    sum_first, sum_second, sum_point = (value.astype(F32) for value in sums)
+    sum_first, sum_second, sum_point = widen(*(value.shape for value in sums))(info, *sums)
     return (
         block_output,
         input_grad,

time: 509 us -> 491 us (0.965)
  other arithmetic: 19.1 us -> 8.58 us
  Pallas kernels: 340 us -> 332 us
    pallas_call x1, Pallas kernels: 54 us -> 39.8 us  [shards(): weights_first(micro, c_in, c_mid, taps, pooled)]
    convert_element_type x3 -> x0, other arithmetic: 10.5 us -> none  [shards(): sum_first, sum_second, sum_point = (value.astype(F32) for value in sums)]
    pallas_call x0 -> x1, Pallas kernels: none -> 9.68 us  [shards(): widen(*(value.shape for value in sums))(info, *sums)]
  transfers between devices with their start and end apart: 45 -> 45, of which waited for: 35 -> 35; matrix products, arithmetic and copies ran while one was open for 1% -> 1% of each run, Pallas kernels for 26% -> 27%
where the time goes in v3:
time: 491 us; the launch traced here: 487 us
  Pallas kernels  332 us (68%)
  waiting for transfers between devices  85.7 us (17%)
  starting transfers between devices  42.7 us (9%)
  between operations  14.5 us (3%)
  other arithmetic  8.58 us (2%)
    pallas_call x1, Pallas kernels, behind(): backward_first(micro, c_in, c_mid, taps, pooled, c_lane)  62.3 us
    ppermute x42, waiting for transfers between devices, share(): lax.ppermute(rows, BOTH, [(i, i ^ mask) for i in range(devices)])  48.7 us
    pallas_call x1, Pallas kernels, shards(): forward_first(micro, c_in, c_mid, taps, pooled)  46.1 us
    ppermute x42, starting transfers between devices, share(): lax.ppermute(rows, BOTH, [(i, i ^ mask) for i in range(devices)])  42.2 us
    pallas_call x1, Pallas kernels, shards(): weights_first(micro, c_in, c_mid, taps, pooled)  39.8 us
    psum x1, waiting for transfers between devices, shards(): sums = lax.psum((grad_first, grad_second, grad_point), BOTH)  34.6 us
    pallas_call x1, Pallas kernels, shards(): backward_second(micro, c_in, c_mid, c_res, taps_b, pooled, c_lane)  24.6 us
    pallas_call x1, Pallas kernels, behind(): finish_first(micro, c_in, pooled, c_lane)  20 us
  transfers between devices with their start and end apart: 45, of which 35 were waited for; matrix products, arithmetic and copies ran while one was open for 1% of the time, Pallas kernels for 27%

profile of v3, /device:TPU:0, one launch (start us, length us, event | category | flops | bytes accessed | tf_op | source)
XLA Modules:
  0.0 486.8 jit_solution(16483871955354261305)
XLA Ops:
  8.1 16.7 %load_features.1 = (bf16[3,2,656,1024]{3,2,1,0:T(8,128)(2,1)}, f32[8,768]{1,0:T(8,128)}) custom-call(s32[4]{0:T(128)S(1)} %pad_add_fusion.refs_0_, bf16[3,652,2,2048]{3,2,1,0:T(2,128)(2,1)} %bitcast.13), custom_call_target="tpu_custom_call" | custom-call | tf_op jit(solution)/shard_map/load_features/pallas_call | solution.py:1171
  24.8 2.9 collective-permute-start.10
  27.9 1.9 collective-permute-done.10
  29.8 1.5 collective-permute-done.11
  32.0 1.5 collective-permute-start.12
  33.5 1.6 collective-permute-start.13
  35.8 1.6 collective-permute-done.13
  37.4 2.4 collective-permute-done.14
  39.8 2.9 collective-permute-start.15
  44.8 16.9 %activate.1.refs_1_ = bf16[3,3984,1024]{2,1,0:T(8,128)(2,1)} custom-call(s32[4]{0:T(128)S(1)} %pad_add_fusion.refs_0_, bf16[3,2,656,1024]{3,2,1,0:T(8,128)(2,1)} %get-tuple-element.145.refs_1_, f32[8,768]{1,0:T(8,128)S(1)} %add.138.refs_2_.refs_3_.refs_5_, f32[8,768]{1,0:T(8,128)S(1)} %prepare_table.1.refs_3_.refs_2_.refs_4_.refs_5_.refs_7_.refs_8_), custom_call_target="tpu_custom_call" | custom-call | tf_op jit(solution)/shard_map/activate/pallas_call | solution.py:1178
  61.7 46.1 %forward_first.1 = (bf16[3,768,1024]{2,1,0:T(8,128)(2,1)S(1)}, f32[3,768,1024]{2,1,0:T(8,128)}, f32[8,768]{1,0:T(8,128)}) custom-call(s32[4]{0:T(128)S(1)} %pad_add_fusion.refs_0_, bf16[3,3984,1024]{2,1,0:T(8,128)(2,1)} %activate.1.refs_1_, f32[8,768]{1,0:T(8,128)S(1)} %prepare_table.1.refs_3_.refs_2_.refs_4_.refs_5_.refs_7_.refs_8_, ...), custom_call_target="tpu_custom_call" | custom-call | tf_op jit(solution)/shard_map/forward_first/pallas_call | solution.py:1179
  109.8 2.3 collective-permute-done.17
  113.9 2.6 collective-permute-start.21
  118.6 2.7 collective-permute-start.22
  121.4 8.2 %turn_cotangent.1 = (bf16[3,768,1024]{2,1,0:T(8,128)(2,1)}, f32[3,384,1024]{2,1,0:T(8,128)}, f32[8,768]{1,0:T(8,128)S(1)}) custom-call(s32[4]{0:T(128)S(1)} %pad_add_fusion.refs_0_, bf16[3,2,1024,768]{3,2,1,0:T(8,128)(2,1)} %refs_1_.3, bf16[384,768]{1,0:T(8,128)(2,1)S(1)} %copy-done.1), custom_call_target="tpu_custom_call" | custom-call | tf_op jit(solution)/shard_map/turn_cotangent/pallas_call | solution.py:1181
  129.5 19.5 %forward_second.1 = (f32[3,384,1024]{2,1,0:T(8,128)}, bf16[3,768,1024]{2,1,0:T(8,128)(2,1)}, f32[8,384]{1,0:T(8,128)}) custom-call(s32[4]{0:T(128)S(1)} %pad_add_fusion.refs_0_, bf16[3,768,1024]{2,1,0:T(8,128)(2,1)S(1)} %get-tuple-element.147.refs_1_.refs_8_.refs_2_, f32[8,768]{1,0:T(8,128)S(1)} %add.138.refs_2_.refs_3_.refs_5_, ...), custom_call_target="tpu_custom_call" | custom-call | tf_op jit(solution)/shard_map/forward_second/pallas_call | solution.py:1182
  150.8 2.0 collective-permute-done.24
  155.6 1.8 collective-permute-start.27
  159.3 2.7 collective-permute-done.28
  162.2 4.4 collective-permute-done.29
  166.6 10.3 %norm_third.1 = (bf16[3,384,1024]{2,1,0:T(8,128)(2,1)}, f32[3,384,1024]{2,1,0:T(8,128)}, f32[8,384]{1,0:T(8,128)}) custom-call(s32[4]{0:T(128)S(1)} %pad_add_fusion.refs_0_, f32[3,384,1024]{2,1,0:T(8,128)} %get-tuple-element.150.refs_1_.refs_2_, f32[3,384,1024]{2,1,0:T(8,128)} %get-tuple-element.151.refs_2_, f32[8,768]{1,0:T(8,128)S(1)} %add.138.refs_2_.refs_3_.refs_5_, ...), custom_call_target="tpu_custom_call" | custom-call | tf_op jit(solution)/shard_map/norm_third/pallas_call | solution.py:1186
  178.8 2.1 collective-permute-done.31
  182.9 2.6 collective-permute-start.35
  185.9 1.6 collective-permute-done.35
  187.7 4.4 collective-permute-done.36
  192.1 24.6 %backward_second.1 = (f32[3,768,1024]{2,1,0:T(8,128)}, f32[8,768]{1,0:T(8,128)}, bf16[3,1152,1024]{2,1,0:T(8,128)(2,1)}) custom-call(s32[4]{0:T(128)S(1)} %pad_add_fusion.refs_0_, f32[3,384,1024]{2,1,0:T(8,128)} %get-tuple-element.153.refs_1_, f32[3,384,1024]{2,1,0:T(8,128)} %get-tuple-element.150.refs_1_.refs_2_, ...), custom_call_target="tpu_custom_call" | custom-call | tf_op jit(solution)/shard_map/backward_second/pallas_call | solution.py:1190
  218.7 2.2 collective-permute-done.38
  223.6 1.8 collective-permute-start.41
  227.4 2.7 collective-permute-done.42
  230.4 13.8 %weights_second.1 = (bf16[3,768,384]{2,1,0:T(8,128)(2,1)}, bf16[384,768]{1,0:T(8,128)(2,1)}) custom-call(s32[4]{0:T(128)S(1)} %pad_add_fusion.refs_0_, bf16[3,768,1024]{2,1,0:T(8,128)(2,1)} %get-tuple-element.159.refs_1_, bf16[3,1152,1024]{2,1,0:T(8,128)(2,1)} %get-tuple-element.160.refs_2_, bf16[3,768,1024]{2,1,0:T(8,128)(2,1)} %get-tuple-element.156.refs_3_, ...), custom_call_target="tpu_custom_call" | custom-call | tf_op jit(solution)/shard_map/weights_second/pallas_call | solution.py:1194
  244.3 17.3 %gradient_first.1 = (bf16[3,2,768,1024]{3,2,1,0:T(8,128)(2,1)}, f32[8,768]{1,0:T(8,128)S(1)}) custom-call(s32[4]{0:T(128)S(1)} %pad_add_fusion.refs_0_, f32[3,768,1024]{2,1,0:T(8,128)} %get-tuple-element.155.refs_1_, bf16[3,768,1024]{2,1,0:T(8,128)(2,1)S(1)} %get-tuple-element.147.refs_1_.refs_8_.refs_2_, bf16[3,768,1024]{2,1,0:T(8,128)(2,1)} %get-tuple-element.156.refs_3_, ...), custom_call_target="tpu_custom_call" | custom-call | tf_op jit(solution)/shard_map/gradient_first/pallas_call | solution.py:1197
  261.5 39.8 %weights_first.1 = bf16[5,652,768]{2,1,0:T(8,128)(2,1)} custom-call(s32[4]{0:T(128)S(1)} %pad_add_fusion.refs_0_, bf16[3,3984,1024]{2,1,0:T(8,128)(2,1)} %activate.1.refs_1_, bf16[3,2,768,1024]{3,2,1,0:T(8,128)(2,1)} %get-tuple-element.163.refs_2_.refs_3_, bf16[3,2,768,1024]{3,2,1,0:T(8,128)(2,1)} %get-tuple-element.163.refs_2_.refs_3_, ...), custom_call_target="tpu_custom_call" | custom-call | tf_op jit(solution)/shard_map/weights_first/pallas_call | solution.py:1200
  302.1 133.4 %conditional.1 = (bf16[3,326,2,2048]{3,2,1,0:T(2,128)(2,1)}, f32[652]{0:T(1024)S(1)}, f32[652]{0:T(1024)}, f32[768]{0:T(1024)}, f32[768]{0:T(1024)}, /*index=5*/...) conditional(s32[]{:T(128)} %bitcast.2, () %tuple.16, ...), branch_computations={%region_0.1_spmd, %region_1.2_spmd} | conditional | flops 4761600 | bytes 68936216 | solution.py:1234
  302.2 62.3 %backward_first.1 = (f32[3,2,656,1024]{3,2,1,0:T(8,128)}, f32[8,768]{1,0:T(8,128)}) custom-call(s32[4]{0:T(128)S(1)} %get-tuple-element.44.refs_0_, bf16[3,2,768,1024]{3,2,1,0:T(8,128)(2,1)} %get-tuple-element.45.refs_1_, bf16[3,2,656,1024]{3,2,1,0:T(8,128)(2,1)} %get-tuple-element.46.refs_2_, f32[8,768]{1,0:T(8,128)S(1)} %get-tuple-element.47.refs_3_.refs_1_, ...), custom_call_target="tpu_custom_call" | custom-call | tf_op jit(solution)/shard_map/cond/branch_1_fun/backward_first/pallas_call | solution.py:1209
  364.5 1.8 collective-permute-start.2
  366.3 2.2 collective-permute-done.1
  369.5 3.3 collective-permute-start.5
  375.8 2.4 collective-permute-start.6
  378.2 3.2 collective-permute-done.6
  382.0 20.0 %finish_first.1 = (bf16[3,326,2048]{2,1,0:T(8,128)(2,1)}, bf16[3,326,2048]{2,1,0:T(8,128)(2,1)}) custom-call(s32[4]{0:T(128)S(1)} %get-tuple-element.44.refs_0_, f32[3,2,656,1024]{3,2,1,0:T(8,128)} %get-tuple-element.52.refs_1_, bf16[3,2,656,1024]{3,2,1,0:T(8,128)(2,1)} %get-tuple-element.46.refs_2_, f32[8,768]{1,0:T(8,128)S(1)} %get-tuple-element.47.refs_3_.refs_1_, ...), custom_call_target="tpu_custom_call" | custom-call | tf_op jit(solution)/shard_map/cond/branch_1_fun/finish_first/pallas_call | solution.py:1217
  402.0 10.1 %point_output.1 = (bf16[3,1024,384]{2,1,0:T(8,128)(2,1)}, bf16[3,1024,384]{2,1,0:T(8,128)(2,1)}) custom-call(s32[4]{0:T(128)S(1)} %get-tuple-element.44.refs_0_, bf16[3,384,1024]{2,1,0:T(8,128)(2,1)} %get-tuple-element.57.refs_1_, bf16[3,768,1024]{2,1,0:T(8,128)(2,1)S(1)} %bitcast.12, f32[8,768]{1,0:T(8,128)S(1)} %get-tuple-element.48.refs_4_.refs_5_.refs_3_, ...), custom_call_target="tpu_custom_call" | custom-call | tf_op jit(solution)/shard_map/cond/branch_1_fun/point_output/pallas_call | solution.py:1213
  412.6 2.0 small_outputs.1
  414.6 2.3 collective-permute-done.8
  416.9 2.1 select_bitcast_fusion.1
  419.6 2.7 copy.47
  422.3 13.3 %pair_windows.1 = bf16[3,326,2,2048]{3,2,1,0:T(2,128)(2,1)} custom-call(s32[4]{0:T(128)S(1)} %get-tuple-element.44.refs_0_, bf16[3,326,2048]{2,1,0:T(8,128)(2,1)} %get-tuple-element.54.refs_1_, bf16[3,326,2048]{2,1,0:T(8,128)(2,1)} %collective-permute-done.7.refs_2_), custom_call_target="tpu_custom_call" | custom-call | tf_op jit(solution)/shard_map/cond/branch_1_fun/pair_windows/pallas_call | solution.py:1224
  435.5 34.6 %all-reduce.3.cloned.1.call-done = (bf16[5,652,768]{2,1,0:T(8,128)(2,1)}, bf16[3,768,384]{2,1,0:T(8,128)(2,1)}, bf16[384,768]{1,0:T(8,128)(2,1)}) async-done(((bf16[5,652,768]{2,1,0:T(8,128)(2,1)}, bf16[3,768,384]{2,1,0:T(8,128)(2,1)}, bf16[384,768]{1,0:T(8,128)(2,1)}), (bf16[5,652,768]{2,1,0:T(8,128)(2,1)}, bf16[3,768,384]{2,1,0:T(8,128)(2,1)}, bf16[384,768]{1,0:T(8,128)(2,1)})) %all-reduce.3.cloned.1.call-update) | async-done | bytes 7366672 | tf_op jit(solution)/shard_map/psum | solution.py:1203
  470.1 9.7 %widen.1 = (f32[5,652,768]{2,1,0:T(8,128)}, f32[3,768,384]{2,1,0:T(8,128)}, f32[384,768]{1,0:T(8,128)}) custom-call(s32[4]{0:T(128)S(1)} %pad_add_fusion.refs_0_, bf16[5,652,768]{2,1,0:T(8,128)(2,1)} %get-tuple-element.217.refs_1_, bf16[3,768,384]{2,1,0:T(8,128)(2,1)} %get-tuple-element.218.refs_2_, bf16[384,768]{1,0:T(8,128)(2,1)} %get-tuple-element.219.refs_3_), custom_call_target="tpu_custom_call" | custom-call | tf_op jit(solution)/shard_map/widen/pallas_call | solution.py:1236
  (110 shorter events, 34.8 us)
Async XLA Ops:
  7.2 462.9 %all-reduce.3.cloned.1.call-start = ((), (), s32[]{:S(2)}) async-start(), calls=%async_computation | async-start | bytes 14794752 | tf_op jit(solution)/shard_map/psum | solution.py:1203
  24.8 4.9 %collective-permute-start.10 = (f32[8,768]{1,0:T(8,128)}, f32[8,768]{1,0:T(8,128)S(1)}, u32[]{:S(2)}, u32[]{:S(2)}) collective-permute-start(f32[8,768]{1,0:T(8,128)} %get-tuple-element.146), channel_id=1, source_target_pairs={{0,1},{1,0},{2,3},{3,2},{4,5},{5,4},{6,7},{7,6},{8,9},{9,8},{10,11... | collective-permute-start | bytes 73736 | tf_op jit(solution)/shard_map/ppermute | solution.py:1129
  27.7 3.5 collective-permute-start.11
  27.7 3.5 collective-permute-start.9
  32.0 3.8 collective-permute-start.12
  33.5 3.9 collective-permute-start.13
  35.1 4.7 collective-permute-start.14
  39.8 4.9 %collective-permute-start.15 = (f32[8,768]{1,0:T(8,128)S(1)}, f32[8,768]{1,0:T(8,128)S(1)}, u32[]{:S(2)}, u32[]{:S(2)}) collective-permute-start(f32[8,768]{1,0:T(8,128)S(1)} %add_add_fusion.6), channel_id=1, source_target_pairs={{0,8},{1,9},{2,10},{3,11},{4,12},{5,13},{6,14},{7,15},{8,0},{9,1},... | collective-permute-start | bytes 73736 | tf_op jit(solution)/shard_map/ppermute | solution.py:1129
  61.7 59.7 %copy-start.1 = (bf16[384,768]{1,0:T(8,128)(2,1)S(1)}, bf16[384,768]{1,0:T(8,128)(2,1)}, u32[]{:S(2)}) copy-start(bf16[384,768]{1,0:T(8,128)(2,1)} %refs_2_.3) | copy-start | bytes 1769476
  107.8 136.4 %copy-start = (bf16[3,768,1024]{2,1,0:T(8,128)(2,1)}, bf16[3,768,1024]{2,1,0:T(8,128)(2,1)S(1)}, u32[]{:S(2)}) copy-start(bf16[3,768,1024]{2,1,0:T(8,128)(2,1)S(1)} %get-tuple-element.147.refs_1_.refs_8_.refs_2_) | copy-start | bytes 14155780
  107.8 1.9 collective-permute-start.16
  107.9 4.1 collective-permute-start.17
  108.8 3.5 collective-permute-start.18
  113.0 3.8 collective-permute-start.19
  113.6 3.9 collective-permute-start.20
  113.9 4.7 collective-permute-start.21
  118.6 10.9 %collective-permute-start.22 = (f32[8,768]{1,0:T(8,128)S(1)}, f32[8,768]{1,0:T(8,128)S(1)}, u32[]{:S(2)}, u32[]{:S(2)}) collective-permute-start(f32[8,768]{1,0:T(8,128)S(1)} %add_add_fusion.4), channel_id=1, source_target_pairs={{0,8},{1,9},{2,10},{3,11},{4,12},{5,13},{6,14},{7,15},{8,0},{9,1},... | collective-permute-start | bytes 73736 | tf_op jit(solution)/shard_map/ppermute | solution.py:1129
  149.0 1.9 collective-permute-start.23
  149.0 3.9 collective-permute-start.24
  150.1 3.3 collective-permute-start.25
  154.2 3.7 collective-permute-start.26
  155.6 3.7 collective-permute-start.27
  157.4 4.6 collective-permute-start.28
  162.0 4.6 collective-permute-start.29
  176.9 1.9 collective-permute-start.30
  177.0 4.0 collective-permute-start.31
  177.9 3.3 collective-permute-start.32
  182.0 3.7 collective-permute-start.33
  182.2 3.7 collective-permute-start.34
  182.9 4.6 collective-permute-start.35
  187.5 4.6 collective-permute-start.36
  216.7 1.9 collective-permute-start.37
  216.8 4.1 collective-permute-start.38
  217.9 3.5 collective-permute-start.39
  222.1 3.8 collective-permute-start.40
  223.6 3.8 collective-permute-start.41
  225.4 4.7 collective-permute-start.42
  230.1 14.1 %collective-permute-start.43 = (f32[8,768]{1,0:T(8,128)S(1)}, f32[8,768]{1,0:T(8,128)S(1)}, u32[]{:S(2)}, u32[]{:S(2)}) collective-permute-start(f32[8,768]{1,0:T(8,128)S(1)} %add_add_fusion.2), channel_id=1, source_target_pairs={{0,8},{1,9},{2,10},{3,11},{4,12},{5,13},{6,14},{7,15},{8,0},{9,1},... | collective-permute-start | bytes 73736 | tf_op jit(solution)/shard_map/ppermute | solution.py:1129
  302.2 99.8 %slice-start = ((s8[4718592]{0:T(1024)(128)(4,1)}), s8[4194304]{0:T(1024)(128)(4,1)S(1)}, s32[]{:S(2)}) async-start(s8[4718592]{0:T(1024)(128)(4,1)} %bitcast.11), calls=%async_computation.1 | async-start | bytes 8388608 | tf_op jit(solution)/shard_map/cond
  364.5 1.9 collective-permute-start
  364.5 4.1 collective-permute-start.1
  364.5 4.1 collective-permute-start.2
  369.3 4.2 collective-permute-start.3
  369.3 5.1 %collective-permute-start.4 = (f32[8,768]{1,0:T(8,128)S(1)}, f32[8,768]{1,0:T(8,128)S(1)}, u32[]{:S(2)}, u32[]{:S(2)}) collective-permute-start(f32[8,768]{1,0:T(8,128)S(1)} %add_add_fusion.1), channel_id=1, source_target_pairs={{0,4},{1,5},{2,6},{3,7},{4,0},{5,1},{6,2},{7,3},{8,12},{9,13},{10,... | collective-permute-start | bytes 73736 | tf_op jit(solution)/shard_map/cond/branch_1_fun/ppermute | solution.py:1129
  369.5 6.3 %collective-permute-start.5 = (f32[8,768]{1,0:T(8,128)S(1)}, f32[8,768]{1,0:T(8,128)S(1)}, u32[]{:S(2)}, u32[]{:S(2)}) collective-permute-start(f32[8,768]{1,0:T(8,128)S(1)} %add_add_fusion.1), channel_id=1, source_target_pairs={{0,6},{1,7},{2,4},{3,5},{4,2},{5,3},{6,0},{7,1},{8,14},{9,15},{10,... | collective-permute-start | bytes 73736 | tf_op jit(solution)/shard_map/cond/branch_1_fun/ppermute | solution.py:1129
  375.8 5.6 %collective-permute-start.6 = (f32[8,768]{1,0:T(8,128)S(1)}, f32[8,768]{1,0:T(8,128)S(1)}, u32[]{:S(2)}, u32[]{:S(2)}) collective-permute-start(f32[8,768]{1,0:T(8,128)S(1)} %add_add_fusion), channel_id=1, source_target_pairs={{0,8},{1,9},{2,10},{3,11},{4,12},{5,13},{6,14},{7,15},{8,0},{9,1},... | collective-permute-start | bytes 73736 | tf_op jit(solution)/shard_map/cond/branch_1_fun/ppermute | solution.py:1129
  402.0 20.3 %collective-permute-start.7 = (bf16[3,326,2048]{2,1,0:T(8,128)(2,1)}, bf16[3,326,2048]{2,1,0:T(8,128)(2,1)}, u32[]{:S(2)}, u32[]{:S(2)}) collective-permute-start(bf16[3,326,2048]{2,1,0:T(8,128)(2,1)} %get-tuple-element.55), channel_id=1, source_target_pairs={{0,16},{16,0},{1,17},{17,1},{2,18},{18,2},{3,19},{19,3},{4,20},{20... | collective-permute-start | bytes 12017672 | tf_op jit(solution)/shard_map/cond/branch_1_fun/ppermute | solution.py:1113
  412.1 4.8 collective-permute-start.8
  (9 other events, 69.3 us)
Sparse Core Ops, SparseCore 0:
  301.5 168.5 all-reduce.2
